TPU v7x, 512 devices: a whole 4x8x8 slice. The times are simulated.
512 devices in a mesh: dp: 32 (over z, x), mp: 16 (over y, core).
Axes of the slice: x: 4, y: 8, z: 8, core: 2. Of those that a mesh axis runs over, the one named last changes fastest.
Arguments:
- activations: bfloat16 [49152, 8192], P('dp', 'mp'), may hold values from -6 to 6
- cotangent: bfloat16 [49152, 1024], P('dp', 'mp'), may hold values from -6 to 6
- key_weight: bfloat16 [8192, 1024], P('mp'), may hold values from -0.1875 to 0.1875
- adapter_down: bfloat16 [32, 64, 8192], P('dp', None, 'mp'), may hold values from -0.0625 to 0.0625
- adapter_up: bfloat16 [32, 64, 1024], P('dp', None, 'mp'), may hold values from -0.1875 to 0.1875
- sequence_tenant: int32 [128], P('dp'), may hold values from 0 to 31
- slot_holder_tenant: int32 [32], replicated, may hold values from 0 to 31, each once
Outputs:
- input_gradient: bfloat16 [49152, 8192], P('dp', 'mp')
- grad_a: float32 [32, 64, 8192], P('dp', None, 'mp')
- grad_b: float32 [32, 64, 1024], P('dp', None, 'mp')
All inputs are finite; a program needn't handle non-finite values.
Results may differ from a plain program's by a relative error of at most 0.015.
Values may be sent and summed in bfloat16 or wider, within the bound.
No kernel may reach another device: no remote copies, remote signals or barrier semaphores. Data moves between devices by JAX's collectives and lax.ppermute only.
A program may use at most 64 MiB of HBM per device.

v0:
```python
import math

import jax
import jax.numpy as jnp
from jax import lax
from jax.sharding import PartitionSpec as P

ADAPTER_SCALE = 2.0


def local(
    activations,
    cotangent,
    key_weight,
    adapter_down,
    adapter_up,
    sequence_tenant,
    slot_holder_tenant,
):
    seqs = sequence_tenant.shape[0]
    rows = activations.shape[0] // seqs
    width_total = activations.shape[1]
    keys_local = cotangent.shape[1]
    scaled_gradient = ADAPTER_SCALE / math.sqrt(seqs * rows)
    x_seq = activations.reshape(seqs, rows, width_total)
    dy_seq = cotangent.reshape(seqs, rows, keys_local)
    all_a, all_b = (
        lax.all_gather(adapter_down, "dp", axis=0, tiled=True),
        lax.all_gather(adapter_up, "dp", axis=0, tiled=True),
    )
    picker = (sequence_tenant[:, None] == slot_holder_tenant[None, :]).astype(jnp.bfloat16)
    pick_a = jnp.einsum("st,trd->srd", picker, all_a, preferred_element_type=jnp.float32)
    pick_b = jnp.einsum("st,trd->srd", picker, all_b, preferred_element_type=jnp.float32)
    pick_a = pick_a.astype(jnp.bfloat16)
    pick_b = pick_b.astype(jnp.bfloat16)
    part_u = jnp.einsum("snd,srd->snr", x_seq, pick_a, preferred_element_type=jnp.float32)
    part_g = jnp.einsum("snk,srk->snr", dy_seq, pick_b, preferred_element_type=jnp.float32)
    low_u, rank_gradient = lax.psum((part_u, part_g), "mp")
    low_u = low_u.astype(jnp.bfloat16)
    rank_gradient = rank_gradient.astype(jnp.bfloat16)
    frozen_product = lax.dot_general(
        lax.all_gather(cotangent, "mp", axis=1, tiled=True),
        key_weight,
        (((1,), (1,)), ((), ())),
        preferred_element_type=jnp.float32,
    )
    adapter_update = jnp.einsum(
        "snr,srd->snd", rank_gradient, pick_a, preferred_element_type=jnp.float32
    )
    input_gradient = (
        frozen_product + ADAPTER_SCALE * adapter_update.reshape(-1, width_total)
    ).astype(jnp.bfloat16)
    seq_a = scaled_gradient * jnp.einsum(
        "snr,snd->srd", rank_gradient, x_seq, preferred_element_type=jnp.float32
    )
    seq_b = scaled_gradient * jnp.einsum(
        "snr,snk->srk", low_u, dy_seq, preferred_element_type=jnp.float32
    )
    owners_hit = (sequence_tenant[:, None] == slot_holder_tenant[None, :]).astype(jnp.float32)
    slot_a = jnp.einsum("st,srd->trd", owners_hit, seq_a, precision=lax.Precision.HIGHEST)
    slot_b = jnp.einsum("st,srd->trd", owners_hit, seq_b, precision=lax.Precision.HIGHEST)
    grad_a, grad_b = (
        lax.psum_scatter(slot_a.astype(jnp.bfloat16), "dp", scatter_dimension=0, tiled=True).astype(
            jnp.float32
        ),
        lax.psum_scatter(slot_b.astype(jnp.bfloat16), "dp", scatter_dimension=0, tiled=True).astype(
            jnp.float32
        ),
    )
    return (input_gradient, grad_a, grad_b)


def solution(mesh):
    in_specs = (
        P("dp", "mp"),
        P("dp", "mp"),
        P("mp", None),
        P("dp", None, "mp"),
        P("dp", None, "mp"),
        P("dp"),
        P(),
    )
    out_specs = (P("dp", "mp"), P("dp", None, "mp"), P("dp", None, "mp"))
    return jax.shard_map(local, mesh=mesh, in_specs=in_specs, out_specs=out_specs, check_vma=False)
```

profile of v0, /device:TPU:1, one launch (start us, length us, event | category | flops | bytes accessed | tf_op | source)
XLA Modules:
  0.0 606.0 jit_solution(9379469363502068597)
XLA Ops:
  8.1 0.7 all-gather.5.cloned.1.call-update
  8.7 0.0 reduce-scatter.5.cloned.1.call-start
  8.8 44.8 %all_gather.10 = bf16[32,64,64]{2,1,0:T(8,128)(2,1)S(1)} all-gather(bf16[1,64,64]{2,1,0:T(8,128)(2,1)} %param.11), channel_id=1, replica_groups=mesh['dp'=32,'mp'=16] {'dp'}, dimensions={0}, use_global_device_ids=true | all-gather | bytes 270336 | tf_op jit(solution)/shard_map/all_gather | solution.py:29
  53.6 1.1 fusion.6
  54.7 1.1 convolution_bitcast_fusion.1
  55.8 41.8 %all-gather.5.cloned.1.call-done = bf16[32,64,512]{2,1,0:T(8,128)(2,1)} async-done(((bf16[1,64,512]{2,1,0:T(8,128)(2,1)}), bf16[32,64,512]{2,1,0:T(8,128)(2,1)}) %all-gather.5.cloned.1.call-update) | async-done | bytes 2097168 | tf_op jit(solution)/shard_map/all_gather | solution.py:28
  97.6 2.9 fusion.3
  100.5 0.6 convolution_bitcast_fusion
  101.1 54.7 %all-reduce.2 = (bf16[4,384,64]{1,2,0:T(8,128)(2,1)S(1)}, bf16[4,384,64]{1,2,0:T(8,128)(2,1)S(1)}) all-reduce(f32[4,384,64]{1,2,0:T(8,128)S(1)} %convolution_bitcast_fusion.1, f32[4,384,64]{1,2,0:T(8,128)S(1)} %convolution_bitcast_fusion), channel_id=1, replica_groups=mesh['dp'=32,'mp'=16] {'mp'}, use_global_device_ids=true, to_apply=%region_0.0 | all-reduce | flops 196608 | bytes 1179648 | tf_op jit(solution)/shard_map/psum | solution.py:38
  155.9 0.2 fusion.11
  156.1 0.7 convolution_convert_fusion.1
  156.8 1.0 copy.19
  157.8 0.0 all-gather.3.cloned.1.call-start
  157.9 0.5 all-gather.3.cloned.1.call-update
  158.4 0.0 reduce-scatter.3.cloned.1.call-start
  158.5 0.4 fusion.39
  158.9 2.3 convolution_convert_fusion
  161.2 2.5 copy.18
  163.7 2.3 convolution_multiply_fusion
  166.0 206.2 %reduce-scatter.5.cloned.1.call-done = bf16[1,64,64]{2,1,0:T(8,128)(2,1)} async-done(((bf16[32,64,64]{2,1,0:T(8,128)(2,1)}), bf16[1,64,64]{2,1,0:T(8,128)(2,1)}) %reduce-scatter.5.cloned.1.call-update) | async-done | bytes 8208 | tf_op jit(solution)/shard_map/reduce_scatter | solution.py:66
  372.2 1.3 convert_element_type.37
  373.5 5.8 fusion
  379.4 218.0 %reduce-scatter.3.cloned.1.call-done = bf16[1,64,512]{2,1,0:T(8,128)(2,1)} async-done(((bf16[32,64,512]{2,1,0:T(8,128)(2,1)}), bf16[1,64,512]{2,1,0:T(8,128)(2,1)}) %reduce-scatter.3.cloned.1.call-update) | async-done | bytes 65552 | tf_op jit(solution)/shard_map/reduce_scatter | solution.py:63
  597.4 1.5 convert_element_type.34
  (14 shorter events, 0.1 us)
Async XLA Ops:
  8.0 92.5 %copy-start = (bf16[1536,512]{1,0:T(8,128)(2,1)S(1)}, bf16[1536,512]{1,0:T(8,128)(2,1)}, u32[]{:S(2)}) copy-start(bf16[1536,512]{1,0:T(8,128)(2,1)} %param.7) | copy-start | bytes 4718596
  8.0 89.6 %all-gather.5.cloned.1.call-start = ((), (), s32[]{:S(2)}) async-start(), calls=%async_computation.3 | async-start | bytes 2162688 | tf_op jit(solution)/shard_map/all_gather | solution.py:28
  8.7 363.5 %reduce-scatter.5.cloned.1.call-start = ((), (), s32[]{:S(2)}) async-start(), calls=%async_computation.5 | async-start | bytes 540672 | tf_op jit(solution)/shard_map/reduce_scatter | solution.py:66
  100.5 55.4 %copy-start.1 = (bf16[1536,64]{0,1:T(8,128)(2,1)S(1)}, bf16[1536,64]{0,1:T(8,128)(2,1)}, u32[]{:S(2)}) copy-start(bf16[1536,64]{0,1:T(8,128)(2,1)} %param.8) | copy-start | bytes 589828
  100.5 55.6 %copy-start.2 = (s32[32]{0:T(128)S(1)}, s32[32]{0:T(128)}, u32[]{:S(2)}) copy-start(s32[32]{0:T(128)} %param.13) | copy-start | bytes 388
  100.5 55.6 %copy-start.3 = (s32[4]{0:T(128)S(1)}, s32[4]{0:T(128)}, u32[]{:S(2)}) copy-start(s32[4]{0:T(128)} %param.12) | copy-start | bytes 52
  157.8 215.7 %all-gather.3.cloned.1.call-start = ((), (), s32[]{:S(2)}) async-start(), calls=%async_computation.2 | async-start | bytes 3342336 | tf_op jit(solution)/shard_map/all_gather | solution.py:42
  158.4 438.9 %reduce-scatter.3.cloned.1.call-start = ((), (), s32[]{:S(2)}) async-start(), calls=%async_computation.4 | async-start | bytes 2162688 | tf_op jit(solution)/shard_map/reduce_scatter | solution.py:63
  163.7 209.8 %copy-start.4 = (bf16[512,1024]{1,0:T(8,128)(2,1)S(1)}, bf16[512,1024]{1,0:T(8,128)(2,1)}, u32[]{:S(2)}) copy-start(bf16[512,1024]{1,0:T(8,128)(2,1)} %param.9) | copy-start | bytes 3145732
Sparse Core Ops, SparseCore 0:
  12.0 85.5 all-gather.4
  158.0 214.1 reduce-scatter.4
  377.3 220.0 reduce-scatter.2
Sparse Core Ops, SparseCore 1:
  160.4 43.8 all-gather.2
where the time goes:
time: 611 us; the launch traced here: 606 us
  waiting for transfers between devices  467 us (76%)
  blocking collectives  99.6 us (16%)
  matrix products  17.4 us (3%)
  between operations  15.3 us (3%)
    reduce_scatter x1, waiting for transfers between devices, local(): lax.psum_scatter(slot_a.astype(jnp.bfloat16), 'dp', scatter_dimension=0,...  218 us
    reduce_scatter x1, waiting for transfers between devices, local(): lax.psum_scatter(slot_b.astype(jnp.bfloat16), 'dp', scatter_dimension=0,...  206 us
    psum x1, blocking collectives, local(): low_u, rank_gradient = lax.psum((part_u, part_g), 'mp')  54.7 us
    all_gather x1, blocking collectives, local(): lax.all_gather(adapter_up, 'dp', axis=0, tiled=True)  44.8 us
    all_gather x1, waiting for transfers between devices, local(): lax.all_gather(adapter_down, 'dp', axis=0, tiled=True)  41.8 us
  transfers between devices with their start and end apart: 4, of which 3 were waited for; matrix products, arithmetic and copies ran while one was open for 3% of the time, Pallas kernels for 0%

commit v1 on v0

v1 whole, which is shorter than its diff:
```python
import math

import jax
import jax.numpy as jnp
from jax import lax
from jax.sharding import PartitionSpec as P

ADAPTER_SCALE = 2.0
F32 = jnp.float32
BF16 = jnp.bfloat16


def local(
    activations,
    cotangent,
    key_weight,
    adapter_down,
    adapter_up,
    sequence_tenant,
    slot_holder_tenant,
):
    seqs = sequence_tenant.shape[0]
    rows = activations.shape[0] // seqs
    width = activations.shape[1]
    keys = cotangent.shape[1]
    rank = adapter_down.shape[1]
    slots = slot_holder_tenant.shape[0]
    scale = ADAPTER_SCALE / math.sqrt(seqs * rows)
    packs = width // keys
    prows = rank // packs

    dy_t = lax.all_gather(cotangent.T, "mp", axis=0, tiled=True)
    groups = dy_t.shape[0] // keys

    up = adapter_up[0].reshape(packs, prows, keys).transpose(1, 0, 2).reshape(prows, width)
    panel = jnp.concatenate([adapter_down[0], up], axis=0)
    sent = jnp.broadcast_to(panel[None], (slots,) + panel.shape)
    panels = lax.all_to_all(sent, "dp", 0, 0, tiled=True)
    hits = sequence_tenant[:, None] == slot_holder_tenant[None, :]
    slot_of = jnp.sum(jnp.where(hits, jnp.arange(slots, dtype=jnp.int32)[None, :], 0), axis=1)
    picked = jnp.stack(
        [lax.dynamic_index_in_dim(panels, slot_of[s], 0, keepdims=False) for s in range(seqs)]
    )
    pick_a = picked[:, :rank]
    pick_b = (
        picked[:, rank:].reshape(seqs, prows, packs, keys).transpose(0, 2, 1, 3).reshape(seqs, rank, keys)
    )

    x_seq = activations.reshape(seqs, rows, width)
    dy_seq = dy_t.reshape(groups * keys, seqs, rows)
    low_u = jnp.einsum("snd,srd->snr", x_seq, pick_a, preferred_element_type=F32).astype(BF16)
    part_b = jnp.einsum("ksn,snr->skr", dy_seq, low_u, preferred_element_type=F32).astype(BF16)
    part_b = part_b.reshape(seqs, groups, keys, rank).transpose(1, 0, 2, 3)
    spread_b = jnp.broadcast_to(pick_b.transpose(0, 2, 1)[None], (groups, seqs, keys, rank))
    got = lax.all_to_all(jnp.concatenate([part_b, spread_b], axis=3), "mp", 0, 0, tiled=True)
    seq_b = scale * jnp.sum(got[..., :rank].astype(F32), axis=0)
    full_b = got[..., rank:].transpose(1, 0, 2, 3).reshape(seqs, groups * keys, rank)

    low_g = jnp.einsum("ksn,skr->srn", dy_seq, full_b, preferred_element_type=F32).astype(BF16)
    seq_a = scale * jnp.einsum("srn,snd->srd", low_g, x_seq, preferred_element_type=F32)

    owner_a = [jnp.sum(jnp.where(hits[:, t, None, None], seq_a, 0.0), axis=0) for t in range(slots)]
    owner_a = jnp.stack(owner_a).astype(BF16)
    owner_b = [jnp.sum(jnp.where(hits[:, t, None, None], seq_b, 0.0), axis=0) for t in range(slots)]
    owner_b = jnp.stack(owner_b).astype(BF16).transpose(0, 2, 1)
    owner_b = owner_b.reshape(slots, packs, prows, keys).transpose(0, 2, 1, 3).reshape(slots, prows, width)
    parts = lax.all_to_all(jnp.concatenate([owner_a, owner_b], axis=1), "dp", 0, 0, tiled=True)
    total = jnp.sum(parts.astype(F32), axis=0)
    grad_a = total[None, :rank]
    grad_b = total[rank:].reshape(prows, packs, keys).transpose(1, 0, 2).reshape(1, rank, keys)

    frozen = lax.dot_general(
        dy_t, key_weight, (((0,), (1,)), ((), ())), preferred_element_type=F32
    )
    update = jnp.einsum("srn,srd->snd", low_g, pick_a, preferred_element_type=F32)
    input_gradient = (frozen + ADAPTER_SCALE * update.reshape(-1, width)).astype(BF16)
    return (input_gradient, grad_a, grad_b)


def solution(mesh):
    in_specs = (
        P("dp", "mp"),
        P("dp", "mp"),
        P("mp", None),
        P("dp", None, "mp"),
        P("dp", None, "mp"),
        P("dp"),
        P(),
    )
    out_specs = (P("dp", "mp"), P("dp", None, "mp"), P("dp", None, "mp"))
    return jax.shard_map(local, mesh=mesh, in_specs=in_specs, out_specs=out_specs, check_vma=False)
```

time: 611 us -> 222 us (0.36)
  waiting for transfers between devices: 467 us -> 123 us
  blocking collectives: 99.6 us -> 0 us
  starting transfers between devices: 0.16 us -> 29.9 us
  local copies, waits for them, and re-layouts: 3.55 us -> 23 us
  other arithmetic: 2.84 us -> 10 us
  between operations: 15.3 us -> 22.4 us
    reduce_scatter x2 -> x0, waiting for transfers between devices: 424 us -> none  [the longest x1 218 us: local(): lax.psum_scatter(slot_a.astype(jnp.bfloat16), 'dp', scatter_dimension=0,...]
    all_to_all x0 -> x3, waiting for transfers between devices: none -> 123 us  [the longest x1 49.9 us: local(): lax.all_to_all(jnp.concatenate([owner_a, owner_b], axis=1), 'dp', 0, 0, t...]
    psum x1 -> x0, blocking collectives: 54.7 us -> none  [local(): low_u, rank_gradient = lax.psum((part_u, part_g), 'mp')]
    all_gather x1 -> x0, blocking collectives: 44.8 us -> none  [local(): lax.all_gather(adapter_up, 'dp', axis=0, tiled=True)]
    all_gather x2 -> x1, waiting for transfers between devices: 41.8 us -> 0.02 us  [local(): dy_t = lax.all_gather(cotangent.T, 'mp', axis=0, tiled=True)]
    all_to_all x0 -> x3, starting transfers between devices: none -> 29.9 us  [the longest x1 14 us: local(): panels = lax.all_to_all(sent, 'dp', 0, 0, tiled=True)]
    dot_general x10 -> x5, matrix products: 17.4 us -> 12.7 us  [the longest x1 4.36 us: local(): lax.dot_general(dy_t, key_weight, (((0,), (1,)), ((), ())), preferred_ele...]
  transfers between devices with their start and end apart: 4 -> 4, of which waited for: 3 -> 3; matrix products, arithmetic and copies ran while one was open for 3% -> 5% of each run, Pallas kernels for 0% -> 0%
where the time goes in v1:
time: 222 us; the launch traced here: 221 us
  waiting for transfers between devices  123 us (55%)
  starting transfers between devices  29.9 us (13%)
  local copies, waits for them, and re-layouts  23 us (10%)
  between operations  22.4 us (10%)
  matrix products  12.7 us (6%)
  other arithmetic  10 us (5%)
    all_to_all x1, waiting for transfers between devices, local(): lax.all_to_all(jnp.concatenate([owner_a, owner_b], axis=1), 'dp', 0, 0, t...  49.9 us
    all_to_all x1, waiting for transfers between devices, local(): panels = lax.all_to_all(sent, 'dp', 0, 0, tiled=True)  45.5 us
    all_to_all x1, waiting for transfers between devices, local(): lax.all_to_all(jnp.concatenate([part_b, spread_b], axis=3), 'mp', 0, 0, t...  27.2 us
    all_to_all x1, starting transfers between devices, local(): panels = lax.all_to_all(sent, 'dp', 0, 0, tiled=True)  14 us
    all_to_all x1, starting transfers between devices, local(): lax.all_to_all(jnp.concatenate([part_b, spread_b], axis=3), 'mp', 0, 0, t...  9.85 us
    all_to_all x1, starting transfers between devices, local(): lax.all_to_all(jnp.concatenate([owner_a, owner_b], axis=1), 'dp', 0, 0, t...  6.04 us
    all_gather x1, local copies, waits for them, and re-layouts, local(): dy_t = lax.all_gather(cotangent.T, 'mp', axis=0, tiled=True)  4.7 us
  transfers between devices with their start and end apart: 4, of which 3 were waited for; matrix products, arithmetic and copies ran while one was open for 5% of the time, Pallas kernels for 0%

profile of v1, /device:TPU:1, one launch (start us, length us, event | category | flops | bytes accessed | tf_op | source)
XLA Modules:
  0.0 221.2 jit_solution(14201322740682620801)
XLA Ops:
  9.6 1.6 broadcast_in_dim.490
  11.1 14.0 %all-to-all-start = ((bf16[32,72,512]{2,1,0:T(8,128)(2,1)}), bf16[32,72,512]{2,1,0:T(8,128)(2,1)}, u32[]{:S(2)}, u32[]{:S(2)}) async-start(bf16[32,72,512]{2,1,0:T(8,128)(2,1)} %broadcast_in_dim.490), calls=%async_computation | async-start | bytes 4718592 | tf_op jit(solution)/shard_map/all_to_all | solution.py:38
  33.6 45.5 %all-to-all-done = bf16[32,72,512]{2,1,0:T(8,128)(2,1)} async-done(((bf16[32,72,512]{2,1,0:T(8,128)(2,1)}), bf16[32,72,512]{2,1,0:T(8,128)(2,1)}, u32[]{:S(2)}, u32[]{:S(2)}) %all-to-all-start) | async-done | bytes 2359328 | tf_op jit(solution)/shard_map/all_to_all | solution.py:38
  79.0 1.0 constant_dynamic-slice_fusion.2
  80.4 4.7 %copy.37 = bf16[1024,1536]{0,1:T(8,128)(2,1)} copy(bf16[1024,1536]{1,0:T(8,128)(2,1)} %all-gather.2.cloned.1.call-done) | data formatting | bytes 6291456 | tf_op jit(solution)/shard_map/all_gather | solution.py:32
  85.1 3.0 %fusion.1 = bf16[4,1024,64]{1,2,0:T(8,128)(2,1)S(1)} fusion(bf16[1024,4,384]{0,2,1:T(8,128)(2,1)} %bitcast.246, bf16[4,384,512]{2,1,0:T(8,128)(2,1)S(1)} %bitcast.244, bf16[4,72,512]{2,1,0:T(8,128)(2,1)S(1)} %pad_maximum_fusion.2), kind=kOutput, calls=%fused_computation.7 | convolution fusion | flops 302350336 | bytes 5505024 | tf_op jit(solution)/shard_map/ksn,snr->skr/dot_general | solution.py:52
  88.1 1.6 reshape.81
  89.7 1.8 copy.39
  91.8 1.7 pad_maximum_fusion.1
  93.5 9.8 %all-to-all-start.1 = ((bf16[16,4,64,128]{3,2,1,0:T(8,128)(2,1)}), bf16[16,4,64,128]{3,2,1,0:T(8,128)(2,1)S(1)}, u32[]{:S(2)}, u32[]{:S(2)}) async-start(bf16[16,4,64,128]{3,2,1,0:T(8,128)(2,1)} %pad_maximum_fusion.1), calls=%async_computation.1 | async-start | bytes 2097152 | tf_op jit(solution)/shard_map/all_to_all | solution.py:55
  104.0 27.2 %all-to-all-done.1 = bf16[16,4,64,128]{3,2,1,0:T(8,128)(2,1)S(1)} async-done(((bf16[16,4,64,128]{3,2,1,0:T(8,128)(2,1)}), bf16[16,4,64,128]{3,2,1,0:T(8,128)(2,1)S(1)}, u32[]{:S(2)}, u32[]{:S(2)}) %all-to-all-start.1) | async-done | bytes 1048608 | tf_op jit(solution)/shard_map/all_to_all | solution.py:55
  131.3 1.4 slice_bitcast_fusion
  132.7 2.7 %copy.42 = bf16[4,16,64,64]{2,1,3,0:T(8,128)(2,1)} copy(bf16[4,16,64,64]{3,2,0,1:T(8,128)(2,1)} %slice_bitcast_fusion) | data formatting | bytes 1048576 | tf_op jit(solution)/shard_map/transpose | solution.py:57
  135.3 1.9 reshape.84
  137.3 3.7 %convolution_convert_fusion.1 = bf16[4,64,384]{2,1,0:T(8,128)(2,1)} fusion(bf16[4,1024,64]{1,2,0:T(8,128)(2,1)S(1)} %reshape.84, bf16[1024,4,384]{0,2,1:T(8,128)(2,1)} %bitcast.247), kind=kOutput, calls=%fused_computation.9 | convolution fusion | flops 201424896 | bytes 3866624 | tf_op jit(solution)/shard_map/ksn,skr->srn/dot_general | solution.py:59
  141.3 1.0 select_reduce_fusion.33
  142.4 1.3 select_reduce_fusion.32
  145.6 1.2 select_reduce_fusion
  147.2 1.6 pad_maximum_fusion
  148.8 6.0 %all-to-all-start.2 = ((bf16[32,72,512]{2,1,0:T(8,128)(2,1)}), bf16[32,72,512]{2,1,0:T(8,128)(2,1)}, u32[]{:S(2)}, u32[]{:S(2)}) async-start(bf16[32,72,512]{2,1,0:T(8,128)(2,1)} %pad_maximum_fusion), calls=%async_computation.2 | async-start | bytes 4718592 | tf_op jit(solution)/shard_map/all_to_all | solution.py:67
  155.5 1.3 copy-done.1
  156.7 4.4 %fusion = bf16[1536,512]{1,0:T(8,128)(2,1)} fusion(f32[1536,512]{1,0:T(8,128)S(1)} %bitcast.249, bf16[1024,1536]{1,0:T(8,128)(2,1)S(1)} %copy-done.1, bf16[512,1024]{1,0:T(8,128)(2,1)} %param.9), kind=kOutput, calls=%fused_computation.2 | convolution fusion | flops 1612185600 | bytes 8912896 | tf_op jit(solution)/shard_map/dot_general | solution.py:72
  161.1 49.9 %all-to-all-done.2 = bf16[32,72,512]{2,1,0:T(8,128)(2,1)} async-done(((bf16[32,72,512]{2,1,0:T(8,128)(2,1)}), bf16[32,72,512]{2,1,0:T(8,128)(2,1)}, u32[]{:S(2)}, u32[]{:S(2)}) %all-to-all-start.2) | async-done | bytes 2359328 | tf_op jit(solution)/shard_map/all_to_all | solution.py:67
  211.0 2.0 convert_reduce_fusion
  (108 shorter events, 8.6 us)
Async XLA Ops:
  7.2 77.9 %copy-start = (bf16[1536,512]{1,0:T(8,128)(2,1)S(1)}, bf16[1536,512]{1,0:T(8,128)(2,1)}, u32[]{:S(2)}) copy-start(bf16[1536,512]{1,0:T(8,128)(2,1)} %param.7) | copy-start | bytes 4718596
  7.2 73.2 %all-gather.2.cloned.1.call-start = ((), (), s32[]{:S(2)}) async-start(), calls=%async_computation.3 | async-start | bytes 3342336 | tf_op jit(solution)/shard_map/all_gather | solution.py:32
  11.1 14.0 %copy-start.7 = (s32[32]{0:T(128)S(1)}, s32[32]{0:T(128)}, u32[]{:S(2)}) copy-start(s32[32]{0:T(128)} %param.13) | copy-start | bytes 388
  11.1 14.0 %copy-start.8 = (s32[4]{0:T(128)S(1)}, s32[4]{0:T(128)}, u32[]{:S(2)}) copy-start(s32[4]{0:T(128)} %param.12) | copy-start | bytes 52
  11.1 67.9 %all-to-all-start = ((bf16[32,72,512]{2,1,0:T(8,128)(2,1)}), bf16[32,72,512]{2,1,0:T(8,128)(2,1)}, u32[]{:S(2)}, u32[]{:S(2)}) async-start(bf16[32,72,512]{2,1,0:T(8,128)(2,1)} %broadcast_in_dim.490), calls=%async_computation | async-start | bytes 4718592 | tf_op jit(solution)/shard_map/all_to_all | solution.py:38
  93.5 37.8 %all-to-all-start.1 = ((bf16[16,4,64,128]{3,2,1,0:T(8,128)(2,1)}), bf16[16,4,64,128]{3,2,1,0:T(8,128)(2,1)S(1)}, u32[]{:S(2)}, u32[]{:S(2)}) async-start(bf16[16,4,64,128]{3,2,1,0:T(8,128)(2,1)} %pad_maximum_fusion.1), calls=%async_computation.1 | async-start | bytes 2097152 | tf_op jit(solution)/shard_map/all_to_all | solution.py:55
  141.1 3.4 %copy-start.2 = (bf16[4,64,384]{2,1,0:T(8,128)(2,1)S(1)}, bf16[4,64,384]{2,1,0:T(8,128)(2,1)}, u32[]{:S(2)}) copy-start(bf16[4,64,384]{2,1,0:T(8,128)(2,1)} %convolution_convert_fusion.1) | copy-start | bytes 589828
  141.2 3.4 %copy-start.3 = (pred[4]{0:T(512)(128)(4,1)S(1)}, pred[4]{0:T(512)(128)(4,1)}, u32[]{:S(2)}) copy-start(pred[4]{0:T(512)(128)(4,1)} %get-tuple-element.98) | copy-start | bytes 16
  141.2 3.4 %copy-start.4 = (pred[4]{0:T(512)(128)(4,1)S(1)}, pred[4]{0:T(512)(128)(4,1)}, u32[]{:S(2)}) copy-start(pred[4]{0:T(512)(128)(4,1)} %get-tuple-element.99) | copy-start | bytes 16
  141.2 3.4 %copy-start.5 = (pred[4]{0:T(512)(128)(4,1)S(1)}, pred[4]{0:T(512)(128)(4,1)}, u32[]{:S(2)}) copy-start(pred[4]{0:T(512)(128)(4,1)} %get-tuple-element.100) | copy-start | bytes 16
  141.2 3.4 %copy-start.6 = (pred[4]{0:T(512)(128)(4,1)S(1)}, pred[4]{0:T(512)(128)(4,1)}, u32[]{:S(2)}) copy-start(pred[4]{0:T(512)(128)(4,1)} %get-tuple-element.101) | copy-start | bytes 16
  148.8 62.2 %all-to-all-start.2 = ((bf16[32,72,512]{2,1,0:T(8,128)(2,1)}), bf16[32,72,512]{2,1,0:T(8,128)(2,1)}, u32[]{:S(2)}, u32[]{:S(2)}) async-start(bf16[32,72,512]{2,1,0:T(8,128)(2,1)} %pad_maximum_fusion), calls=%async_computation.2 | async-start | bytes 4718592 | tf_op jit(solution)/shard_map/all_to_all | solution.py:67
  154.8 1.9 copy-start.1
Sparse Core Ops, SparseCore 0:
  10.1 49.3 all-gather.1

commit v2 on v1

v2 whole, which is shorter than its diff:
```python
import functools
import math

import jax
import jax.numpy as jnp
from jax import lax
from jax.experimental import pallas as pl
from jax.experimental.pallas import tpu as pltpu
from jax.sharding import Mesh, PartitionSpec as P

ADAPTER_SCALE = 2.0
F32 = jnp.float32
BF16 = jnp.bfloat16
LANES = 128
COLUMNS = 4
PARAMS = pltpu.CompilerParams(vmem_limit_bytes=40 * 2**20)
SERIAL = pltpu.CompilerParams(
    vmem_limit_bytes=40 * 2**20, dimension_semantics=("arbitrary",)
)
VMEM = pl.BlockSpec(memory_space=pltpu.VMEM)
SMEM = pl.BlockSpec(memory_space=pltpu.SMEM)


def left_half(shape):
    return lax.broadcasted_iota(jnp.int32, shape, 1) < LANES // 2


def pack(tall):
    slabs = []
    for i in range(0, tall.shape[0], 16):
        upper, lower = tall[i : i + 8], pltpu.roll(tall[i + 8 : i + 16], LANES // 2, 1)
        slabs.append(jnp.where(left_half(upper.shape), upper, lower))
    return jnp.concatenate(slabs, axis=1)


def unpack(flat, right):
    pieces = []
    for i in range(0, flat.shape[1], LANES):
        slab = flat[:, i : i + LANES]
        turned = pltpu.roll(slab, LANES // 2, 1)
        left = left_half(slab.shape)
        for piece in (turned, slab) if right else (slab, turned):
            pieces.append(jnp.where(left != right, piece, 0.0))
    return jnp.concatenate(pieces, axis=0)


def prepare(tenant_ref, holder_ref, down_ref, up_ref, sent_ref, slot_ref):
    for s in range(tenant_ref.shape[0]):
        slot = jnp.int32(0)
        for t in range(holder_ref.shape[0]):
            slot = jnp.where(holder_ref[t] == tenant_ref[s], jnp.int32(t), slot)
        slot_ref[s] = slot
    up = up_ref[0].astype(F32).T
    packed = pack(jnp.concatenate([up, jnp.zeros_like(up)], axis=1))
    panel = jnp.concatenate([down_ref[0].astype(F32), packed], axis=0).astype(BF16)
    for z in range(sent_ref.shape[0]):
        sent_ref[z] = panel


def project(slot_ref, panel_ref, x_ref, dy_ref, sent_ref, down_ref):
    rank = down_ref.shape[1]
    groups, _, keys, _ = sent_ref.shape
    panel = panel_ref[0, 0]
    down = panel[:rank]
    wide = jnp.concatenate([down, jnp.zeros_like(down)], axis=0)
    low_u = lax.dot_general(
        x_ref[...], wide, (((1,), (1,)), ((), ())), preferred_element_type=F32
    ).astype(BF16)
    part = jnp.dot(dy_ref[...], low_u, preferred_element_type=F32)
    up = unpack(panel.astype(F32)[rank:], True)
    sent_ref[:, 0] = (part.reshape(groups, keys, 2 * rank) + up[None]).astype(BF16)
    down_ref[0] = down


def combine(
    scale,
    slot_ref,
    got_ref,
    dy_ref,
    x_ref,
    weight_ref,
    down_ref,
    input_ref,
    sent_ref,
):
    rank, width = down_ref.shape[1:]
    columns = sent_ref.shape[0]
    got = got_ref[:, 0]
    dy = dy_ref[...]
    both = lax.dot_general(
        got.reshape(-1, 2 * rank), dy, (((0,), (0,)), ((), ())), preferred_element_type=F32
    )
    low_g = both[rank:].astype(BF16)
    part_a = jnp.dot(low_g, x_ref[...], preferred_element_type=F32)
    part_b = jnp.sum(got.astype(F32), axis=0)
    slot = slot_ref[pl.program_id(0)]
    for x in range(columns):
        place = jnp.where(slot % columns == x, slot // columns, -1).astype(F32)
        tail = jnp.concatenate([scale * pack(part_b), jnp.full((8, width), place, F32)], axis=0)
        sent_ref[x, 0] = jnp.concatenate([scale * part_a, tail], axis=0).astype(BF16)
    frozen = lax.dot_general(
        dy, weight_ref[...], (((0,), (1,)), ((), ())), preferred_element_type=F32
    )
    update = lax.dot_general(
        low_g, down_ref[0], (((0,), (0,)), ((), ())), preferred_element_type=F32
    )
    input_ref[...] = (frozen + ADAPTER_SCALE * update).astype(BF16)


def sort(got_ref, sent_ref):
    columns, seqs = got_ref.shape[:2]
    tall = sent_ref.shape[1]
    rank = tall - 8
    for z in range(sent_ref.shape[0]):
        head = tail = 0.0
        for x in range(columns):
            for s in range(seqs):
                low = got_ref[x, s, rank:].astype(F32)
                here = low[8:9] == z
                head = head + jnp.where(here, got_ref[x, s, :rank].astype(F32), 0.0)
                tail = tail + jnp.where(here, low[:8], 0.0)
        sent_ref[z] = jnp.concatenate([head, tail], axis=0).astype(BF16)


def finish(got_ref, down_ref, up_ref):
    rank = down_ref.shape[1]
    total = got_ref[0].astype(F32)
    for p in range(1, got_ref.shape[0]):
        total = total + got_ref[p].astype(F32)
    down_ref[0] = total[:rank]
    up_ref[0] = unpack(total[rank:], False)[:, :rank].T


def local(
    columns,
    activations,
    cotangent,
    key_weight,
    adapter_down,
    adapter_up,
    sequence_tenant,
    slot_holder_tenant,
):
    seqs = sequence_tenant.shape[0]
    rows = activations.shape[0] // seqs
    width = activations.shape[1]
    keys = cotangent.shape[1]
    rank = adapter_down.shape[1]
    slots = slot_holder_tenant.shape[0]
    tall = rank + rank * keys // width
    scale = ADAPTER_SCALE / math.sqrt(seqs * rows)
    struct = jax.ShapeDtypeStruct

    dy = lax.all_gather(cotangent.T, "mp", axis=0, tiled=True)
    key_width = dy.shape[0]
    groups = key_width // keys

    sent, slot_of = pl.pallas_call(
        prepare,
        out_shape=(struct((slots // columns, tall, width), BF16), struct((seqs,), jnp.int32)),
        in_specs=[SMEM, SMEM, VMEM, VMEM],
        out_specs=(VMEM, SMEM),
        compiler_params=PARAMS,
        name="prepare",
    )(sequence_tenant, slot_holder_tenant, adapter_down, adapter_up)
    panels = lax.all_to_all(sent, "z", 0, 0, tiled=True)
    panels = jnp.broadcast_to(panels[None], (columns,) + panels.shape)
    panels = lax.all_to_all(panels, "x", 0, 0, tiled=True)

    sent, down = pl.pallas_call(
        project,
        grid_spec=pltpu.PrefetchScalarGridSpec(
            num_scalar_prefetch=1,
            grid=(seqs,),
            in_specs=[
                pl.BlockSpec(
                    (1, 1, tall, width),
                    lambda s, slot: (slot[s] % columns, slot[s] // columns, 0, 0),
                ),
                pl.BlockSpec((rows, width), lambda s, slot: (s, 0)),
                pl.BlockSpec((key_width, rows), lambda s, slot: (0, s)),
            ],
            out_specs=(
                pl.BlockSpec((groups, 1, keys, 2 * rank), lambda s, slot: (0, s, 0, 0)),
                pl.BlockSpec((1, rank, width), lambda s, slot: (s, 0, 0)),
            ),
        ),
        out_shape=(
            struct((groups, seqs, keys, 2 * rank), BF16),
            struct((seqs, rank, width), BF16),
        ),
        compiler_params=SERIAL,
        name="project",
    )(slot_of, panels, activations, dy)
    got = lax.all_to_all(sent, "mp", 0, 0, tiled=True)

    input_gradient, sent = pl.pallas_call(
        functools.partial(combine, scale),
        grid_spec=pltpu.PrefetchScalarGridSpec(
            num_scalar_prefetch=1,
            grid=(seqs,),
            in_specs=[
                pl.BlockSpec((groups, 1, keys, 2 * rank), lambda s, slot: (0, s, 0, 0)),
                pl.BlockSpec((key_width, rows), lambda s, slot: (0, s)),
                pl.BlockSpec((rows, width), lambda s, slot: (s, 0)),
                pl.BlockSpec((width, key_width), lambda s, slot: (0, 0)),
                pl.BlockSpec((1, rank, width), lambda s, slot: (s, 0, 0)),
            ],
            out_specs=(
                pl.BlockSpec((rows, width), lambda s, slot: (s, 0)),
                pl.BlockSpec((columns, 1, tall + 8, width), lambda s, slot: (0, s, 0, 0)),
            ),
        ),
        out_shape=(
            struct(activations.shape, BF16),
            struct((columns, seqs, tall + 8, width), BF16),
        ),
        compiler_params=SERIAL,
        name="combine",
    )(slot_of, got, dy, activations, key_weight, down)
    got = lax.all_to_all(sent, "x", 0, 0, tiled=True)

    sent = pl.pallas_call(
        sort,
        out_shape=struct((slots // columns, tall, width), BF16),
        in_specs=[VMEM],
        out_specs=VMEM,
        compiler_params=PARAMS,
        name="sort",
    )(got)
    got = lax.all_to_all(sent, "z", 0, 0, tiled=True)

    grad_a, grad_b = pl.pallas_call(
        finish,
        out_shape=(struct((1, rank, width), F32), struct((1, rank, keys), F32)),
        in_specs=[VMEM],
        out_specs=(VMEM, VMEM),
        compiler_params=PARAMS,
        name="finish",
    )(got)
    return (input_gradient, grad_a, grad_b)


def solution(mesh):
    columns = min(COLUMNS, mesh.shape["dp"] // 2)
    grid = Mesh(mesh.devices.reshape(-1, columns, mesh.shape["mp"]), ("z", "x", "mp"))
    dp = ("z", "x")
    in_specs = (
        P(dp, "mp"),
        P(dp, "mp"),
        P("mp", None),
        P(dp, None, "mp"),
        P(dp, None, "mp"),
        P(dp),
        P(),
    )
    out_specs = (P(dp, "mp"), P(dp, None, "mp"), P(dp, None, "mp"))
    body = functools.partial(local, columns)
    return jax.shard_map(body, mesh=grid, in_specs=in_specs, out_specs=out_specs, check_vma=False)
```

time: 222 us -> 176 us (0.79)
  blocking collectives: 0 us -> 140 us
  waiting for transfers between devices: 123 us -> 0.68 us
  starting transfers between devices: 29.9 us -> 0.04 us
  local copies, waits for them, and re-layouts: 23 us -> 6.36 us
  Pallas kernels: 0 us -> 14.5 us
  matrix products: 12.7 us -> 0 us
  other arithmetic: 10 us -> 0 us
  between operations: 22.4 us -> 14.1 us
    all_to_all x0 -> x5, blocking collectives: none -> 140 us  [the longest x1 39.5 us: local(): got = lax.all_to_all(sent, 'mp', 0, 0, tiled=True)]
    all_to_all x3 -> x0, waiting for transfers between devices: 123 us -> none  [the longest x1 49.9 us: local(): lax.all_to_all(jnp.concatenate([owner_a, owner_b], axis=1), 'dp', 0, 0, t...]
    all_to_all x3 -> x0, starting transfers between devices: 29.9 us -> none  [the longest x1 14 us: local(): panels = lax.all_to_all(sent, 'dp', 0, 0, tiled=True)]
    pallas_call x0 -> x5, Pallas kernels: none -> 14.5 us  [the longest x1 6.04 us: local(): pl.pallas_call(functools.partial(combine, scale), grid_spec=pltpu.Prefetc...]
    dot_general x5 -> x0, matrix products: 12.7 us -> none  [the longest x1 4.36 us: local(): lax.dot_general(dy_t, key_weight, (((0,), (1,)), ((), ())), preferred_ele...]
    reshape x8 -> x0, local copies, waits for them, and re-layouts: 6.02 us -> none  [the longest x2 3.47 us: local(): part_b = part_b.reshape(seqs, groups, keys, rank).transpose(1, 0, 2, 3)]
    reduce_sum x6 -> x0, other arithmetic: 5.83 us -> none  [the longest x2 2.34 us: local(): jnp.sum(jnp.where(hits[:, t, None, None], seq_b, 0.0), axis=0)]
    transpose x6 -> x0, local copies, waits for them, and re-layouts: 5.6 us -> none  [the longest x2 4.05 us: local(): got[..., rank:].transpose(1, 0, 2, 3).reshape(seqs, groups * keys, rank)]
  transfers between devices with their start and end apart: 4 -> 1, of which waited for: 3 -> 0; matrix products, arithmetic and copies ran while one was open for 5% -> 0% of each run, Pallas kernels for 0% -> 1%
where the time goes in v2:
time: 176 us; the launch traced here: 175 us
  blocking collectives  140 us (80%)
  Pallas kernels  14.5 us (8%)
  between operations  14.1 us (8%)
  local copies, waits for them, and re-layouts  6.36 us (4%)
    all_to_all x1, blocking collectives, local(): got = lax.all_to_all(sent, 'mp', 0, 0, tiled=True)  39.5 us
    all_to_all x1, blocking collectives, local(): panels = lax.all_to_all(panels, 'x', 0, 0, tiled=True)  30 us
    all_to_all x1, blocking collectives, local(): panels = lax.all_to_all(sent, 'z', 0, 0, tiled=True)  28.1 us
    all_to_all x1, blocking collectives, local(): got = lax.all_to_all(sent, 'z', 0, 0, tiled=True)  22.1 us
    all_to_all x1, blocking collectives, local(): got = lax.all_to_all(sent, 'x', 0, 0, tiled=True)  19.8 us
    unnamed x16, local copies, waits for them, and re-layouts  6.17 us
    pallas_call x1, Pallas kernels, local(): pl.pallas_call(functools.partial(combine, scale), grid_spec=pltpu.Prefetc...  6.04 us
    pallas_call x1, Pallas kernels, local(): pl.pallas_call(project, grid_spec=pltpu.PrefetchScalarGridSpec(num_scalar...  3.68 us
  transfers between devices with their start and end apart: 1, of which 0 were waited for; matrix products, arithmetic and copies ran while one was open for 0% of the time, Pallas kernels for 1%

profile of v2, /device:TPU:1, one launch (start us, length us, event | category | flops | bytes accessed | tf_op | source)
XLA Modules:
  0.0 175.2 jit_solution(15665885139231202620)
XLA Ops:
  7.2 0.0 all-gather.2.cloned.1.call-start
  7.2 0.7 all-gather.2.cloned.1.call-update
  7.9 0.0 copy-start.4
  7.9 0.8 copy-done.4
  8.7 0.0 copy-start.5
  8.7 0.7 copy-done.5
  9.5 0.7 copy-done.6
  10.1 0.7 copy-done.7
  10.8 1.3 prepare.1
  12.1 28.1 %all_to_all.25 = bf16[8,72,512]{2,1,0:T(8,128)(2,1)S(1)} all-to-all(bf16[8,72,512]{2,1,0:T(8,128)(2,1)S(1)} %get-tuple-element.12), channel_id=1, replica_groups=mesh['z'=8,'x'=4,'mp'=16] {'z'}, dimensions={0} | all-to-all | bytes 1179648 | tf_op jit(solution)/shard_map/all_to_all | solution.py:166
  40.2 0.2 broadcast_in_dim.2
  40.4 30.0 %all_to_all.26.panel_ref = bf16[4,8,72,512]{3,2,1,0:T(8,128)(2,1)S(1)} all-to-all(bf16[4,8,72,512]{3,2,1,0:T(8,128)(2,1)S(1)} %broadcast_in_dim.2), channel_id=1, replica_groups=mesh['z'=8,'x'=4,'mp'=16] {'x'}, dimensions={0} | all-to-all | bytes 4718592 | tf_op jit(solution)/shard_map/all_to_all | solution.py:168
  70.4 1.9 %copy-done = bf16[1024,1536]{1,0:T(8,128)(2,1)S(1)} copy-done((bf16[1024,1536]{1,0:T(8,128)(2,1)S(1)}, bf16[1024,1536]{1,0:T(8,128)(2,1)}, u32[]{:S(2)}) %copy-start) | copy-done | bytes 3145752
  72.3 1.4 copy-done.2
  73.7 3.7 %project.1 = (bf16[16,4,64,128]{3,2,1,0:T(8,128)(2,1)S(1)}, bf16[4,64,512]{2,1,0:T(8,128)(2,1)S(1)}) custom-call(s32[4]{0:T(128)S(1)} %get-tuple-element.11.slot_ref, bf16[4,8,72,512]{3,2,1,0:T(8,128)(2,1)S(1)} %all_to_all.26.panel_ref, bf16[1536,512]{1,0:T(8,128)(2,1)S(1)} %copy-done.2, bf16[1024,1536]{1,0:T(8,128)(2,1)S(1)} %copy-done), custom_call_target="tpu_custom_call" | custom-call | tf_op jit(solution)/shard_map/project/pallas_call | solution.py:170
  77.4 0.0 copy-start.3
  77.4 39.5 %all_to_all.27.got_ref = bf16[16,4,64,128]{3,2,1,0:T(8,128)(2,1)S(1)} all-to-all(bf16[16,4,64,128]{3,2,1,0:T(8,128)(2,1)S(1)} %get-tuple-element.13), channel_id=1, replica_groups=mesh['z'=8,'x'=4,'mp'=16] {'mp'}, dimensions={0} | all-to-all | bytes 2097152 | tf_op jit(solution)/shard_map/all_to_all | solution.py:195
  116.9 0.0 copy-done.1
  116.9 0.0 copy-done.3
  116.9 6.0 %combine.1 = (bf16[1536,512]{1,0:T(8,128)(2,1)}, bf16[4,4,80,512]{3,2,1,0:T(8,128)(2,1)S(1)}) custom-call(s32[4]{0:T(128)S(1)} %get-tuple-element.11.slot_ref, bf16[16,4,64,128]{3,2,1,0:T(8,128)(2,1)S(1)} %all_to_all.27.got_ref, bf16[1024,1536]{1,0:T(8,128)(2,1)S(1)} %copy-done.1, bf16[1536,512]{1,0:T(8,128)(2,1)S(1)} %copy-done.2, ...), custom_call_target="tpu_custom_call" | custom-call | tf_op jit(solution)/shard_map/combine/pallas_call | solution.py:197
  122.9 19.8 %all_to_all.28.got_ref = bf16[4,4,80,512]{3,2,1,0:T(8,128)(2,1)S(1)} all-to-all(bf16[4,4,80,512]{3,2,1,0:T(8,128)(2,1)S(1)} %get-tuple-element.16), channel_id=1, replica_groups=mesh['z'=8,'x'=4,'mp'=16] {'x'}, dimensions={0} | all-to-all | bytes 2621440 | tf_op jit(solution)/shard_map/all_to_all | solution.py:221
  142.8 2.7 %sort.1 = bf16[8,72,512]{2,1,0:T(8,128)(2,1)S(1)} custom-call(bf16[4,4,80,512]{3,2,1,0:T(8,128)(2,1)S(1)} %all_to_all.28.got_ref), custom_call_target="tpu_custom_call" | custom-call | tf_op jit(solution)/shard_map/sort/pallas_call | solution.py:223
  145.5 22.1 %all_to_all.29.got_ref = bf16[8,72,512]{2,1,0:T(8,128)(2,1)S(1)} all-to-all(bf16[8,72,512]{2,1,0:T(8,128)(2,1)S(1)} %sort.1), channel_id=1, replica_groups=mesh['z'=8,'x'=4,'mp'=16] {'z'}, dimensions={0} | all-to-all | bytes 1179648 | tf_op jit(solution)/shard_map/all_to_all | solution.py:231
  167.5 0.8 finish.1
  (6 shorter events, 0.0 us)
Async XLA Ops:
  7.2 63.2 %all-gather.2.cloned.1.call-start = ((), (), s32[]{:S(2)}) async-start(), calls=%async_computation.5 | async-start | bytes 3342336 | tf_op jit(solution)/shard_map/all_gather | solution.py:154
  7.9 0.8 copy-start.4
  8.7 0.7 copy-start.5
  9.5 0.7 copy-start.6
  10.1 0.7 copy-start.7
  70.4 1.9 %copy-start = (bf16[1024,1536]{1,0:T(8,128)(2,1)S(1)}, bf16[1024,1536]{1,0:T(8,128)(2,1)}, u32[]{:S(2)}) copy-start(bf16[1024,1536]{1,0:T(8,128)(2,1)} %all-gather.2.cloned.1.call-done.dy_ref) | copy-start | bytes 9437188
  72.3 1.4 copy-start.2
  73.7 43.2 %copy-start.1 = (bf16[1024,1536]{1,0:T(8,128)(2,1)S(1)}, bf16[1024,1536]{1,0:T(8,128)(2,1)}, u32[]{:S(2)}) copy-start(bf16[1024,1536]{1,0:T(8,128)(2,1)} %all-gather.2.cloned.1.call-done.dy_ref) | copy-start | bytes 9437188
  77.4 39.5 %copy-start.3 = (bf16[512,1024]{1,0:T(8,128)(2,1)S(1)}, bf16[512,1024]{1,0:T(8,128)(2,1)}, u32[]{:S(2)}) copy-start(bf16[512,1024]{1,0:T(8,128)(2,1)} %weight_ref.1) | copy-start | bytes 3145732
Sparse Core Ops, SparseCore 0:
  10.1 49.3 all-gather.1

commit v3 on v2

--- a/solution.py
+++ b/solution.py
@@ -13,10 +13,9 @@
 BF16 = jnp.bfloat16
 LANES = 128
 COLUMNS = 4
-PARAMS = pltpu.CompilerParams(vmem_limit_bytes=40 * 2**20)
-SERIAL = pltpu.CompilerParams(
-    vmem_limit_bytes=40 * 2**20, dimension_semantics=("arbitrary",)
-)
+ALL = pltpu.CompilerParams(vmem_limit_bytes=58 * 2**20, dimension_semantics=("arbitrary",))
+WHOLE = pltpu.CompilerParams(vmem_limit_bytes=58 * 2**20)
+PART = pltpu.CompilerParams(vmem_limit_bytes=24 * 2**20)
 VMEM = pl.BlockSpec(memory_space=pltpu.VMEM)
 SMEM = pl.BlockSpec(memory_space=pltpu.SMEM)
 
@@ -44,17 +43,26 @@
     return jnp.concatenate(pieces, axis=0)
 
 
-def prepare(tenant_ref, holder_ref, down_ref, up_ref, sent_ref, slot_ref):
-    for s in range(tenant_ref.shape[0]):
-        slot = jnp.int32(0)
-        for t in range(holder_ref.shape[0]):
-            slot = jnp.where(holder_ref[t] == tenant_ref[s], jnp.int32(t), slot)
-        slot_ref[s] = slot
+def prepare(down_ref, up_ref, sent_ref):
     up = up_ref[0].astype(F32).T
     packed = pack(jnp.concatenate([up, jnp.zeros_like(up)], axis=1))
     panel = jnp.concatenate([down_ref[0].astype(F32), packed], axis=0).astype(BF16)
     for z in range(sent_ref.shape[0]):
         sent_ref[z] = panel
+
+
+def select(columns, panel_ref, holder_ref, *refs):
+    tenant_refs, (sent_ref, slot_ref, table) = refs[:columns], refs[columns:]
+    for t in range(holder_ref.shape[0]):
+        table[holder_ref[t]] = jnp.int32(t)
+    here = lax.axis_index("x")
+    for back, tenant_ref in enumerate(tenant_refs):
+        there = lax.rem(here + columns - back, columns)
+        for s in range(tenant_ref.shape[0]):
+            slot = table[tenant_ref[s]]
+            if back == 0:
+                slot_ref[s] = slot
+            sent_ref[there, s] = panel_ref[slot // columns]
 
 
 def project(slot_ref, panel_ref, x_ref, dy_ref, sent_ref, down_ref):
@@ -78,12 +86,10 @@
     got_ref,
     dy_ref,
     x_ref,
-    weight_ref,
-    down_ref,
-    input_ref,
+    low_ref,
     sent_ref,
 ):
-    rank, width = down_ref.shape[1:]
+    rank, width = low_ref.shape[1], x_ref.shape[1]
     columns = sent_ref.shape[0]
     got = got_ref[:, 0]
     dy = dy_ref[...]
@@ -91,6 +97,7 @@
         got.reshape(-1, 2 * rank), dy, (((0,), (0,)), ((), ())), preferred_element_type=F32
     )
     low_g = both[rank:].astype(BF16)
+    low_ref[0] = low_g
     part_a = jnp.dot(low_g, x_ref[...], preferred_element_type=F32)
     part_b = jnp.sum(got.astype(F32), axis=0)
     slot = slot_ref[pl.program_id(0)]
@@ -98,11 +105,14 @@
         place = jnp.where(slot % columns == x, slot // columns, -1).astype(F32)
         tail = jnp.concatenate([scale * pack(part_b), jnp.full((8, width), place, F32)], axis=0)
         sent_ref[x, 0] = jnp.concatenate([scale * part_a, tail], axis=0).astype(BF16)
+
+
+def backward(low_ref, dy_ref, weight_ref, down_ref, input_ref):
     frozen = lax.dot_general(
-        dy, weight_ref[...], (((0,), (1,)), ((), ())), preferred_element_type=F32
+        dy_ref[...], weight_ref[...], (((0,), (1,)), ((), ())), preferred_element_type=F32
     )
     update = lax.dot_general(
-        low_g, down_ref[0], (((0,), (0,)), ((), ())), preferred_element_type=F32
+        low_ref[0], down_ref[0], (((0,), (0,)), ((), ())), preferred_element_type=F32
     )
     input_ref[...] = (frozen + ADAPTER_SCALE * update).astype(BF16)
 
@@ -155,17 +165,32 @@
     key_width = dy.shape[0]
     groups = key_width // keys
 
+    tenants = [sequence_tenant] + [
+        lax.ppermute(sequence_tenant, "x", [(x, (x + d) % columns) for x in range(columns)])
+        for d in range(1, columns)
+    ]
+    sent = pl.pallas_call(
+        prepare,
+        out_shape=struct((slots // columns, tall, width), BF16),
+        in_specs=[VMEM, VMEM],
+        out_specs=VMEM,
+        compiler_params=WHOLE,
+        name="prepare",
+    )(adapter_down, adapter_up)
+    panels = lax.all_to_all(sent, "z", 0, 0, tiled=True)
     sent, slot_of = pl.pallas_call(
-        prepare,
-        out_shape=(struct((slots // columns, tall, width), BF16), struct((seqs,), jnp.int32)),
-        in_specs=[SMEM, SMEM, VMEM, VMEM],
+        functools.partial(select, columns),
+        out_shape=(
+            struct((columns, seqs, tall, width), BF16),
+            struct((seqs,), jnp.int32),
+        ),
+        in_specs=[VMEM] + [SMEM] * (1 + columns),
         out_specs=(VMEM, SMEM),
-        compiler_params=PARAMS,
-        name="prepare",
-    )(sequence_tenant, slot_holder_tenant, adapter_down, adapter_up)
-    panels = lax.all_to_all(sent, "z", 0, 0, tiled=True)
-    panels = jnp.broadcast_to(panels[None], (columns,) + panels.shape)
-    panels = lax.all_to_all(panels, "x", 0, 0, tiled=True)
+        scratch_shapes=[pltpu.SMEM((slots,), jnp.int32)],
+        compiler_params=PART,
+        name="select",
+    )(panels, slot_holder_tenant, *tenants)
+    panels = lax.all_to_all(sent, "x", 0, 0, tiled=True)
 
     sent, down = pl.pallas_call(
         project,
@@ -175,7 +200,7 @@
             in_specs=[
                 pl.BlockSpec(
                     (1, 1, tall, width),
-                    lambda s, slot: (slot[s] % columns, slot[s] // columns, 0, 0),
+                    lambda s, slot: (slot[s] % columns, s, 0, 0),
                 ),
                 pl.BlockSpec((rows, width), lambda s, slot: (s, 0)),
                 pl.BlockSpec((key_width, rows), lambda s, slot: (0, s)),
@@ -189,12 +214,12 @@
             struct((groups, seqs, keys, 2 * rank), BF16),
             struct((seqs, rank, width), BF16),
         ),
-        compiler_params=SERIAL,
+        compiler_params=ALL,
         name="project",
     )(slot_of, panels, activations, dy)
     got = lax.all_to_all(sent, "mp", 0, 0, tiled=True)
 
-    input_gradient, sent = pl.pallas_call(
+    low_g, sent = pl.pallas_call(
         functools.partial(combine, scale),
         grid_spec=pltpu.PrefetchScalarGridSpec(
             num_scalar_prefetch=1,
@@ -203,21 +228,38 @@
                 pl.BlockSpec((groups, 1, keys, 2 * rank), lambda s, slot: (0, s, 0, 0)),
                 pl.BlockSpec((key_width, rows), lambda s, slot: (0, s)),
                 pl.BlockSpec((rows, width), lambda s, slot: (s, 0)),
-                pl.BlockSpec((width, key_width), lambda s, slot: (0, 0)),
-                pl.BlockSpec((1, rank, width), lambda s, slot: (s, 0, 0)),
             ],
             out_specs=(
-                pl.BlockSpec((rows, width), lambda s, slot: (s, 0)),
+                pl.BlockSpec((1, rank, rows), lambda s, slot: (s, 0, 0)),
                 pl.BlockSpec((columns, 1, tall + 8, width), lambda s, slot: (0, s, 0, 0)),
             ),
         ),
         out_shape=(
-            struct(activations.shape, BF16),
+            struct((seqs, rank, rows), BF16),
             struct((columns, seqs, tall + 8, width), BF16),
         ),
-        compiler_params=SERIAL,
+        compiler_params=ALL,
         name="combine",
-    )(slot_of, got, dy, activations, key_weight, down)
+    )(slot_of, got, dy, activations)
+    input_gradient = pl.pallas_call(
+        backward,
+        grid=(seqs,),
+        in_specs=[
+            pl.BlockSpec((1, rank, rows), lambda s: (s, 0, 0)),
+            pl.BlockSpec((key_width, rows), lambda s: (0, s)),
+            pl.BlockSpec((width, key_width), lambda s: (0, 0)),
+            pl.BlockSpec((1, rank, width), lambda s: (s, 0, 0)),
+        ],
+        out_specs=pl.BlockSpec((rows, width), lambda s: (s, 0)),
+        out_shape=struct(activations.shape, BF16),
+        compiler_params=ALL,
+        cost_estimate=pl.CostEstimate(
+            flops=2 * activations.shape[0] * width * (key_width + rank),
+            bytes_accessed=2 * (activations.shape[0] + width) * (key_width + width),
+            transcendentals=0,
+        ),
+        name="backward",
+    )(low_g, dy, key_weight, down)
     got = lax.all_to_all(sent, "x", 0, 0, tiled=True)
 
     sent = pl.pallas_call(
@@ -225,7 +267,7 @@
         out_shape=struct((slots // columns, tall, width), BF16),
         in_specs=[VMEM],
         out_specs=VMEM,
-        compiler_params=PARAMS,
+        compiler_params=PART,
         name="sort",
     )(got)
     got = lax.all_to_all(sent, "z", 0, 0, tiled=True)
@@ -235,7 +277,7 @@
         out_shape=(struct((1, rank, width), F32), struct((1, rank, keys), F32)),
         in_specs=[VMEM],
         out_specs=(VMEM, VMEM),
-        compiler_params=PARAMS,
+        compiler_params=PART,
         name="finish",
     )(got)
     return (input_gradient, grad_a, grad_b)

time: 176 us -> 167 us (0.949)
  blocking collectives: 140 us -> 78.1 us
  starting transfers between devices: 0.04 us -> 25.6 us
  waiting for transfers between devices: 0.68 us -> 22.2 us
  Pallas kernels: 14.5 us -> 25.6 us
  local copies, waits for them, and re-layouts: 6.36 us -> 0.51 us
    all_to_all x3 -> x1, blocking collectives: 80.2 us -> 19.4 us  [local(): panels = lax.all_to_all(sent, 'x', 0, 0, tiled=True)]
    all_to_all x0 -> x2, waiting for transfers between devices: none -> 20.8 us  [the longest x1 13.4 us: local(): got = lax.all_to_all(sent, 'z', 0, 0, tiled=True)]
    all_to_all x0 -> x2, starting transfers between devices: none -> 14.4 us  [the longest x1 10.9 us: local(): panels = lax.all_to_all(sent, 'z', 0, 0, tiled=True)]
    ppermute x0 -> x3, starting transfers between devices: none -> 11.1 us  [local(): lax.ppermute(sequence_tenant, 'x', [(x, (x + d) % columns) for x in range...]
    pallas_call x1 -> x3, Pallas kernels: 1.29 us -> 9.11 us  [the longest x1 6.02 us: local(): pl.pallas_call(backward, grid=(seqs,), in_specs=[pl.BlockSpec((1, rank, r...]
    unnamed x16 -> x6, local copies, waits for them, and re-layouts: 6.17 us -> 0.51 us
    pallas_call x1, Pallas kernels: 3.68 us -> 6.18 us  [local(): pl.pallas_call(project, grid_spec=pltpu.PrefetchScalarGridSpec(num_scalar...]
    all_to_all x1, blocking collectives: 39.5 us -> 37.7 us  [local(): got = lax.all_to_all(sent, 'mp', 0, 0, tiled=True)]
  transfers between devices with their start and end apart: 1 -> 6, of which waited for: 0 -> 3; matrix products, arithmetic and copies ran while one was open for 0% -> 0% of each run, Pallas kernels for 1% -> 5%
where the time goes in v3:
time: 167 us; the launch traced here: 166 us
  blocking collectives  78.1 us (47%)
  starting transfers between devices  25.6 us (15%)
  Pallas kernels  25.6 us (15%)
  waiting for transfers between devices  22.2 us (13%)
  between operations  14.1 us (8%)
    all_to_all x1, blocking collectives, local(): got = lax.all_to_all(sent, 'mp', 0, 0, tiled=True)  37.7 us
    all_to_all x1, blocking collectives, local(): got = lax.all_to_all(sent, 'x', 0, 0, tiled=True)  20.9 us
    all_to_all x1, blocking collectives, local(): panels = lax.all_to_all(sent, 'x', 0, 0, tiled=True)  19.4 us
    all_to_all x1, waiting for transfers between devices, local(): got = lax.all_to_all(sent, 'z', 0, 0, tiled=True)  13.4 us
    ppermute x3, starting transfers between devices, local(): lax.ppermute(sequence_tenant, 'x', [(x, (x + d) % columns) for x in range...  11.1 us
    all_to_all x1, starting transfers between devices, local(): panels = lax.all_to_all(sent, 'z', 0, 0, tiled=True)  10.9 us
    all_to_all x1, waiting for transfers between devices, local(): panels = lax.all_to_all(sent, 'z', 0, 0, tiled=True)  7.49 us
    pallas_call x1, Pallas kernels, local(): pl.pallas_call(project, grid_spec=pltpu.PrefetchScalarGridSpec(num_scalar...  6.18 us
  transfers between devices with their start and end apart: 6, of which 3 were waited for; matrix products, arithmetic and copies ran while one was open for 0% of the time, Pallas kernels for 5%

profile of v3, /device:TPU:1, one launch (start us, length us, event | category | flops | bytes accessed | tf_op | source)
XLA Modules:
  0.0 166.1 jit_solution(7782395287870940809)
XLA Ops:
  7.2 0.0 all-gather.2.cloned.1.call-start
  7.2 0.7 all-gather.2.cloned.1.call-update
  7.9 1.8 %prepare.1 = bf16[8,72,512]{2,1,0:T(8,128)(2,1)} custom-call(bf16[1,64,512]{2,1,0:T(8,128)(2,1)} %down_ref.1, bf16[1,64,64]{2,1,0:T(8,128)(2,1)} %up_ref.1), custom_call_target="tpu_custom_call" | custom-call | tf_op jit(solution)/shard_map/prepare/pallas_call | solution.py:172
  9.7 10.9 %all-to-all-start = ((bf16[8,72,512]{2,1,0:T(8,128)(2,1)}), bf16[8,72,512]{2,1,0:T(8,128)(2,1)S(1)}, u32[]{:S(2)}, u32[]{:S(2)}) async-start(bf16[8,72,512]{2,1,0:T(8,128)(2,1)} %prepare.1), calls=%async_computation | async-start | bytes 1179648 | tf_op jit(solution)/shard_map/all_to_all | solution.py:180
  20.6 4.7 %collective-permute-start.1 = (s32[4]{0:T(128)S(1)}, s32[4]{0:T(128)S(1)}, u32[]{:S(2)}, u32[]{:S(2)}) collective-permute-start(s32[4]{0:T(128)S(1)} %copy-done.2), channel_id=1, source_target_pairs={{0,32},{16,48},{32,0},{48,16},{1,33},{17,49},{33,1},{49,17},{2,34}... | collective-permute-start | bytes 56 | tf_op jit(solution)/shard_map/ppermute | solution.py:169
  25.3 2.2 %collective-permute-start = (s32[4]{0:T(128)S(1)}, s32[4]{0:T(128)S(1)}, u32[]{:S(2)}, u32[]{:S(2)}) collective-permute-start(s32[4]{0:T(128)S(1)} %copy-done.2), channel_id=1, source_target_pairs={{0,16},{16,32},{32,48},{48,0},{1,17},{17,33},{33,49},{49,1},{2,18}... | collective-permute-start | bytes 56 | tf_op jit(solution)/shard_map/ppermute | solution.py:169
  27.5 4.3 %collective-permute-start.2 = (s32[4]{0:T(128)S(1)}, s32[4]{0:T(128)S(1)}, u32[]{:S(2)}, u32[]{:S(2)}) collective-permute-start(s32[4]{0:T(128)S(1)} %copy-done.2), channel_id=1, source_target_pairs={{0,48},{16,0},{32,16},{48,32},{1,49},{17,1},{33,17},{49,33},{2,50}... | collective-permute-start | bytes 56 | tf_op jit(solution)/shard_map/ppermute | solution.py:169
  31.8 0.0 collective-permute-done.1.refs_2_
  31.8 0.0 collective-permute-done.refs_1_
  31.8 0.7 collective-permute-done.2.refs_3_
  32.5 7.5 %all-to-all-done.panel_ref = bf16[8,72,512]{2,1,0:T(8,128)(2,1)S(1)} async-done(((bf16[8,72,512]{2,1,0:T(8,128)(2,1)}), bf16[8,72,512]{2,1,0:T(8,128)(2,1)S(1)}, u32[]{:S(2)}, u32[]{:S(2)}) %all-to-all-start) | async-done | bytes 589856 | tf_op jit(solution)/shard_map/all_to_all | solution.py:180
  40.0 1.3 select.1
  41.3 0.0 copy-start
  41.3 0.5 copy-done
  41.8 19.4 %all_to_all.25.panel_ref = bf16[4,4,72,512]{3,2,1,0:T(8,128)(2,1)} all-to-all(bf16[4,4,72,512]{3,2,1,0:T(8,128)(2,1)S(1)} %get-tuple-element.12), channel_id=1, replica_groups=mesh['z'=8,'x'=4,'mp'=16] {'x'}, dimensions={0} | all-to-all | bytes 2359296 | tf_op jit(solution)/shard_map/all_to_all | solution.py:193
  61.2 6.2 %project.1 = (bf16[16,4,64,128]{3,2,1,0:T(8,128)(2,1)}, bf16[4,64,512]{2,1,0:T(8,128)(2,1)}) custom-call(s32[4]{0:T(128)} %copy-done, bf16[4,4,72,512]{3,2,1,0:T(8,128)(2,1)} %all_to_all.25.panel_ref, bf16[1536,512]{1,0:T(8,128)(2,1)} %x_ref.3, bf16[1024,1536]{1,0:T(8,128)(2,1)} %all-gather.2.cloned.1.call-done.dy_ref), custom_call_target="tpu_custom_call" | custom-call | tf_op jit(solution)/shard_map/project/pallas_call | solution.py:195
  67.4 37.7 %all_to_all.26.got_ref = bf16[16,4,64,128]{3,2,1,0:T(8,128)(2,1)} all-to-all(bf16[16,4,64,128]{3,2,1,0:T(8,128)(2,1)} %get-tuple-element.13), channel_id=1, replica_groups=mesh['z'=8,'x'=4,'mp'=16] {'mp'}, dimensions={0} | all-to-all | bytes 2097152 | tf_op jit(solution)/shard_map/all_to_all | solution.py:220
  105.1 5.8 %combine.1 = (bf16[4,64,384]{2,1,0:T(8,128)(2,1)}, bf16[4,4,80,512]{3,2,1,0:T(8,128)(2,1)}) custom-call(s32[4]{0:T(128)} %copy-done, bf16[16,4,64,128]{3,2,1,0:T(8,128)(2,1)} %all_to_all.26.got_ref, bf16[1024,1536]{1,0:T(8,128)(2,1)} %all-gather.2.cloned.1.call-done.dy_ref, bf16[1536,512]{1,0:T(8,128)(2,1)} %x_ref.3), custom_call_target="tpu_custom_call" | custom-call | tf_op jit(solution)/shard_map/combine/pallas_call | solution.py:222
  110.9 20.9 %all_to_all.27.got_ref = bf16[4,4,80,512]{3,2,1,0:T(8,128)(2,1)S(1)} all-to-all(bf16[4,4,80,512]{3,2,1,0:T(8,128)(2,1)} %get-tuple-element.16), channel_id=1, replica_groups=mesh['z'=8,'x'=4,'mp'=16] {'x'}, dimensions={0} | all-to-all | bytes 2621440 | tf_op jit(solution)/shard_map/all_to_all | solution.py:263
  131.9 3.6 %sort.1 = bf16[8,72,512]{2,1,0:T(8,128)(2,1)} custom-call(bf16[4,4,80,512]{3,2,1,0:T(8,128)(2,1)S(1)} %all_to_all.27.got_ref), custom_call_target="tpu_custom_call" | custom-call | tf_op jit(solution)/shard_map/sort/pallas_call | solution.py:265
  135.5 3.5 %all-to-all-start.4 = ((bf16[8,72,512]{2,1,0:T(8,128)(2,1)}), bf16[8,72,512]{2,1,0:T(8,128)(2,1)S(1)}, u32[]{:S(2)}, u32[]{:S(2)}) async-start(bf16[8,72,512]{2,1,0:T(8,128)(2,1)} %sort.1), calls=%async_computation.4 | async-start | bytes 1179648 | tf_op jit(solution)/shard_map/all_to_all | solution.py:273
  139.1 6.0 %backward.1 = bf16[1536,512]{1,0:T(8,128)(2,1)} custom-call(bf16[4,64,384]{2,1,0:T(8,128)(2,1)} %get-tuple-element.14.low_ref, bf16[1024,1536]{1,0:T(8,128)(2,1)} %all-gather.2.cloned.1.call-done.dy_ref, bf16[512,1024]{1,0:T(8,128)(2,1)} %weight_ref.1, bf16[4,64,512]{2,1,0:T(8,128)(2,1)} %get-tuple-element.15.down_ref), custom_call_target="tpu_custom_call" | custom-call | flops 1711276032 | bytes 6291456 | tf_op jit(solution)/shard_map/backward/pallas_call | solution.py:244
  145.1 13.4 %all-to-all-done.4.got_ref = bf16[8,72,512]{2,1,0:T(8,128)(2,1)S(1)} async-done(((bf16[8,72,512]{2,1,0:T(8,128)(2,1)}), bf16[8,72,512]{2,1,0:T(8,128)(2,1)S(1)}, u32[]{:S(2)}, u32[]{:S(2)}) %all-to-all-start.4) | async-done | bytes 589856 | tf_op jit(solution)/shard_map/all_to_all | solution.py:273
  158.4 0.8 finish.1
  (5 shorter events, 0.0 us)
Async XLA Ops:
  7.2 13.4 %copy-start.2 = (s32[4]{0:T(128)S(1)}, s32[4]{0:T(128)}, u32[]{:S(2)}) copy-start(s32[4]{0:T(128)} %refs_0_.1) | copy-start | bytes 52
  7.2 32.8 %copy-start.1 = (s32[32]{0:T(128)S(1)}, s32[32]{0:T(128)}, u32[]{:S(2)}) copy-start(s32[32]{0:T(128)} %holder_ref.1) | copy-start | bytes 388
  7.2 54.0 %all-gather.2.cloned.1.call-start = ((), (), s32[]{:S(2)}) async-start(), calls=%async_computation.5 | async-start | bytes 3342336 | tf_op jit(solution)/shard_map/all_gather | solution.py:164
  9.7 30.2 %all-to-all-start = ((bf16[8,72,512]{2,1,0:T(8,128)(2,1)}), bf16[8,72,512]{2,1,0:T(8,128)(2,1)S(1)}, u32[]{:S(2)}, u32[]{:S(2)}) async-start(bf16[8,72,512]{2,1,0:T(8,128)(2,1)} %prepare.1), calls=%async_computation | async-start | bytes 1179648 | tf_op jit(solution)/shard_map/all_to_all | solution.py:180
  20.6 11.2 %collective-permute-start.1 = (s32[4]{0:T(128)S(1)}, s32[4]{0:T(128)S(1)}, u32[]{:S(2)}, u32[]{:S(2)}) collective-permute-start(s32[4]{0:T(128)S(1)} %copy-done.2), channel_id=1, source_target_pairs={{0,32},{16,48},{32,0},{48,16},{1,33},{17,49},{33,1},{49,17},{2,34}... | collective-permute-start | bytes 56 | tf_op jit(solution)/shard_map/ppermute | solution.py:169
  25.3 6.5 %collective-permute-start = (s32[4]{0:T(128)S(1)}, s32[4]{0:T(128)S(1)}, u32[]{:S(2)}, u32[]{:S(2)}) collective-permute-start(s32[4]{0:T(128)S(1)} %copy-done.2), channel_id=1, source_target_pairs={{0,16},{16,32},{32,48},{48,0},{1,17},{17,33},{33,49},{49,1},{2,18}... | collective-permute-start | bytes 56 | tf_op jit(solution)/shard_map/ppermute | solution.py:169
  27.5 5.0 %collective-permute-start.2 = (s32[4]{0:T(128)S(1)}, s32[4]{0:T(128)S(1)}, u32[]{:S(2)}, u32[]{:S(2)}) collective-permute-start(s32[4]{0:T(128)S(1)} %copy-done.2), channel_id=1, source_target_pairs={{0,48},{16,0},{32,16},{48,32},{1,49},{17,1},{33,17},{49,33},{2,50}... | collective-permute-start | bytes 56 | tf_op jit(solution)/shard_map/ppermute | solution.py:169
  41.3 0.5 copy-start
  135.5 22.9 %all-to-all-start.4 = ((bf16[8,72,512]{2,1,0:T(8,128)(2,1)}), bf16[8,72,512]{2,1,0:T(8,128)(2,1)S(1)}, u32[]{:S(2)}, u32[]{:S(2)}) async-start(bf16[8,72,512]{2,1,0:T(8,128)(2,1)} %sort.1), calls=%async_computation.4 | async-start | bytes 1179648 | tf_op jit(solution)/shard_map/all_to_all | solution.py:273
Sparse Core Ops, SparseCore 0:
  10.1 49.3 all-gather.1

commit v4 on v3

--- a/solution.py
+++ b/solution.py
@@ -13,8 +13,10 @@
 BF16 = jnp.bfloat16
 LANES = 128
 COLUMNS = 4
+SWAP = [(0, 1), (1, 0)]
+WHOLE = pltpu.CompilerParams(vmem_limit_bytes=58 * 2**20)
 ALL = pltpu.CompilerParams(vmem_limit_bytes=58 * 2**20, dimension_semantics=("arbitrary",))
-WHOLE = pltpu.CompilerParams(vmem_limit_bytes=58 * 2**20)
+STEPS = pltpu.CompilerParams(vmem_limit_bytes=24 * 2**20, dimension_semantics=("arbitrary",))
 PART = pltpu.CompilerParams(vmem_limit_bytes=24 * 2**20)
 VMEM = pl.BlockSpec(memory_space=pltpu.VMEM)
 SMEM = pl.BlockSpec(memory_space=pltpu.SMEM)
@@ -52,7 +54,7 @@
 
 
 def select(columns, panel_ref, holder_ref, *refs):
-    tenant_refs, (sent_ref, slot_ref, table) = refs[:columns], refs[columns:]
+    tenant_refs, (sent_ref, slot_ref, table) = refs[:columns], refs[-3:]
     for t in range(holder_ref.shape[0]):
         table[holder_ref[t]] = jnp.int32(t)
     here = lax.axis_index("x")
@@ -65,51 +67,107 @@
             sent_ref[there, s] = panel_ref[slot // columns]
 
 
-def project(slot_ref, panel_ref, x_ref, dy_ref, sent_ref, down_ref):
+def stack(chips, *refs):
+    slices, (out_ref, sem) = refs[:chips], refs[chips:]
+    here = lax.axis_index("y")
+    copies = []
+    for back, ref in enumerate(slices):
+        there = lax.rem(here + chips - back, chips)
+        copies.append(pltpu.make_async_copy(ref, out_ref.at[there], sem.at[back]))
+        copies[-1].start()
+    for copy in copies:
+        copy.wait()
+
+
+def low(slot_ref, panel0_ref, panel1_ref, x_ref, low_ref, down_ref, ups_ref):
     rank = down_ref.shape[1]
-    groups, _, keys, _ = sent_ref.shape
-    panel = panel_ref[0, 0]
-    down = panel[:rank]
-    wide = jnp.concatenate([down, jnp.zeros_like(down)], axis=0)
-    low_u = lax.dot_general(
-        x_ref[...], wide, (((1,), (1,)), ((), ())), preferred_element_type=F32
-    ).astype(BF16)
-    part = jnp.dot(dy_ref[...], low_u, preferred_element_type=F32)
-    up = unpack(panel.astype(F32)[rank:], True)
-    sent_ref[:, 0] = (part.reshape(groups, keys, 2 * rank) + up[None]).astype(BF16)
-    down_ref[0] = down
-
-
-def combine(
-    scale,
-    slot_ref,
-    got_ref,
-    dy_ref,
-    x_ref,
-    low_ref,
-    sent_ref,
-):
-    rank, width = low_ref.shape[1], x_ref.shape[1]
+    rows = low_ref.shape[1]
+    total = ups = 0.0
+    for side, panel_ref in enumerate((panel0_ref, panel1_ref)):
+        panel = panel_ref[0, 0]
+        down = panel[:rank]
+        down_ref[side] = down
+        blank = jnp.zeros_like(down)
+        wide = jnp.concatenate([blank, down] if side else [down, blank], axis=0)
+        total = total + lax.dot_general(
+            x_ref[side * rows : (side + 1) * rows],
+            wide,
+            (((1,), (1,)), ((), ())),
+            preferred_element_type=F32,
+        )
+        ups = ups + unpack(panel.astype(F32)[rank:], side == 1)
+    low_ref[0] = total.astype(BF16)
+    ups_ref[0] = ups.astype(BF16)
+
+
+def project(low_ref, other_ref, ups_ref, dy_ref, sent_ref):
+    rows = low_ref.shape[1]
+    chips, keys, _ = dy_ref.shape
+    low_u = (low_ref[0].astype(F32) + other_ref[0].astype(F32)).astype(BF16)
+    dy = dy_ref[...].reshape(chips * keys, 2 * rows)
+    parts = [
+        jnp.dot(dy[:, side * rows : (side + 1) * rows], low_u, preferred_element_type=F32)
+        for side in range(2)
+    ]
+    part = jnp.where(left_half(parts[0].shape), parts[0], parts[1])
+    sent_ref[:, 0, :keys] = part.reshape(chips, keys, LANES).astype(BF16)
+    for y in range(chips):
+        sent_ref[y, 0, keys:] = ups_ref[0]
+
+
+def lower(got_ref, dy_ref, low_ref):
+    _, rank, rows = low_ref.shape
+    chips, keys, _ = dy_ref.shape
+    ups = got_ref[:, 0, keys:].reshape(chips * keys, LANES)
+    dy = dy_ref[...].reshape(chips * keys, 2 * rows)
+    for side in range(2):
+        both = lax.dot_general(
+            ups,
+            dy[:, side * rows : (side + 1) * rows],
+            (((0,), (0,)), ((), ())),
+            preferred_element_type=F32,
+        )
+        low_ref[side] = both[side * rank : (side + 1) * rank].astype(BF16)
+
+
+def tally(scale, got_ref, part_ref):
+    keys = got_ref.shape[2] // 2
+    for pair in range(got_ref.shape[1]):
+        total = 0.0
+        for y in range(got_ref.shape[0]):
+            total = total + got_ref[y, pair, :keys].astype(F32)
+        total = scale * total
+        part_ref[2 * pair] = pack(total)
+        part_ref[2 * pair + 1] = pack(pltpu.roll(total, LANES // 2, 1))
+
+
+def combine(scale, slot_ref, low_ref, other_ref, part_ref, x_ref, low_g_ref, sent_ref):
     columns = sent_ref.shape[0]
-    got = got_ref[:, 0]
-    dy = dy_ref[...]
-    both = lax.dot_general(
-        got.reshape(-1, 2 * rank), dy, (((0,), (0,)), ((), ())), preferred_element_type=F32
-    )
-    low_g = both[rank:].astype(BF16)
-    low_ref[0] = low_g
-    part_a = jnp.dot(low_g, x_ref[...], preferred_element_type=F32)
-    part_b = jnp.sum(got.astype(F32), axis=0)
+    width = x_ref.shape[1]
+    low_g = (low_ref[0].astype(F32) + other_ref[0].astype(F32)).astype(BF16)
+    low_g_ref[0] = low_g
+    part_a = scale * jnp.dot(low_g, x_ref[...], preferred_element_type=F32)
+    part_a = part_a.astype(BF16)
+    rank = part_a.shape[0]
     slot = slot_ref[pl.program_id(0)]
     for x in range(columns):
         place = jnp.where(slot % columns == x, slot // columns, -1).astype(F32)
-        tail = jnp.concatenate([scale * pack(part_b), jnp.full((8, width), place, F32)], axis=0)
-        sent_ref[x, 0] = jnp.concatenate([scale * part_a, tail], axis=0).astype(BF16)
-
-
-def backward(low_ref, dy_ref, weight_ref, down_ref, input_ref):
+        tail = jnp.concatenate([part_ref[0], jnp.full((8, width), place, F32)], axis=0)
+        sent_ref[x, 0, :rank] = part_a
+        sent_ref[x, 0, rank:] = tail.astype(BF16)
+
+
+def backward(low_ref, dy_ref, other_ref, weight_ref, down_ref, input_ref):
+    first = lax.axis_index("c") == 0
+    dy, other = dy_ref[...], other_ref[...]
+    both = jnp.concatenate(
+        [jnp.where(first, dy, other), jnp.where(first, other, dy)], axis=1
+    )
     frozen = lax.dot_general(
-        dy_ref[...], weight_ref[...], (((0,), (1,)), ((), ())), preferred_element_type=F32
+        both.reshape(-1, dy.shape[2]),
+        weight_ref[...],
+        (((0,), (1,)), ((), ())),
+        preferred_element_type=F32,
     )
     update = lax.dot_general(
         low_ref[0], down_ref[0], (((0,), (0,)), ((), ())), preferred_element_type=F32
@@ -143,6 +201,7 @@
 
 def local(
     columns,
+    chips,
     activations,
     cotangent,
     key_weight,
@@ -161,9 +220,23 @@
     scale = ADAPTER_SCALE / math.sqrt(seqs * rows)
     struct = jax.ShapeDtypeStruct
 
-    dy = lax.all_gather(cotangent.T, "mp", axis=0, tiled=True)
-    key_width = dy.shape[0]
-    groups = key_width // keys
+    own = cotangent.T
+    slices = [own] + [
+        lax.ppermute(own, "y", [(y, (y + d) % chips) for y in range(chips)])
+        for d in range(1, chips)
+    ]
+    near = [slices[d] for d in sorted({1, 2, chips - 2, chips - 1} & set(range(1, chips)))]
+    anywhere = pl.BlockSpec(memory_space=pl.ANY)
+    dy = pl.pallas_call(
+        functools.partial(stack, chips),
+        out_shape=struct((chips,) + own.shape, BF16),
+        in_specs=[anywhere] * chips,
+        out_specs=anywhere,
+        scratch_shapes=[pltpu.SemaphoreType.DMA((chips,))],
+        compiler_params=PART,
+        name="stack",
+    )(*slices)
+    other_dy = lax.ppermute(dy, "c", SWAP)
 
     tenants = [sequence_tenant] + [
         lax.ppermute(sequence_tenant, "x", [(x, (x + d) % columns) for x in range(columns)])
@@ -184,49 +257,91 @@
             struct((columns, seqs, tall, width), BF16),
             struct((seqs,), jnp.int32),
         ),
-        in_specs=[VMEM] + [SMEM] * (1 + columns),
+        in_specs=[VMEM] + [SMEM] * (1 + columns) + [anywhere] * len(near),
         out_specs=(VMEM, SMEM),
         scratch_shapes=[pltpu.SMEM((slots,), jnp.int32)],
         compiler_params=PART,
         name="select",
-    )(panels, slot_holder_tenant, *tenants)
+    )(panels, slot_holder_tenant, *tenants, *near)
     panels = lax.all_to_all(sent, "x", 0, 0, tiled=True)
 
-    sent, down = pl.pallas_call(
-        project,
+    pairs = seqs // 2
+    low_u, down, ups = pl.pallas_call(
+        low,
         grid_spec=pltpu.PrefetchScalarGridSpec(
             num_scalar_prefetch=1,
-            grid=(seqs,),
+            grid=(pairs,),
             in_specs=[
                 pl.BlockSpec(
                     (1, 1, tall, width),
-                    lambda s, slot: (slot[s] % columns, s, 0, 0),
+                    lambda p, slot: (slot[2 * p] % columns, 2 * p, 0, 0),
                 ),
-                pl.BlockSpec((rows, width), lambda s, slot: (s, 0)),
-                pl.BlockSpec((key_width, rows), lambda s, slot: (0, s)),
+                pl.BlockSpec(
+                    (1, 1, tall, width),
+                    lambda p, slot: (slot[2 * p + 1] % columns, 2 * p + 1, 0, 0),
+                ),
+                pl.BlockSpec((2 * rows, width), lambda p, slot: (p, 0)),
             ],
             out_specs=(
-                pl.BlockSpec((groups, 1, keys, 2 * rank), lambda s, slot: (0, s, 0, 0)),
-                pl.BlockSpec((1, rank, width), lambda s, slot: (s, 0, 0)),
+                pl.BlockSpec((1, rows, 2 * rank), lambda p, slot: (p, 0, 0)),
+                pl.BlockSpec((2, rank, width), lambda p, slot: (p, 0, 0)),
+                pl.BlockSpec((1, keys, 2 * rank), lambda p, slot: (p, 0, 0)),
             ),
         ),
         out_shape=(
-            struct((groups, seqs, keys, 2 * rank), BF16),
+            struct((pairs, rows, 2 * rank), BF16),
             struct((seqs, rank, width), BF16),
+            struct((pairs, keys, 2 * rank), BF16),
         ),
         compiler_params=ALL,
+        name="low",
+    )(slot_of, panels, panels, activations)
+    other_low = lax.ppermute(low_u, "c", SWAP)
+    dy_pair = pl.BlockSpec((chips, keys, 2 * rows), lambda p: (0, 0, p))
+    mixed = pl.BlockSpec((chips, 1, 2 * keys, 2 * rank), lambda p: (0, p, 0, 0))
+    sent = pl.pallas_call(
+        project,
+        grid=(pairs,),
+        in_specs=[
+            pl.BlockSpec((1, rows, 2 * rank), lambda p: (p, 0, 0)),
+            pl.BlockSpec((1, rows, 2 * rank), lambda p: (p, 0, 0)),
+            pl.BlockSpec((1, keys, 2 * rank), lambda p: (p, 0, 0)),
+            dy_pair,
+        ],
+        out_specs=mixed,
+        out_shape=struct((chips, pairs, 2 * keys, 2 * rank), BF16),
+        compiler_params=STEPS,
         name="project",
-    )(slot_of, panels, activations, dy)
-    got = lax.all_to_all(sent, "mp", 0, 0, tiled=True)
-
+    )(low_u, other_low, ups, dy)
+    got = lax.all_to_all(sent, "y", 0, 0, tiled=True)
+
+    low_g = pl.pallas_call(
+        lower,
+        grid=(pairs,),
+        in_specs=[mixed, dy_pair],
+        out_specs=pl.BlockSpec((2, rank, rows), lambda p: (p, 0, 0)),
+        out_shape=struct((seqs, rank, rows), BF16),
+        compiler_params=STEPS,
+        name="lower",
+    )(got, dy)
+    other_low = lax.ppermute(low_g, "c", SWAP)
+    part_b = pl.pallas_call(
+        functools.partial(tally, scale),
+        in_specs=[VMEM],
+        out_specs=VMEM,
+        out_shape=struct((seqs, tall - rank, width), F32),
+        compiler_params=PART,
+        name="tally",
+    )(got)
     low_g, sent = pl.pallas_call(
         functools.partial(combine, scale),
         grid_spec=pltpu.PrefetchScalarGridSpec(
             num_scalar_prefetch=1,
             grid=(seqs,),
             in_specs=[
-                pl.BlockSpec((groups, 1, keys, 2 * rank), lambda s, slot: (0, s, 0, 0)),
-                pl.BlockSpec((key_width, rows), lambda s, slot: (0, s)),
+                pl.BlockSpec((1, rank, rows), lambda s, slot: (s, 0, 0)),
+                pl.BlockSpec((1, rank, rows), lambda s, slot: (s, 0, 0)),
+                pl.BlockSpec((1, tall - rank, width), lambda s, slot: (s, 0, 0)),
                 pl.BlockSpec((rows, width), lambda s, slot: (s, 0)),
             ],
             out_specs=(
@@ -240,26 +355,27 @@
         ),
         compiler_params=ALL,
         name="combine",
-    )(slot_of, got, dy, activations)
+    )(slot_of, low_g, other_low, part_b, activations)
     input_gradient = pl.pallas_call(
         backward,
         grid=(seqs,),
         in_specs=[
             pl.BlockSpec((1, rank, rows), lambda s: (s, 0, 0)),
-            pl.BlockSpec((key_width, rows), lambda s: (0, s)),
-            pl.BlockSpec((width, key_width), lambda s: (0, 0)),
+            pl.BlockSpec((chips, keys, rows), lambda s: (0, 0, s)),
+            pl.BlockSpec((chips, keys, rows), lambda s: (0, 0, s)),
+            pl.BlockSpec(key_weight.shape, lambda s: (0, 0)),
             pl.BlockSpec((1, rank, width), lambda s: (s, 0, 0)),
         ],
         out_specs=pl.BlockSpec((rows, width), lambda s: (s, 0)),
         out_shape=struct(activations.shape, BF16),
         compiler_params=ALL,
         cost_estimate=pl.CostEstimate(
-            flops=2 * activations.shape[0] * width * (key_width + rank),
-            bytes_accessed=2 * (activations.shape[0] + width) * (key_width + width),
+            flops=2 * activations.shape[0] * width * (key_weight.shape[1] + rank),
+            bytes_accessed=2 * (activations.shape[0] + width) * (key_weight.shape[1] + width),
             transcendentals=0,
         ),
         name="backward",
-    )(low_g, dy, key_weight, down)
+    )(low_g, dy, other_dy, key_weight, down)
     got = lax.all_to_all(sent, "x", 0, 0, tiled=True)
 
     sent = pl.pallas_call(
@@ -285,17 +401,18 @@
 
 def solution(mesh):
     columns = min(COLUMNS, mesh.shape["dp"] // 2)
-    grid = Mesh(mesh.devices.reshape(-1, columns, mesh.shape["mp"]), ("z", "x", "mp"))
-    dp = ("z", "x")
+    chips = mesh.shape["mp"] // 2
+    grid = Mesh(mesh.devices.reshape(-1, columns, chips, 2), ("z", "x", "y", "c"))
+    dp, mp = ("z", "x"), ("y", "c")
     in_specs = (
-        P(dp, "mp"),
-        P(dp, "mp"),
-        P("mp", None),
-        P(dp, None, "mp"),
-        P(dp, None, "mp"),
+        P(dp, mp),
+        P(dp, mp),
+        P(mp, None),
+        P(dp, None, mp),
+        P(dp, None, mp),
         P(dp),
         P(),
     )
-    out_specs = (P(dp, "mp"), P(dp, None, "mp"), P(dp, None, "mp"))
-    body = functools.partial(local, columns)
+    out_specs = (P(dp, mp), P(dp, None, mp), P(dp, None, mp))
+    body = functools.partial(local, columns, chips)
     return jax.shard_map(body, mesh=grid, in_specs=in_specs, out_specs=out_specs, check_vma=False)

time: 167 us -> 168 us (level)
  blocking collectives: 78.1 us -> 18.5 us
  starting transfers between devices: 25.6 us -> 77.2 us
  waiting for transfers between devices: 22.2 us -> 41.5 us
  between operations: 14.1 us -> 0.95 us
  local copies, waits for them, and re-layouts: 0.51 us -> 2.86 us
    all_to_all x3 -> x1, blocking collectives: 78.1 us -> 18.5 us  [local(): got = lax.all_to_all(sent, 'y', 0, 0, tiled=True)]
    ppermute x0 -> x10, starting transfers between devices: none -> 40.9 us  [the longest x7 26 us: local(): lax.ppermute(own, 'y', [(y, (y + d) % chips) for y in range(chips)])]
    all_to_all x0 -> x2, waiting for transfers between devices: none -> 14.8 us  [the longest x1 14.8 us: local(): got = lax.all_to_all(sent, 'x', 0, 0, tiled=True)]
    ppermute x0 -> x10, waiting for transfers between devices: none -> 10.1 us  [the longest x7 9.87 us: local(): lax.ppermute(own, 'y', [(y, (y + d) % chips) for y in range(chips)])]
    all_to_all x0 -> x2, starting transfers between devices: none -> 7.84 us  [the longest x1 4.09 us: local(): got = lax.all_to_all(sent, 'x', 0, 0, tiled=True)]
    all_to_all x1, waiting for transfers between devices: 7.49 us -> 0.01 us  [local(): panels = lax.all_to_all(sent, 'z', 0, 0, tiled=True)]
    ppermute x3, waiting for transfers between devices: 0.68 us -> 5.19 us  [local(): lax.ppermute(sequence_tenant, 'x', [(x, (x + d) % columns) for x in range...]
    all_to_all x1, starting transfers between devices: 3.54 us -> 6.65 us  [local(): got = lax.all_to_all(sent, 'z', 0, 0, tiled=True)]
  transfers between devices with their start and end apart: 6 -> 17, of which waited for: 3 -> 7; matrix products, arithmetic and copies ran while one was open for 0% -> 0% of each run, Pallas kernels for 5% -> 9%
where the time goes in v4:
time: 168 us; the launch traced here: 167 us
  starting transfers between devices  77.2 us (46%)
  waiting for transfers between devices  41.5 us (25%)
  Pallas kernels  25.9 us (15%)
  blocking collectives  18.5 us (11%)
  local copies, waits for them, and re-layouts  2.86 us (2%)
    ppermute x7, starting transfers between devices, local(): lax.ppermute(own, 'y', [(y, (y + d) % chips) for y in range(chips)])  26 us
    all_to_all x1, blocking collectives, local(): got = lax.all_to_all(sent, 'y', 0, 0, tiled=True)  18.5 us
    all_to_all x1, waiting for transfers between devices, local(): got = lax.all_to_all(sent, 'x', 0, 0, tiled=True)  14.8 us
    all_to_all x1, waiting for transfers between devices, local(): got = lax.all_to_all(sent, 'z', 0, 0, tiled=True)  11.4 us
    ppermute x3, starting transfers between devices, local(): lax.ppermute(sequence_tenant, 'x', [(x, (x + d) % columns) for x in range...  10.9 us
    all_to_all x1, starting transfers between devices, local(): panels = lax.all_to_all(sent, 'z', 0, 0, tiled=True)  10.9 us
    ppermute x7, waiting for transfers between devices, local(): lax.ppermute(own, 'y', [(y, (y + d) % chips) for y in range(chips)])  9.87 us
    ppermute x1, starting transfers between devices, local(): other_low = lax.ppermute(low_u, 'c', SWAP)  8.09 us
  transfers between devices with their start and end apart: 17, of which 7 were waited for; matrix products, arithmetic and copies ran while one was open for 0% of the time, Pallas kernels for 9%

profile of v4, /device:TPU:1, one launch (start us, length us, event | category | flops | bytes accessed | tf_op | source)
XLA Modules:
  0.0 166.9 jit_solution(16795796799283281031)
XLA Ops:
  2.5 10.9 %all-to-all-start = ((bf16[8,72,512]{2,1,0:T(8,128)(2,1)}), bf16[8,72,512]{2,1,0:T(8,128)(2,1)S(1)}, u32[]{:S(2)}, u32[]{:S(2)}) async-start(bf16[8,72,512]{2,1,0:T(8,128)(2,1)} %prepare.1), calls=%async_computation | async-start | bytes 1179648 | tf_op jit(solution)/shard_map/all_to_all | solution.py:253
  13.4 5.1 %collective-permute-start.6 = (bf16[64,1536]{1,0:T(8,128)(2,1)S(1)}, bf16[64,1536]{1,0:T(8,128)(2,1)S(1)}, u32[]{:S(2)}, u32[]{:S(2)}) collective-permute-start(bf16[64,1536]{1,0:T(8,128)(2,1)S(1)} %bitcast.1), channel_id=1, source_target_pairs={{0,14},{2,0},{4,2},{6,4},{8,6},{10,8},{12,10},{14,12},{1,15},{3,1}... | collective-permute-start | bytes 589832 | tf_op jit(solution)/shard_map/ppermute | solution.py:225
  18.5 3.8 %collective-permute-start.5 = (bf16[64,1536]{1,0:T(8,128)(2,1)S(1)}, bf16[64,1536]{1,0:T(8,128)(2,1)S(1)}, u32[]{:S(2)}, u32[]{:S(2)}) collective-permute-start(bf16[64,1536]{1,0:T(8,128)(2,1)S(1)} %bitcast.2), channel_id=1, source_target_pairs={{0,12},{2,14},{4,0},{6,2},{8,4},{10,6},{12,8},{14,10},{1,13},{3,15... | collective-permute-start | bytes 589832 | tf_op jit(solution)/shard_map/ppermute | solution.py:225
  26.6 4.7 %collective-permute-start.1 = (s32[4]{0:T(128)S(1)}, s32[4]{0:T(128)S(1)}, u32[]{:S(2)}, u32[]{:S(2)}) collective-permute-start(s32[4]{0:T(128)S(1)} %copy-done.8), channel_id=1, source_target_pairs={{0,32},{16,48},{32,0},{48,16},{1,33},{17,49},{33,1},{49,17},{2,34}... | collective-permute-start | bytes 56 | tf_op jit(solution)/shard_map/ppermute | solution.py:242
  32.7 3.1 %collective-permute-start = (s32[4]{0:T(128)S(1)}, s32[4]{0:T(128)S(1)}, u32[]{:S(2)}, u32[]{:S(2)}) collective-permute-start(s32[4]{0:T(128)S(1)} %copy-done.8), channel_id=1, source_target_pairs={{0,16},{16,32},{32,48},{48,0},{1,17},{17,33},{33,49},{49,1},{2,18}... | collective-permute-start | bytes 56 | tf_op jit(solution)/shard_map/ppermute | solution.py:242
  35.8 2.7 %collective-permute-done.refs_1_ = s32[4]{0:T(128)S(1)} collective-permute-done((s32[4]{0:T(128)S(1)}, s32[4]{0:T(128)S(1)}, u32[]{:S(2)}, u32[]{:S(2)}) %collective-permute-start) | collective-permute-done | bytes 48 | tf_op jit(solution)/shard_map/ppermute | solution.py:242
  38.5 3.2 %collective-permute-start.2 = (s32[4]{0:T(128)S(1)}, s32[4]{0:T(128)S(1)}, u32[]{:S(2)}, u32[]{:S(2)}) collective-permute-start(s32[4]{0:T(128)S(1)} %copy-done.8), channel_id=1, source_target_pairs={{0,48},{16,0},{32,16},{48,32},{1,49},{17,1},{33,17},{49,33},{2,50}... | collective-permute-start | bytes 56 | tf_op jit(solution)/shard_map/ppermute | solution.py:242
  45.1 3.7 %all-to-all-start.1 = ((bf16[4,4,72,512]{3,2,1,0:T(8,128)(2,1)}), bf16[4,4,72,512]{3,2,1,0:T(8,128)(2,1)S(1)}, u32[]{:S(2)}, u32[]{:S(2)}) async-start(bf16[4,4,72,512]{3,2,1,0:T(8,128)(2,1)} %get-tuple-element.13), calls=%async_computation.1 | async-start | bytes 2359296 | tf_op jit(solution)/shard_map/all_to_all | solution.py:266
  48.8 6.0 %collective-permute-start.10 = (bf16[64,1536]{1,0:T(8,128)(2,1)S(1)}, bf16[64,1536]{1,0:T(8,128)(2,1)S(1)}, u32[]{:S(2)}, u32[]{:S(2)}) collective-permute-start(bf16[64,1536]{1,0:T(8,128)(2,1)S(1)} %bitcast.5), channel_id=1, source_target_pairs={{0,10},{2,12},{4,14},{6,0},{8,2},{10,4},{12,6},{14,8},{1,11},{3,13... | collective-permute-start | bytes 589832 | tf_op jit(solution)/shard_map/ppermute | solution.py:225
  54.9 2.7 %collective-permute-start.9 = (bf16[64,1536]{1,0:T(8,128)(2,1)S(1)}, bf16[64,1536]{1,0:T(8,128)(2,1)S(1)}, u32[]{:S(2)}, u32[]{:S(2)}) collective-permute-start(bf16[64,1536]{1,0:T(8,128)(2,1)S(1)} %bitcast.6), channel_id=1, source_target_pairs={{0,8},{2,10},{4,12},{6,14},{8,0},{10,2},{12,4},{14,6},{1,9},{3,11}... | collective-permute-start | bytes 589832 | tf_op jit(solution)/shard_map/ppermute | solution.py:225
  57.6 4.0 %collective-permute-start.8 = (bf16[64,1536]{1,0:T(8,128)(2,1)S(1)}, bf16[64,1536]{1,0:T(8,128)(2,1)S(1)}, u32[]{:S(2)}, u32[]{:S(2)}) collective-permute-start(bf16[64,1536]{1,0:T(8,128)(2,1)S(1)} %bitcast.7), channel_id=1, source_target_pairs={{0,6},{2,8},{4,10},{6,12},{8,14},{10,0},{12,2},{14,4},{1,7},{3,9},... | collective-permute-start | bytes 589832 | tf_op jit(solution)/shard_map/ppermute | solution.py:225
  62.7 3.3 %low.1 = (bf16[2,384,128]{2,1,0:T(8,128)(2,1)}, bf16[4,64,512]{2,1,0:T(8,128)(2,1)}, bf16[2,64,128]{2,1,0:T(8,128)(2,1)}) custom-call(s32[4]{0:T(128)} %copy-done.6, bf16[4,4,72,512]{3,2,1,0:T(8,128)(2,1)} %copy-done.9, bf16[4,4,72,512]{3,2,1,0:T(8,128)(2,1)} %copy-done.9, bf16[1536,512]{1,0:T(8,128)(2,1)} %x_ref.3), custom_call_target="tpu_custom_call" | custom-call | tf_op jit(solution)/shard_map/low/pallas_call | solution.py:269
  66.0 8.1 %collective-permute-start.7 = (bf16[2,384,128]{2,1,0:T(8,128)(2,1)}, bf16[2,384,128]{2,1,0:T(8,128)(2,1)S(1)}, u32[]{:S(2)}, u32[]{:S(2)}) collective-permute-start(bf16[2,384,128]{2,1,0:T(8,128)(2,1)} %get-tuple-element.14.low_ref), channel_id=1, source_target_pairs={{0,1},{1,0},{2,3},{3,2},{4,5},{5,4},{6,7},{7,6},{8,9},{9,8},{10,11... | collective-permute-start | bytes 589832 | tf_op jit(solution)/shard_map/ppermute | solution.py:299
  74.1 9.9 %collective-permute-done.8.refs_3_ = bf16[64,1536]{1,0:T(8,128)(2,1)S(1)} collective-permute-done((bf16[64,1536]{1,0:T(8,128)(2,1)S(1)}, bf16[64,1536]{1,0:T(8,128)(2,1)S(1)}, u32[]{:S(2)}, u32[]{:S(2)}) %collective-permute-start.8) | collective-permute-done | bytes 196640 | tf_op jit(solution)/shard_map/ppermute | solution.py:225
  87.1 18.5 %all_to_all.25.got_ref = bf16[8,2,128,128]{3,2,1,0:T(8,128)(2,1)S(1)} all-to-all(bf16[8,2,128,128]{3,2,1,0:T(8,128)(2,1)S(1)} %project.1), channel_id=1, replica_groups=mesh['z'=8,'x'=4,'y'=8,'c'=2] {'y'}, dimensions={0} | all-to-all | bytes 1048576 | tf_op jit(solution)/shard_map/all_to_all | solution.py:316
  106.4 4.2 %collective-permute-start.11 = (bf16[4,64,384]{2,1,0:T(8,128)(2,1)S(1)}, bf16[4,64,384]{2,1,0:T(8,128)(2,1)S(1)}, u32[]{:S(2)}, u32[]{:S(2)}) collective-permute-start(bf16[4,64,384]{2,1,0:T(8,128)(2,1)S(1)} %lower.1.low_ref), channel_id=1, source_target_pairs={{0,1},{1,0},{2,3},{3,2},{4,5},{5,4},{6,7},{7,6},{8,9},{9,8},{10,11... | collective-permute-start | bytes 589832 | tf_op jit(solution)/shard_map/ppermute | solution.py:327
  112.4 4.7 %combine.1 = (bf16[4,64,384]{2,1,0:T(8,128)(2,1)}, bf16[4,4,80,512]{3,2,1,0:T(8,128)(2,1)}) custom-call(s32[4]{0:T(128)} %copy-done.6, bf16[4,64,384]{2,1,0:T(8,128)(2,1)} %copy-done.1, bf16[4,64,384]{2,1,0:T(8,128)(2,1)} %copy-done.10, f32[4,8,512]{2,1,0:T(8,128)} %copy-done.2, bf16[1536,512]{1,0:T(8,128)(2,1)} %x_ref.3), custom_call_target="tpu_custom_call" | custom-call | tf_op jit(solution)/shard_map/combine/pallas_call | solution.py:336
  117.1 4.1 %all-to-all-start.3 = ((bf16[4,4,80,512]{3,2,1,0:T(8,128)(2,1)}), bf16[4,4,80,512]{3,2,1,0:T(8,128)(2,1)S(1)}, u32[]{:S(2)}, u32[]{:S(2)}) async-start(bf16[4,4,80,512]{3,2,1,0:T(8,128)(2,1)} %get-tuple-element.18), calls=%async_computation.3 | async-start | bytes 2621440 | tf_op jit(solution)/shard_map/all_to_all | solution.py:379
  121.2 2.5 %collective-permute-start.12 = (bf16[8,64,1536]{2,1,0:T(8,128)(2,1)S(1)}, bf16[8,64,1536]{2,1,0:T(8,128)(2,1)}, u32[]{:S(2)}, u32[]{:S(2)}) collective-permute-start(bf16[8,64,1536]{2,1,0:T(8,128)(2,1)S(1)} %stack.1.dy_ref), channel_id=1, source_target_pairs={{0,1},{1,0},{2,3},{3,2},{4,5},{5,4},{6,7},{7,6},{8,9},{9,8},{10,11... | collective-permute-start | bytes 4718600 | tf_op jit(solution)/shard_map/ppermute | solution.py:239
  123.8 14.8 %all-to-all-done.3.got_ref = bf16[4,4,80,512]{3,2,1,0:T(8,128)(2,1)S(1)} async-done(((bf16[4,4,80,512]{3,2,1,0:T(8,128)(2,1)}), bf16[4,4,80,512]{3,2,1,0:T(8,128)(2,1)S(1)}, u32[]{:S(2)}, u32[]{:S(2)}) %all-to-all-start.3) | async-done | bytes 1310752 | tf_op jit(solution)/shard_map/all_to_all | solution.py:379
  138.5 3.5 %sort.1 = bf16[8,72,512]{2,1,0:T(8,128)(2,1)} custom-call(bf16[4,4,80,512]{3,2,1,0:T(8,128)(2,1)S(1)} %all-to-all-done.3.got_ref), custom_call_target="tpu_custom_call" | custom-call | tf_op jit(solution)/shard_map/sort/pallas_call | solution.py:381
  142.1 6.6 %all-to-all-start.4 = ((bf16[8,72,512]{2,1,0:T(8,128)(2,1)}), bf16[8,72,512]{2,1,0:T(8,128)(2,1)S(1)}, u32[]{:S(2)}, u32[]{:S(2)}) async-start(bf16[8,72,512]{2,1,0:T(8,128)(2,1)} %sort.1), calls=%async_computation.4 | async-start | bytes 1179648 | tf_op jit(solution)/shard_map/all_to_all | solution.py:389
  148.7 5.9 %backward.1 = bf16[1536,512]{1,0:T(8,128)(2,1)} custom-call(bf16[4,64,384]{2,1,0:T(8,128)(2,1)} %get-tuple-element.16.low_ref, bf16[8,64,1536]{2,1,0:T(8,128)(2,1)} %copy-done, bf16[8,64,1536]{2,1,0:T(8,128)(2,1)} %collective-permute-done.12.other_ref, bf16[512,1024]{1,0:T(8,128)(2,1)} %weight_ref.1, bf16[4,64,512]{2,1,0:T(8,128)(2,1)} %get-tuple-element.17.down_ref), custom_call_target="tpu_custom_call" | custom-call | flops 1711276032 | bytes 6291456 | tf_op jit(solution)/shard_map/backward/pallas_call | solution.py:359
  154.6 11.4 %all-to-all-done.4.got_ref = bf16[8,72,512]{2,1,0:T(8,128)(2,1)S(1)} async-done(((bf16[8,72,512]{2,1,0:T(8,128)(2,1)}), bf16[8,72,512]{2,1,0:T(8,128)(2,1)S(1)}, u32[]{:S(2)}, u32[]{:S(2)}) %all-to-all-start.4) | async-done | bytes 589856 | tf_op jit(solution)/shard_map/all_to_all | solution.py:389
  (44 shorter events, 18.5 us)
Async XLA Ops:
  0.6 12.8 %copy-start.3 = (bf16[1536,64]{0,1:T(8,128)(2,1)S(1)}, bf16[1536,64]{0,1:T(8,128)(2,1)}, u32[]{:S(2)}) copy-start(bf16[1536,64]{0,1:T(8,128)(2,1)} %param.8) | copy-start | bytes 589828
  0.6 26.0 %copy-start.8 = (s32[4]{0:T(128)S(1)}, s32[4]{0:T(128)}, u32[]{:S(2)}) copy-start(s32[4]{0:T(128)} %refs_0_.1) | copy-start | bytes 52
  0.7 42.2 %copy-start.7 = (s32[32]{0:T(128)S(1)}, s32[32]{0:T(128)}, u32[]{:S(2)}) copy-start(s32[32]{0:T(128)} %holder_ref.1) | copy-start | bytes 388
  2.5 40.3 %all-to-all-start = ((bf16[8,72,512]{2,1,0:T(8,128)(2,1)}), bf16[8,72,512]{2,1,0:T(8,128)(2,1)S(1)}, u32[]{:S(2)}, u32[]{:S(2)}) async-start(bf16[8,72,512]{2,1,0:T(8,128)(2,1)} %prepare.1), calls=%async_computation | async-start | bytes 1179648 | tf_op jit(solution)/shard_map/all_to_all | solution.py:253
  13.4 29.4 %collective-permute-start.6 = (bf16[64,1536]{1,0:T(8,128)(2,1)S(1)}, bf16[64,1536]{1,0:T(8,128)(2,1)S(1)}, u32[]{:S(2)}, u32[]{:S(2)}) collective-permute-start(bf16[64,1536]{1,0:T(8,128)(2,1)S(1)} %bitcast.1), channel_id=1, source_target_pairs={{0,14},{2,0},{4,2},{6,4},{8,6},{10,8},{12,10},{14,12},{1,15},{3,1}... | collective-permute-start | bytes 589832 | tf_op jit(solution)/shard_map/ppermute | solution.py:225
  18.5 24.3 %collective-permute-start.5 = (bf16[64,1536]{1,0:T(8,128)(2,1)S(1)}, bf16[64,1536]{1,0:T(8,128)(2,1)S(1)}, u32[]{:S(2)}, u32[]{:S(2)}) collective-permute-start(bf16[64,1536]{1,0:T(8,128)(2,1)S(1)} %bitcast.2), channel_id=1, source_target_pairs={{0,12},{2,14},{4,0},{6,2},{8,4},{10,6},{12,8},{14,10},{1,13},{3,15... | collective-permute-start | bytes 589832 | tf_op jit(solution)/shard_map/ppermute | solution.py:225
  22.3 20.5 %collective-permute-start.4 = (bf16[64,1536]{1,0:T(8,128)(2,1)S(1)}, bf16[64,1536]{1,0:T(8,128)(2,1)S(1)}, u32[]{:S(2)}, u32[]{:S(2)}) collective-permute-start(bf16[64,1536]{1,0:T(8,128)(2,1)S(1)} %bitcast.3), channel_id=1, source_target_pairs={{0,4},{2,6},{4,8},{6,10},{8,12},{10,14},{12,0},{14,2},{1,5},{3,7},... | collective-permute-start | bytes 589832 | tf_op jit(solution)/shard_map/ppermute | solution.py:225
  24.7 18.1 %collective-permute-start.3 = (bf16[64,1536]{1,0:T(8,128)(2,1)S(1)}, bf16[64,1536]{1,0:T(8,128)(2,1)S(1)}, u32[]{:S(2)}, u32[]{:S(2)}) collective-permute-start(bf16[64,1536]{1,0:T(8,128)(2,1)S(1)} %bitcast.4), channel_id=1, source_target_pairs={{0,2},{2,4},{4,6},{6,8},{8,10},{10,12},{12,14},{14,0},{1,3},{3,5},... | collective-permute-start | bytes 589832 | tf_op jit(solution)/shard_map/ppermute | solution.py:225
  26.6 6.1 %collective-permute-start.1 = (s32[4]{0:T(128)S(1)}, s32[4]{0:T(128)S(1)}, u32[]{:S(2)}, u32[]{:S(2)}) collective-permute-start(s32[4]{0:T(128)S(1)} %copy-done.8), channel_id=1, source_target_pairs={{0,32},{16,48},{32,0},{48,16},{1,33},{17,49},{33,1},{49,17},{2,34}... | collective-permute-start | bytes 56 | tf_op jit(solution)/shard_map/ppermute | solution.py:242
  32.7 5.8 %collective-permute-start = (s32[4]{0:T(128)S(1)}, s32[4]{0:T(128)S(1)}, u32[]{:S(2)}, u32[]{:S(2)}) collective-permute-start(s32[4]{0:T(128)S(1)} %copy-done.8), channel_id=1, source_target_pairs={{0,16},{16,32},{32,48},{48,0},{1,17},{17,33},{33,49},{49,1},{2,18}... | collective-permute-start | bytes 56 | tf_op jit(solution)/shard_map/ppermute | solution.py:242
  38.5 4.3 %collective-permute-start.2 = (s32[4]{0:T(128)S(1)}, s32[4]{0:T(128)S(1)}, u32[]{:S(2)}, u32[]{:S(2)}) collective-permute-start(s32[4]{0:T(128)S(1)} %copy-done.8), channel_id=1, source_target_pairs={{0,48},{16,0},{32,16},{48,32},{1,49},{17,1},{33,17},{49,33},{2,50}... | collective-permute-start | bytes 56 | tf_op jit(solution)/shard_map/ppermute | solution.py:242
  45.1 16.6 %all-to-all-start.1 = ((bf16[4,4,72,512]{3,2,1,0:T(8,128)(2,1)}), bf16[4,4,72,512]{3,2,1,0:T(8,128)(2,1)S(1)}, u32[]{:S(2)}, u32[]{:S(2)}) async-start(bf16[4,4,72,512]{3,2,1,0:T(8,128)(2,1)} %get-tuple-element.13), calls=%async_computation.1 | async-start | bytes 2359296 | tf_op jit(solution)/shard_map/all_to_all | solution.py:266
  48.8 25.2 %collective-permute-start.10 = (bf16[64,1536]{1,0:T(8,128)(2,1)S(1)}, bf16[64,1536]{1,0:T(8,128)(2,1)S(1)}, u32[]{:S(2)}, u32[]{:S(2)}) collective-permute-start(bf16[64,1536]{1,0:T(8,128)(2,1)S(1)} %bitcast.5), channel_id=1, source_target_pairs={{0,10},{2,12},{4,14},{6,0},{8,2},{10,4},{12,6},{14,8},{1,11},{3,13... | collective-permute-start | bytes 589832 | tf_op jit(solution)/shard_map/ppermute | solution.py:225
  54.9 19.2 %collective-permute-start.9 = (bf16[64,1536]{1,0:T(8,128)(2,1)S(1)}, bf16[64,1536]{1,0:T(8,128)(2,1)S(1)}, u32[]{:S(2)}, u32[]{:S(2)}) collective-permute-start(bf16[64,1536]{1,0:T(8,128)(2,1)S(1)} %bitcast.6), channel_id=1, source_target_pairs={{0,8},{2,10},{4,12},{6,14},{8,0},{10,2},{12,4},{14,6},{1,9},{3,11}... | collective-permute-start | bytes 589832 | tf_op jit(solution)/shard_map/ppermute | solution.py:225
  57.6 26.3 %collective-permute-start.8 = (bf16[64,1536]{1,0:T(8,128)(2,1)S(1)}, bf16[64,1536]{1,0:T(8,128)(2,1)S(1)}, u32[]{:S(2)}, u32[]{:S(2)}) collective-permute-start(bf16[64,1536]{1,0:T(8,128)(2,1)S(1)} %bitcast.7), channel_id=1, source_target_pairs={{0,6},{2,8},{4,10},{6,12},{8,14},{10,0},{12,2},{14,4},{1,7},{3,9},... | collective-permute-start | bytes 589832 | tf_op jit(solution)/shard_map/ppermute | solution.py:225
  66.0 20.1 %copy-start.4 = (bf16[2,384,128]{2,1,0:T(8,128)(2,1)S(1)}, bf16[2,384,128]{2,1,0:T(8,128)(2,1)}, u32[]{:S(2)}) copy-start(bf16[2,384,128]{2,1,0:T(8,128)(2,1)} %get-tuple-element.14.low_ref) | copy-start | bytes 589828
  66.0 20.1 %copy-start.5 = (bf16[2,64,128]{2,1,0:T(8,128)(2,1)S(1)}, bf16[2,64,128]{2,1,0:T(8,128)(2,1)}, u32[]{:S(2)}) copy-start(bf16[2,64,128]{2,1,0:T(8,128)(2,1)} %get-tuple-element.15.ups_ref) | copy-start | bytes 98308
  66.0 20.1 %collective-permute-start.7 = (bf16[2,384,128]{2,1,0:T(8,128)(2,1)}, bf16[2,384,128]{2,1,0:T(8,128)(2,1)S(1)}, u32[]{:S(2)}, u32[]{:S(2)}) collective-permute-start(bf16[2,384,128]{2,1,0:T(8,128)(2,1)} %get-tuple-element.14.low_ref), channel_id=1, source_target_pairs={{0,1},{1,0},{2,3},{3,2},{4,5},{5,4},{6,7},{7,6},{8,9},{9,8},{10,11... | collective-permute-start | bytes 589832 | tf_op jit(solution)/shard_map/ppermute | solution.py:299
  86.1 35.1 %copy-start = (bf16[8,64,1536]{2,1,0:T(8,128)(2,1)}, bf16[8,64,1536]{2,1,0:T(8,128)(2,1)S(1)}, u32[]{:S(2)}) copy-start(bf16[8,64,1536]{2,1,0:T(8,128)(2,1)S(1)} %stack.1.dy_ref) | copy-start | bytes 4718596
  106.4 5.3 %copy-start.1 = (bf16[4,64,384]{2,1,0:T(8,128)(2,1)}, bf16[4,64,384]{2,1,0:T(8,128)(2,1)S(1)}, u32[]{:S(2)}) copy-start(bf16[4,64,384]{2,1,0:T(8,128)(2,1)S(1)} %lower.1.low_ref) | copy-start | bytes 589828
  106.4 5.3 %collective-permute-start.11 = (bf16[4,64,384]{2,1,0:T(8,128)(2,1)S(1)}, bf16[4,64,384]{2,1,0:T(8,128)(2,1)S(1)}, u32[]{:S(2)}, u32[]{:S(2)}) collective-permute-start(bf16[4,64,384]{2,1,0:T(8,128)(2,1)S(1)} %lower.1.low_ref), channel_id=1, source_target_pairs={{0,1},{1,0},{2,3},{3,2},{4,5},{5,4},{6,7},{7,6},{8,9},{9,8},{10,11... | collective-permute-start | bytes 589832 | tf_op jit(solution)/shard_map/ppermute | solution.py:327
  117.1 21.4 %all-to-all-start.3 = ((bf16[4,4,80,512]{3,2,1,0:T(8,128)(2,1)}), bf16[4,4,80,512]{3,2,1,0:T(8,128)(2,1)S(1)}, u32[]{:S(2)}, u32[]{:S(2)}) async-start(bf16[4,4,80,512]{3,2,1,0:T(8,128)(2,1)} %get-tuple-element.18), calls=%async_computation.3 | async-start | bytes 2621440 | tf_op jit(solution)/shard_map/all_to_all | solution.py:379
  121.2 27.5 %collective-permute-start.12 = (bf16[8,64,1536]{2,1,0:T(8,128)(2,1)S(1)}, bf16[8,64,1536]{2,1,0:T(8,128)(2,1)}, u32[]{:S(2)}, u32[]{:S(2)}) collective-permute-start(bf16[8,64,1536]{2,1,0:T(8,128)(2,1)S(1)} %stack.1.dy_ref), channel_id=1, source_target_pairs={{0,1},{1,0},{2,3},{3,2},{4,5},{5,4},{6,7},{7,6},{8,9},{9,8},{10,11... | collective-permute-start | bytes 4718600 | tf_op jit(solution)/shard_map/ppermute | solution.py:239
  142.1 24.0 %all-to-all-start.4 = ((bf16[8,72,512]{2,1,0:T(8,128)(2,1)}), bf16[8,72,512]{2,1,0:T(8,128)(2,1)S(1)}, u32[]{:S(2)}, u32[]{:S(2)}) async-start(bf16[8,72,512]{2,1,0:T(8,128)(2,1)} %sort.1), calls=%async_computation.4 | async-start | bytes 1179648 | tf_op jit(solution)/shard_map/all_to_all | solution.py:389
  (4 other events, 2.9 us)

commit v5 on v4

--- a/solution.py
+++ b/solution.py
@@ -54,29 +54,21 @@
 
 
 def select(columns, panel_ref, holder_ref, *refs):
-    tenant_refs, (sent_ref, slot_ref, table) = refs[:columns], refs[-3:]
+    tenant_refs, (sent_ref, slot_ref, place_ref, table) = refs[:columns], refs[columns:]
+    seqs = sent_ref.shape[1]
     for t in range(holder_ref.shape[0]):
         table[holder_ref[t]] = jnp.int32(t)
     here = lax.axis_index("x")
+    slot_ref[seqs] = lax.axis_index("c")
     for back, tenant_ref in enumerate(tenant_refs):
         there = lax.rem(here + columns - back, columns)
-        for s in range(tenant_ref.shape[0]):
+        for s in range(seqs):
             slot = table[tenant_ref[s]]
+            row, column = slot // columns, slot % columns
             if back == 0:
                 slot_ref[s] = slot
-            sent_ref[there, s] = panel_ref[slot // columns]
-
-
-def stack(chips, *refs):
-    slices, (out_ref, sem) = refs[:chips], refs[chips:]
-    here = lax.axis_index("y")
-    copies = []
-    for back, ref in enumerate(slices):
-        there = lax.rem(here + chips - back, chips)
-        copies.append(pltpu.make_async_copy(ref, out_ref.at[there], sem.at[back]))
-        copies[-1].start()
-    for copy in copies:
-        copy.wait()
+            place_ref[there * seqs + s] = jnp.where(column == here, row, -1)
+            sent_ref[there, s] = panel_ref[row]
 
 
 def low(slot_ref, panel0_ref, panel1_ref, x_ref, low_ref, down_ref, ups_ref):
@@ -100,9 +92,9 @@
     ups_ref[0] = ups.astype(BF16)
 
 
-def project(low_ref, other_ref, ups_ref, dy_ref, sent_ref):
+def project(slot_ref, low_ref, other_ref, ups_ref, dy_ref, sent_ref):
     rows = low_ref.shape[1]
-    chips, keys, _ = dy_ref.shape
+    chips, _, keys, _ = dy_ref.shape
     low_u = (low_ref[0].astype(F32) + other_ref[0].astype(F32)).astype(BF16)
     dy = dy_ref[...].reshape(chips * keys, 2 * rows)
     parts = [
@@ -115,9 +107,9 @@
         sent_ref[y, 0, keys:] = ups_ref[0]
 
 
-def lower(got_ref, dy_ref, low_ref):
+def lower(slot_ref, got_ref, dy_ref, low_ref):
     _, rank, rows = low_ref.shape
-    chips, keys, _ = dy_ref.shape
+    chips, _, keys, _ = dy_ref.shape
     ups = got_ref[:, 0, keys:].reshape(chips * keys, LANES)
     dy = dy_ref[...].reshape(chips * keys, 2 * rows)
     for side in range(2):
@@ -141,33 +133,18 @@
         part_ref[2 * pair + 1] = pack(pltpu.roll(total, LANES // 2, 1))
 
 
-def combine(scale, slot_ref, low_ref, other_ref, part_ref, x_ref, low_g_ref, sent_ref):
-    columns = sent_ref.shape[0]
-    width = x_ref.shape[1]
+def combine(scale, low_ref, other_ref, part_ref, x_ref, low_g_ref, sent_ref):
     low_g = (low_ref[0].astype(F32) + other_ref[0].astype(F32)).astype(BF16)
     low_g_ref[0] = low_g
     part_a = scale * jnp.dot(low_g, x_ref[...], preferred_element_type=F32)
-    part_a = part_a.astype(BF16)
-    rank = part_a.shape[0]
-    slot = slot_ref[pl.program_id(0)]
-    for x in range(columns):
-        place = jnp.where(slot % columns == x, slot // columns, -1).astype(F32)
-        tail = jnp.concatenate([part_ref[0], jnp.full((8, width), place, F32)], axis=0)
-        sent_ref[x, 0, :rank] = part_a
-        sent_ref[x, 0, rank:] = tail.astype(BF16)
-
-
-def backward(low_ref, dy_ref, other_ref, weight_ref, down_ref, input_ref):
-    first = lax.axis_index("c") == 0
-    dy, other = dy_ref[...], other_ref[...]
-    both = jnp.concatenate(
-        [jnp.where(first, dy, other), jnp.where(first, other, dy)], axis=1
-    )
+    panel = jnp.concatenate([part_a, part_ref[0]], axis=0).astype(BF16)
+    for x in range(sent_ref.shape[0]):
+        sent_ref[x, 0] = panel
+
+
+def backward(low_ref, dy_ref, weight_ref, down_ref, input_ref):
     frozen = lax.dot_general(
-        both.reshape(-1, dy.shape[2]),
-        weight_ref[...],
-        (((0,), (1,)), ((), ())),
-        preferred_element_type=F32,
+        dy_ref[...], weight_ref[...], (((0,), (1,)), ((), ())), preferred_element_type=F32
     )
     update = lax.dot_general(
         low_ref[0], down_ref[0], (((0,), (0,)), ((), ())), preferred_element_type=F32
@@ -175,19 +152,18 @@
     input_ref[...] = (frozen + ADAPTER_SCALE * update).astype(BF16)
 
 
-def sort(got_ref, sent_ref):
+def sort(place_ref, got_ref, sent_ref, total):
     columns, seqs = got_ref.shape[:2]
-    tall = sent_ref.shape[1]
-    rank = tall - 8
-    for z in range(sent_ref.shape[0]):
-        head = tail = 0.0
-        for x in range(columns):
-            for s in range(seqs):
-                low = got_ref[x, s, rank:].astype(F32)
-                here = low[8:9] == z
-                head = head + jnp.where(here, got_ref[x, s, :rank].astype(F32), 0.0)
-                tail = tail + jnp.where(here, low[:8], 0.0)
-        sent_ref[z] = jnp.concatenate([head, tail], axis=0).astype(BF16)
+    total[...] = jnp.zeros_like(total)
+    for x in range(columns):
+        for s in range(seqs):
+            place = place_ref[x * seqs + s]
+
+            @pl.when(place >= 0)
+            def _():
+                total[place] += got_ref[x, s].astype(F32)
+
+    sent_ref[...] = total[...].astype(BF16)
 
 
 def finish(got_ref, down_ref, up_ref):
@@ -220,23 +196,8 @@
     scale = ADAPTER_SCALE / math.sqrt(seqs * rows)
     struct = jax.ShapeDtypeStruct
 
-    own = cotangent.T
-    slices = [own] + [
-        lax.ppermute(own, "y", [(y, (y + d) % chips) for y in range(chips)])
-        for d in range(1, chips)
-    ]
-    near = [slices[d] for d in sorted({1, 2, chips - 2, chips - 1} & set(range(1, chips)))]
-    anywhere = pl.BlockSpec(memory_space=pl.ANY)
-    dy = pl.pallas_call(
-        functools.partial(stack, chips),
-        out_shape=struct((chips,) + own.shape, BF16),
-        in_specs=[anywhere] * chips,
-        out_specs=anywhere,
-        scratch_shapes=[pltpu.SemaphoreType.DMA((chips,))],
-        compiler_params=PART,
-        name="stack",
-    )(*slices)
-    other_dy = lax.ppermute(dy, "c", SWAP)
+    dy = lax.all_gather(cotangent.T, ("y", "c"), axis=0, tiled=True)
+    dy_halves = dy.reshape(chips, 2, keys, dy.shape[1])
 
     tenants = [sequence_tenant] + [
         lax.ppermute(sequence_tenant, "x", [(x, (x + d) % columns) for x in range(columns)])
@@ -251,18 +212,19 @@
         name="prepare",
     )(adapter_down, adapter_up)
     panels = lax.all_to_all(sent, "z", 0, 0, tiled=True)
-    sent, slot_of = pl.pallas_call(
+    sent, slot_of, place_of = pl.pallas_call(
         functools.partial(select, columns),
         out_shape=(
             struct((columns, seqs, tall, width), BF16),
-            struct((seqs,), jnp.int32),
-        ),
-        in_specs=[VMEM] + [SMEM] * (1 + columns) + [anywhere] * len(near),
-        out_specs=(VMEM, SMEM),
+            struct((seqs + 1,), jnp.int32),
+            struct((columns * seqs,), jnp.int32),
+        ),
+        in_specs=[VMEM] + [SMEM] * (1 + columns),
+        out_specs=(VMEM, SMEM, SMEM),
         scratch_shapes=[pltpu.SMEM((slots,), jnp.int32)],
         compiler_params=PART,
         name="select",
-    )(panels, slot_holder_tenant, *tenants, *near)
+    )(panels, slot_holder_tenant, *tenants)
     panels = lax.all_to_all(sent, "x", 0, 0, tiled=True)
 
     pairs = seqs // 2
@@ -297,33 +259,41 @@
         name="low",
     )(slot_of, panels, panels, activations)
     other_low = lax.ppermute(low_u, "c", SWAP)
-    dy_pair = pl.BlockSpec((chips, keys, 2 * rows), lambda p: (0, 0, p))
-    mixed = pl.BlockSpec((chips, 1, 2 * keys, 2 * rank), lambda p: (0, p, 0, 0))
+    dy_pair = pl.BlockSpec(
+        (chips, 1, keys, 2 * rows), lambda p, slot: (0, slot[seqs], 0, p)
+    )
+    mixed = pl.BlockSpec((chips, 1, 2 * keys, 2 * rank), lambda p, slot: (0, p, 0, 0))
     sent = pl.pallas_call(
         project,
-        grid=(pairs,),
-        in_specs=[
-            pl.BlockSpec((1, rows, 2 * rank), lambda p: (p, 0, 0)),
-            pl.BlockSpec((1, rows, 2 * rank), lambda p: (p, 0, 0)),
-            pl.BlockSpec((1, keys, 2 * rank), lambda p: (p, 0, 0)),
-            dy_pair,
-        ],
-        out_specs=mixed,
+        grid_spec=pltpu.PrefetchScalarGridSpec(
+            num_scalar_prefetch=1,
+            grid=(pairs,),
+            in_specs=[
+                pl.BlockSpec((1, rows, 2 * rank), lambda p, slot: (p, 0, 0)),
+                pl.BlockSpec((1, rows, 2 * rank), lambda p, slot: (p, 0, 0)),
+                pl.BlockSpec((1, keys, 2 * rank), lambda p, slot: (p, 0, 0)),
+                dy_pair,
+            ],
+            out_specs=mixed,
+        ),
         out_shape=struct((chips, pairs, 2 * keys, 2 * rank), BF16),
-        compiler_params=STEPS,
+        compiler_params=ALL,
         name="project",
-    )(low_u, other_low, ups, dy)
+    )(slot_of, low_u, other_low, ups, dy_halves)
     got = lax.all_to_all(sent, "y", 0, 0, tiled=True)
 
     low_g = pl.pallas_call(
         lower,
-        grid=(pairs,),
-        in_specs=[mixed, dy_pair],
-        out_specs=pl.BlockSpec((2, rank, rows), lambda p: (p, 0, 0)),
+        grid_spec=pltpu.PrefetchScalarGridSpec(
+            num_scalar_prefetch=1,
+            grid=(pairs,),
+            in_specs=[mixed, dy_pair],
+            out_specs=pl.BlockSpec((2, rank, rows), lambda p, slot: (p, 0, 0)),
+        ),
         out_shape=struct((seqs, rank, rows), BF16),
         compiler_params=STEPS,
         name="lower",
-    )(got, dy)
+    )(slot_of, got, dy_halves)
     other_low = lax.ppermute(low_g, "c", SWAP)
     part_b = pl.pallas_call(
         functools.partial(tally, scale),
@@ -333,36 +303,30 @@
         compiler_params=PART,
         name="tally",
     )(got)
+    one = pl.BlockSpec((1, rank, rows), lambda s: (s, 0, 0))
     low_g, sent = pl.pallas_call(
         functools.partial(combine, scale),
-        grid_spec=pltpu.PrefetchScalarGridSpec(
-            num_scalar_prefetch=1,
-            grid=(seqs,),
-            in_specs=[
-                pl.BlockSpec((1, rank, rows), lambda s, slot: (s, 0, 0)),
-                pl.BlockSpec((1, rank, rows), lambda s, slot: (s, 0, 0)),
-                pl.BlockSpec((1, tall - rank, width), lambda s, slot: (s, 0, 0)),
-                pl.BlockSpec((rows, width), lambda s, slot: (s, 0)),
-            ],
-            out_specs=(
-                pl.BlockSpec((1, rank, rows), lambda s, slot: (s, 0, 0)),
-                pl.BlockSpec((columns, 1, tall + 8, width), lambda s, slot: (0, s, 0, 0)),
-            ),
-        ),
+        grid=(seqs,),
+        in_specs=[
+            one,
+            one,
+            pl.BlockSpec((1, tall - rank, width), lambda s: (s, 0, 0)),
+            pl.BlockSpec((rows, width), lambda s: (s, 0)),
+        ],
+        out_specs=(one, pl.BlockSpec((columns, 1, tall, width), lambda s: (0, s, 0, 0))),
         out_shape=(
             struct((seqs, rank, rows), BF16),
-            struct((columns, seqs, tall + 8, width), BF16),
-        ),
-        compiler_params=ALL,
+            struct((columns, seqs, tall, width), BF16),
+        ),
+        compiler_params=STEPS,
         name="combine",
-    )(slot_of, low_g, other_low, part_b, activations)
+    )(low_g, other_low, part_b, activations)
     input_gradient = pl.pallas_call(
         backward,
         grid=(seqs,),
         in_specs=[
-            pl.BlockSpec((1, rank, rows), lambda s: (s, 0, 0)),
-            pl.BlockSpec((chips, keys, rows), lambda s: (0, 0, s)),
-            pl.BlockSpec((chips, keys, rows), lambda s: (0, 0, s)),
+            one,
+            pl.BlockSpec((dy.shape[0], rows), lambda s: (0, s)),
             pl.BlockSpec(key_weight.shape, lambda s: (0, 0)),
             pl.BlockSpec((1, rank, width), lambda s: (s, 0, 0)),
         ],
@@ -375,17 +339,18 @@
             transcendentals=0,
         ),
         name="backward",
-    )(low_g, dy, other_dy, key_weight, down)
+    )(low_g, dy, key_weight, down)
     got = lax.all_to_all(sent, "x", 0, 0, tiled=True)
 
     sent = pl.pallas_call(
         sort,
         out_shape=struct((slots // columns, tall, width), BF16),
-        in_specs=[VMEM],
+        in_specs=[SMEM, VMEM],
         out_specs=VMEM,
+        scratch_shapes=[pltpu.VMEM((slots // columns, tall, width), F32)],
         compiler_params=PART,
         name="sort",
-    )(got)
+    )(place_of, got)
     got = lax.all_to_all(sent, "z", 0, 0, tiled=True)
 
     grad_a, grad_b = pl.pallas_call(

time: 168 us -> 156 us (0.929)
  starting transfers between devices: 77.2 us -> 32.5 us
  blocking collectives: 18.5 us -> 61.6 us
  waiting for transfers between devices: 41.5 us -> 24.9 us
  between operations: 0.95 us -> 14.2 us
  Pallas kernels: 25.9 us -> 21.1 us
  local copies, waits for them, and re-layouts: 2.86 us -> 0.69 us
    all_to_all x0 -> x2, blocking collectives: none -> 38.1 us  [the longest x1 19.4 us: local(): panels = lax.all_to_all(sent, 'x', 0, 0, tiled=True)]
    ppermute x8 -> x0, starting transfers between devices: 28.5 us -> none  [the longest x7 26 us: local(): lax.ppermute(own, 'y', [(y, (y + d) % chips) for y in range(chips)])]
    all_to_all x2 -> x0, waiting for transfers between devices: 14.8 us -> none  [the longest x1 14.8 us: local(): got = lax.all_to_all(sent, 'x', 0, 0, tiled=True)]
    ppermute x8 -> x0, waiting for transfers between devices: 9.87 us -> none  [the longest x7 9.87 us: local(): lax.ppermute(own, 'y', [(y, (y + d) % chips) for y in range(chips)])]
    all_to_all x2 -> x0, starting transfers between devices: 7.84 us -> none  [the longest x1 4.09 us: local(): got = lax.all_to_all(sent, 'x', 0, 0, tiled=True)]
    all_to_all x1, waiting for transfers between devices: 0.01 us -> 7.18 us  [local(): panels = lax.all_to_all(sent, 'z', 0, 0, tiled=True)]
    all_to_all x1, blocking collectives: 18.5 us -> 23.5 us  [local(): got = lax.all_to_all(sent, 'y', 0, 0, tiled=True)]
    ppermute x1, starting transfers between devices: 8.09 us -> 3.84 us  [local(): other_low = lax.ppermute(low_u, 'c', SWAP)]
  transfers between devices with their start and end apart: 17 -> 8, of which waited for: 7 -> 5; matrix products, arithmetic and copies ran while one was open for 0% -> 0% of each run, Pallas kernels for 9% -> 8%
where the time goes in v5:
time: 156 us; the launch traced here: 155 us
  blocking collectives  61.6 us (39%)
  starting transfers between devices  32.5 us (21%)
  waiting for transfers between devices  24.9 us (16%)
  Pallas kernels  21.1 us (14%)
  between operations  14.2 us (9%)
    all_to_all x1, blocking collectives, local(): got = lax.all_to_all(sent, 'y', 0, 0, tiled=True)  23.5 us
    all_to_all x1, blocking collectives, local(): panels = lax.all_to_all(sent, 'x', 0, 0, tiled=True)  19.4 us
    all_to_all x1, blocking collectives, local(): got = lax.all_to_all(sent, 'x', 0, 0, tiled=True)  18.7 us
    all_to_all x1, waiting for transfers between devices, local(): got = lax.all_to_all(sent, 'z', 0, 0, tiled=True)  13.3 us
    all_to_all x1, starting transfers between devices, local(): panels = lax.all_to_all(sent, 'z', 0, 0, tiled=True)  10.9 us
    ppermute x3, starting transfers between devices, local(): lax.ppermute(sequence_tenant, 'x', [(x, (x + d) % columns) for x in range...  10.5 us
    all_to_all x1, waiting for transfers between devices, local(): panels = lax.all_to_all(sent, 'z', 0, 0, tiled=True)  7.18 us
    pallas_call x1, Pallas kernels, local(): pl.pallas_call(backward, grid=(seqs,), in_specs=[one, pl.BlockSpec((dy.sh...  6.01 us
  transfers between devices with their start and end apart: 8, of which 5 were waited for; matrix products, arithmetic and copies ran while one was open for 0% of the time, Pallas kernels for 8%

profile of v5, /device:TPU:1, one launch (start us, length us, event | category | flops | bytes accessed | tf_op | source)
XLA Modules:
  0.0 155.0 jit_solution(9913745078575710292)
XLA Ops:
  7.9 1.8 %prepare.1 = bf16[8,72,512]{2,1,0:T(8,128)(2,1)} custom-call(bf16[1,64,512]{2,1,0:T(8,128)(2,1)} %down_ref.1, bf16[1,64,64]{2,1,0:T(8,128)(2,1)} %up_ref.1), custom_call_target="tpu_custom_call" | custom-call | tf_op jit(solution)/shard_map/prepare/pallas_call | solution.py:206
  9.7 10.9 %all-to-all-start = ((bf16[8,72,512]{2,1,0:T(8,128)(2,1)}), bf16[8,72,512]{2,1,0:T(8,128)(2,1)S(1)}, u32[]{:S(2)}, u32[]{:S(2)}) async-start(bf16[8,72,512]{2,1,0:T(8,128)(2,1)} %prepare.1), calls=%async_computation | async-start | bytes 1179648 | tf_op jit(solution)/shard_map/all_to_all | solution.py:214
  20.6 3.1 %collective-permute-start = (s32[4]{0:T(128)S(1)}, s32[4]{0:T(128)S(1)}, u32[]{:S(2)}, u32[]{:S(2)}) collective-permute-start(s32[4]{0:T(128)S(1)} %copy-done.5), channel_id=1, source_target_pairs={{0,16},{16,32},{32,48},{48,0},{1,17},{17,33},{33,49},{49,1},{2,18}... | collective-permute-start | bytes 56 | tf_op jit(solution)/shard_map/ppermute | solution.py:203
  23.7 4.4 %collective-permute-start.1 = (s32[4]{0:T(128)S(1)}, s32[4]{0:T(128)S(1)}, u32[]{:S(2)}, u32[]{:S(2)}) collective-permute-start(s32[4]{0:T(128)S(1)} %copy-done.5), channel_id=1, source_target_pairs={{0,32},{16,48},{32,0},{48,16},{1,33},{17,49},{33,1},{49,17},{2,34}... | collective-permute-start | bytes 56 | tf_op jit(solution)/shard_map/ppermute | solution.py:203
  28.1 3.1 %collective-permute-start.2 = (s32[4]{0:T(128)S(1)}, s32[4]{0:T(128)S(1)}, u32[]{:S(2)}, u32[]{:S(2)}) collective-permute-start(s32[4]{0:T(128)S(1)} %copy-done.5), channel_id=1, source_target_pairs={{0,48},{16,0},{32,16},{48,32},{1,49},{17,1},{33,17},{49,33},{2,50}... | collective-permute-start | bytes 56 | tf_op jit(solution)/shard_map/ppermute | solution.py:203
  31.2 1.6 %collective-permute-done.2.refs_3_ = s32[4]{0:T(128)S(1)} collective-permute-done((s32[4]{0:T(128)S(1)}, s32[4]{0:T(128)S(1)}, u32[]{:S(2)}, u32[]{:S(2)}) %collective-permute-start.2) | collective-permute-done | bytes 48 | tf_op jit(solution)/shard_map/ppermute | solution.py:203
  32.8 7.2 %all-to-all-done.panel_ref = bf16[8,72,512]{2,1,0:T(8,128)(2,1)S(1)} async-done(((bf16[8,72,512]{2,1,0:T(8,128)(2,1)}), bf16[8,72,512]{2,1,0:T(8,128)(2,1)S(1)}, u32[]{:S(2)}, u32[]{:S(2)}) %all-to-all-start) | async-done | bytes 589856 | tf_op jit(solution)/shard_map/all_to_all | solution.py:214
  40.0 1.3 select.1
  41.3 19.4 %all_to_all.25.panel0_ref.panel1_ref = bf16[4,4,72,512]{3,2,1,0:T(8,128)(2,1)} all-to-all(bf16[4,4,72,512]{3,2,1,0:T(8,128)(2,1)S(1)} %get-tuple-element.14), channel_id=1, replica_groups=mesh['z'=8,'x'=4,'y'=8,'c'=2] {'x'}, dimensions={0} | all-to-all | bytes 2359296 | tf_op jit(solution)/shard_map/all_to_all | solution.py:228
  60.8 3.3 %low.1 = (bf16[2,384,128]{2,1,0:T(8,128)(2,1)}, bf16[4,64,512]{2,1,0:T(8,128)(2,1)}, bf16[2,64,128]{2,1,0:T(8,128)(2,1)}) custom-call(s32[5]{0:T(128)} %copy-done.2, bf16[4,4,72,512]{3,2,1,0:T(8,128)(2,1)} %all_to_all.25.panel0_ref.panel1_ref, bf16[4,4,72,512]{3,2,1,0:T(8,128)(2,1)} %all_to_all.25.panel0_ref.panel1_ref, bf16[1536,512]{1,0:T(8,128)(2,1)} %x_ref.3), custom_call_target="tpu_custom_call" | custom-call | tf_op jit(solution)/shard_map/low/pallas_call | solution.py:231
  64.1 3.8 %collective-permute-start.3 = (bf16[2,384,128]{2,1,0:T(8,128)(2,1)}, bf16[2,384,128]{2,1,0:T(8,128)(2,1)S(1)}, u32[]{:S(2)}, u32[]{:S(2)}) collective-permute-start(bf16[2,384,128]{2,1,0:T(8,128)(2,1)} %get-tuple-element.15.low_ref), channel_id=1, source_target_pairs={{0,1},{1,0},{2,3},{3,2},{4,5},{5,4},{6,7},{7,6},{8,9},{9,8},{10,11... | collective-permute-start | bytes 589832 | tf_op jit(solution)/shard_map/ppermute | solution.py:261
  67.9 1.3 collective-permute-done.3.other_ref
  69.8 3.7 %project.1 = bf16[8,2,128,128]{3,2,1,0:T(8,128)(2,1)} custom-call(s32[5]{0:T(128)} %copy-done.2, bf16[2,384,128]{2,1,0:T(8,128)(2,1)} %get-tuple-element.15.low_ref, bf16[2,384,128]{2,1,0:T(8,128)(2,1)} %copy-done.7, bf16[2,64,128]{2,1,0:T(8,128)(2,1)} %get-tuple-element.16.ups_ref, bf16[8,2,64,1536]{3,2,1,0:T(8,128)(2,1)} %bitcast.2), custom_call_target="tpu_custom_call" | custom-call | tf_op jit(solution)/shard_map/project/pallas_call | solution.py:266
  73.5 23.5 %all_to_all.26.got_ref = bf16[8,2,128,128]{3,2,1,0:T(8,128)(2,1)S(1)} all-to-all(bf16[8,2,128,128]{3,2,1,0:T(8,128)(2,1)} %project.1), channel_id=1, replica_groups=mesh['z'=8,'x'=4,'y'=8,'c'=2] {'y'}, dimensions={0} | all-to-all | bytes 1048576 | tf_op jit(solution)/shard_map/all_to_all | solution.py:283
  97.1 1.4 lower.1.low_ref
  98.5 3.6 %collective-permute-start.4 = (bf16[4,64,384]{2,1,0:T(8,128)(2,1)S(1)}, bf16[4,64,384]{2,1,0:T(8,128)(2,1)S(1)}, u32[]{:S(2)}, u32[]{:S(2)}) collective-permute-start(bf16[4,64,384]{2,1,0:T(8,128)(2,1)S(1)} %lower.1.low_ref), channel_id=1, source_target_pairs={{0,1},{1,0},{2,3},{3,2},{4,5},{5,4},{6,7},{7,6},{8,9},{9,8},{10,11... | collective-permute-start | bytes 589832 | tf_op jit(solution)/shard_map/ppermute | solution.py:297
  102.3 0.9 collective-permute-done.4.other_ref
  103.2 0.9 combine.1
  104.1 18.7 %all_to_all.27.got_ref = bf16[4,4,72,512]{3,2,1,0:T(8,128)(2,1)S(1)} all-to-all(bf16[4,4,72,512]{3,2,1,0:T(8,128)(2,1)S(1)} %get-tuple-element.20), channel_id=1, replica_groups=mesh['z'=8,'x'=4,'y'=8,'c'=2] {'x'}, dimensions={0} | all-to-all | bytes 2359296 | tf_op jit(solution)/shard_map/all_to_all | solution.py:343
  122.8 1.7 %sort.1 = bf16[8,72,512]{2,1,0:T(8,128)(2,1)} custom-call(s32[16]{0:T(128)S(1)} %get-tuple-element.19.place_ref, bf16[4,4,72,512]{3,2,1,0:T(8,128)(2,1)S(1)} %all_to_all.27.got_ref), custom_call_target="tpu_custom_call" | custom-call | tf_op jit(solution)/shard_map/sort/pallas_call | solution.py:345
  124.5 3.5 %all-to-all-start.4 = ((bf16[8,72,512]{2,1,0:T(8,128)(2,1)}), bf16[8,72,512]{2,1,0:T(8,128)(2,1)S(1)}, u32[]{:S(2)}, u32[]{:S(2)}) async-start(bf16[8,72,512]{2,1,0:T(8,128)(2,1)} %sort.1), calls=%async_computation.4 | async-start | bytes 1179648 | tf_op jit(solution)/shard_map/all_to_all | solution.py:354
  128.0 6.0 %backward.1 = bf16[1536,512]{1,0:T(8,128)(2,1)} custom-call(bf16[4,64,384]{2,1,0:T(8,128)(2,1)} %copy-done.6, bf16[1024,1536]{1,0:T(8,128)(2,1)} %all-gather.2.cloned.1.call-done.dy_ref, bf16[512,1024]{1,0:T(8,128)(2,1)} %weight_ref.1, bf16[4,64,512]{2,1,0:T(8,128)(2,1)} %get-tuple-element.18.down_ref), custom_call_target="tpu_custom_call" | custom-call | flops 1711276032 | bytes 6291456 | tf_op jit(solution)/shard_map/backward/pallas_call | solution.py:324
  134.0 13.3 %all-to-all-done.4.got_ref = bf16[8,72,512]{2,1,0:T(8,128)(2,1)S(1)} async-done(((bf16[8,72,512]{2,1,0:T(8,128)(2,1)}), bf16[8,72,512]{2,1,0:T(8,128)(2,1)S(1)}, u32[]{:S(2)}, u32[]{:S(2)}) %all-to-all-start.4) | async-done | bytes 589856 | tf_op jit(solution)/shard_map/all_to_all | solution.py:354
  147.3 0.8 finish.1
  (22 shorter events, 1.6 us)
Async XLA Ops:
  7.2 13.4 %copy-start.5 = (s32[4]{0:T(128)S(1)}, s32[4]{0:T(128)}, u32[]{:S(2)}) copy-start(s32[4]{0:T(128)} %refs_0_.1) | copy-start | bytes 52
  7.2 32.8 %copy-start.4 = (s32[32]{0:T(128)S(1)}, s32[32]{0:T(128)}, u32[]{:S(2)}) copy-start(s32[32]{0:T(128)} %holder_ref.1) | copy-start | bytes 388
  7.2 62.0 %all-gather.2.cloned.1.call-start = ((), (), s32[]{:S(2)}) async-start(), calls=%async_computation.5 | async-start | bytes 3342336 | tf_op jit(solution)/shard_map/all_gather | solution.py:199
  9.7 30.2 %all-to-all-start = ((bf16[8,72,512]{2,1,0:T(8,128)(2,1)}), bf16[8,72,512]{2,1,0:T(8,128)(2,1)S(1)}, u32[]{:S(2)}, u32[]{:S(2)}) async-start(bf16[8,72,512]{2,1,0:T(8,128)(2,1)} %prepare.1), calls=%async_computation | async-start | bytes 1179648 | tf_op jit(solution)/shard_map/all_to_all | solution.py:214
  20.6 10.6 %collective-permute-start = (s32[4]{0:T(128)S(1)}, s32[4]{0:T(128)S(1)}, u32[]{:S(2)}, u32[]{:S(2)}) collective-permute-start(s32[4]{0:T(128)S(1)} %copy-done.5), channel_id=1, source_target_pairs={{0,16},{16,32},{32,48},{48,0},{1,17},{17,33},{33,49},{49,1},{2,18}... | collective-permute-start | bytes 56 | tf_op jit(solution)/shard_map/ppermute | solution.py:203
  23.7 7.4 %collective-permute-start.1 = (s32[4]{0:T(128)S(1)}, s32[4]{0:T(128)S(1)}, u32[]{:S(2)}, u32[]{:S(2)}) collective-permute-start(s32[4]{0:T(128)S(1)} %copy-done.5), channel_id=1, source_target_pairs={{0,32},{16,48},{32,0},{48,16},{1,33},{17,49},{33,1},{49,17},{2,34}... | collective-permute-start | bytes 56 | tf_op jit(solution)/shard_map/ppermute | solution.py:203
  28.1 4.7 %collective-permute-start.2 = (s32[4]{0:T(128)S(1)}, s32[4]{0:T(128)S(1)}, u32[]{:S(2)}, u32[]{:S(2)}) collective-permute-start(s32[4]{0:T(128)S(1)} %copy-done.5), channel_id=1, source_target_pairs={{0,48},{16,0},{32,16},{48,32},{1,49},{17,1},{33,17},{49,33},{2,50}... | collective-permute-start | bytes 56 | tf_op jit(solution)/shard_map/ppermute | solution.py:203
  41.3 19.4 %copy-start.2 = (s32[5]{0:T(128)}, s32[5]{0:T(128)S(1)}, u32[]{:S(2)}) copy-start(s32[5]{0:T(128)S(1)} %get-tuple-element.13.slot_ref) | copy-start | bytes 64
  64.1 5.1 %collective-permute-start.3 = (bf16[2,384,128]{2,1,0:T(8,128)(2,1)}, bf16[2,384,128]{2,1,0:T(8,128)(2,1)S(1)}, u32[]{:S(2)}, u32[]{:S(2)}) collective-permute-start(bf16[2,384,128]{2,1,0:T(8,128)(2,1)} %get-tuple-element.15.low_ref), channel_id=1, source_target_pairs={{0,1},{1,0},{2,3},{3,2},{4,5},{5,4},{6,7},{7,6},{8,9},{9,8},{10,11... | collective-permute-start | bytes 589832 | tf_op jit(solution)/shard_map/ppermute | solution.py:261
  69.2 0.7 copy-start.7
  69.8 27.2 %copy-start = (bf16[1024,1536]{1,0:T(8,128)(2,1)S(1)}, bf16[1024,1536]{1,0:T(8,128)(2,1)}, u32[]{:S(2)}) copy-start(bf16[1024,1536]{1,0:T(8,128)(2,1)} %all-gather.2.cloned.1.call-done.dy_ref) | copy-start | bytes 9437188
  69.8 27.2 %copy-start.3 = (s32[5]{0:T(128)S(1)}, s32[5]{0:T(128)}, u32[]{:S(2)}) copy-start(s32[5]{0:T(128)} %copy-done.2) | copy-start | bytes 64
  97.1 6.1 %copy-start.1 = (bf16[1536,512]{1,0:T(8,128)(2,1)S(1)}, bf16[1536,512]{1,0:T(8,128)(2,1)}, u32[]{:S(2)}) copy-start(bf16[1536,512]{1,0:T(8,128)(2,1)} %x_ref.3) | copy-start | bytes 4718596
  98.5 4.7 %collective-permute-start.4 = (bf16[4,64,384]{2,1,0:T(8,128)(2,1)S(1)}, bf16[4,64,384]{2,1,0:T(8,128)(2,1)S(1)}, u32[]{:S(2)}, u32[]{:S(2)}) collective-permute-start(bf16[4,64,384]{2,1,0:T(8,128)(2,1)S(1)} %lower.1.low_ref), channel_id=1, source_target_pairs={{0,1},{1,0},{2,3},{3,2},{4,5},{5,4},{6,7},{7,6},{8,9},{9,8},{10,11... | collective-permute-start | bytes 589832 | tf_op jit(solution)/shard_map/ppermute | solution.py:297
  104.1 18.7 %copy-start.6 = (bf16[4,64,384]{2,1,0:T(8,128)(2,1)}, bf16[4,64,384]{2,1,0:T(8,128)(2,1)S(1)}, u32[]{:S(2)}) copy-start(bf16[4,64,384]{2,1,0:T(8,128)(2,1)S(1)} %get-tuple-element.17.low_ref) | copy-start | bytes 589828
  124.5 22.8 %all-to-all-start.4 = ((bf16[8,72,512]{2,1,0:T(8,128)(2,1)}), bf16[8,72,512]{2,1,0:T(8,128)(2,1)S(1)}, u32[]{:S(2)}, u32[]{:S(2)}) async-start(bf16[8,72,512]{2,1,0:T(8,128)(2,1)} %sort.1), calls=%async_computation.4 | async-start | bytes 1179648 | tf_op jit(solution)/shard_map/all_to_all | solution.py:354
Sparse Core Ops, SparseCore 0:
  10.1 49.3 all-gather.1

commit v6 on v5

--- a/solution.py
+++ b/solution.py
@@ -71,14 +71,12 @@
             sent_ref[there, s] = panel_ref[row]
 
 
-def low(slot_ref, panel0_ref, panel1_ref, x_ref, low_ref, down_ref, ups_ref):
-    rank = down_ref.shape[1]
-    rows = low_ref.shape[1]
+def low(slot_ref, panel0_ref, panel1_ref, x_ref, _, low_ref, ups_ref):
+    rows, rank = low_ref.shape[1], low_ref.shape[2] // 2
     total = ups = 0.0
     for side, panel_ref in enumerate((panel0_ref, panel1_ref)):
         panel = panel_ref[0, 0]
         down = panel[:rank]
-        down_ref[side] = down
         blank = jnp.zeros_like(down)
         wide = jnp.concatenate([blank, down] if side else [down, blank], axis=0)
         total = total + lax.dot_general(
@@ -142,12 +140,15 @@
         sent_ref[x, 0] = panel
 
 
-def backward(low_ref, dy_ref, weight_ref, down_ref, input_ref):
+def backward(slot_ref, low_ref, dy_ref, weight_ref, panel_ref, input_ref):
     frozen = lax.dot_general(
         dy_ref[...], weight_ref[...], (((0,), (1,)), ((), ())), preferred_element_type=F32
     )
     update = lax.dot_general(
-        low_ref[0], down_ref[0], (((0,), (0,)), ((), ())), preferred_element_type=F32
+        low_ref[0],
+        panel_ref[0, 0][: low_ref.shape[1]],
+        (((0,), (0,)), ((), ())),
+        preferred_element_type=F32,
     )
     input_ref[...] = (frozen + ADAPTER_SCALE * update).astype(BF16)
 
@@ -228,7 +229,7 @@
     panels = lax.all_to_all(sent, "x", 0, 0, tiled=True)
 
     pairs = seqs // 2
-    low_u, down, ups = pl.pallas_call(
+    low_u, ups = pl.pallas_call(
         low,
         grid_spec=pltpu.PrefetchScalarGridSpec(
             num_scalar_prefetch=1,
@@ -243,21 +244,20 @@
                     lambda p, slot: (slot[2 * p + 1] % columns, 2 * p + 1, 0, 0),
                 ),
                 pl.BlockSpec((2 * rows, width), lambda p, slot: (p, 0)),
+                pl.BlockSpec(memory_space=pl.ANY),
             ],
             out_specs=(
                 pl.BlockSpec((1, rows, 2 * rank), lambda p, slot: (p, 0, 0)),
-                pl.BlockSpec((2, rank, width), lambda p, slot: (p, 0, 0)),
                 pl.BlockSpec((1, keys, 2 * rank), lambda p, slot: (p, 0, 0)),
             ),
         ),
         out_shape=(
             struct((pairs, rows, 2 * rank), BF16),
-            struct((seqs, rank, width), BF16),
             struct((pairs, keys, 2 * rank), BF16),
         ),
         compiler_params=ALL,
         name="low",
-    )(slot_of, panels, panels, activations)
+    )(slot_of, panels, panels, activations, dy)
     other_low = lax.ppermute(low_u, "c", SWAP)
     dy_pair = pl.BlockSpec(
         (chips, 1, keys, 2 * rows), lambda p, slot: (0, slot[seqs], 0, p)
@@ -277,7 +277,7 @@
             out_specs=mixed,
         ),
         out_shape=struct((chips, pairs, 2 * keys, 2 * rank), BF16),
-        compiler_params=ALL,
+        compiler_params=STEPS,
         name="project",
     )(slot_of, low_u, other_low, ups, dy_halves)
     got = lax.all_to_all(sent, "y", 0, 0, tiled=True)
@@ -323,14 +323,17 @@
     )(low_g, other_low, part_b, activations)
     input_gradient = pl.pallas_call(
         backward,
-        grid=(seqs,),
-        in_specs=[
-            one,
-            pl.BlockSpec((dy.shape[0], rows), lambda s: (0, s)),
-            pl.BlockSpec(key_weight.shape, lambda s: (0, 0)),
-            pl.BlockSpec((1, rank, width), lambda s: (s, 0, 0)),
-        ],
-        out_specs=pl.BlockSpec((rows, width), lambda s: (s, 0)),
+        grid_spec=pltpu.PrefetchScalarGridSpec(
+            num_scalar_prefetch=1,
+            grid=(seqs,),
+            in_specs=[
+                pl.BlockSpec((1, rank, rows), lambda s, slot: (s, 0, 0)),
+                pl.BlockSpec((dy.shape[0], rows), lambda s, slot: (0, s)),
+                pl.BlockSpec(key_weight.shape, lambda s, slot: (0, 0)),
+                pl.BlockSpec((1, 1, tall, width), lambda s, slot: (slot[s] % columns, s, 0, 0)),
+            ],
+            out_specs=pl.BlockSpec((rows, width), lambda s, slot: (s, 0)),
+        ),
         out_shape=struct(activations.shape, BF16),
         compiler_params=ALL,
         cost_estimate=pl.CostEstimate(
@@ -339,7 +342,7 @@
             transcendentals=0,
         ),
         name="backward",
-    )(low_g, dy, key_weight, down)
+    )(slot_of, low_g, dy, key_weight, panels)
     got = lax.all_to_all(sent, "x", 0, 0, tiled=True)
 
     sent = pl.pallas_call(

time: 156 us -> 155 us (level)
    pallas_call x1, Pallas kernels: 3.7 us -> 1.48 us  [local(): pl.pallas_call(project, grid_spec=pltpu.PrefetchScalarGridSpec(num_scalar...]
  transfers between devices with their start and end apart: 8 -> 8, of which waited for: 5 -> 5; matrix products, arithmetic and copies ran while one was open for 0% -> 0% of each run, Pallas kernels for 8% -> 6%
where the time goes in v6:
time: 155 us; the launch traced here: 154 us
  blocking collectives  61.5 us (40%)
  starting transfers between devices  32.4 us (21%)
  waiting for transfers between devices  24.2 us (16%)
  Pallas kernels  19.9 us (13%)
  between operations  14.2 us (9%)
  local copies, waits for them, and re-layouts  2.21 us (1%)
    all_to_all x1, blocking collectives, local(): got = lax.all_to_all(sent, 'y', 0, 0, tiled=True)  23.4 us
    all_to_all x1, blocking collectives, local(): panels = lax.all_to_all(sent, 'x', 0, 0, tiled=True)  19.4 us
    all_to_all x1, blocking collectives, local(): got = lax.all_to_all(sent, 'x', 0, 0, tiled=True)  18.7 us
    all_to_all x1, waiting for transfers between devices, local(): got = lax.all_to_all(sent, 'z', 0, 0, tiled=True)  12.6 us
    all_to_all x1, starting transfers between devices, local(): panels = lax.all_to_all(sent, 'z', 0, 0, tiled=True)  10.9 us
    ppermute x3, starting transfers between devices, local(): lax.ppermute(sequence_tenant, 'x', [(x, (x + d) % columns) for x in range...  10.5 us
    all_to_all x1, waiting for transfers between devices, local(): panels = lax.all_to_all(sent, 'z', 0, 0, tiled=True)  7.18 us
    pallas_call x1, Pallas kernels, local(): pl.pallas_call(backward, grid_spec=pltpu.PrefetchScalarGridSpec(num_scala...  6.72 us
  transfers between devices with their start and end apart: 8, of which 5 were waited for; matrix products, arithmetic and copies ran while one was open for 0% of the time, Pallas kernels for 6%

profile of v6, /device:TPU:1, one launch (start us, length us, event | category | flops | bytes accessed | tf_op | source)
XLA Modules:
  0.0 154.3 jit_solution(15798605021357152567)
XLA Ops:
  7.9 1.8 %prepare.1 = bf16[8,72,512]{2,1,0:T(8,128)(2,1)} custom-call(bf16[1,64,512]{2,1,0:T(8,128)(2,1)} %down_ref.1, bf16[1,64,64]{2,1,0:T(8,128)(2,1)} %up_ref.1), custom_call_target="tpu_custom_call" | custom-call | tf_op jit(solution)/shard_map/prepare/pallas_call | solution.py:207
  9.7 10.9 %all-to-all-start = ((bf16[8,72,512]{2,1,0:T(8,128)(2,1)}), bf16[8,72,512]{2,1,0:T(8,128)(2,1)S(1)}, u32[]{:S(2)}, u32[]{:S(2)}) async-start(bf16[8,72,512]{2,1,0:T(8,128)(2,1)} %prepare.1), calls=%async_computation | async-start | bytes 1179648 | tf_op jit(solution)/shard_map/all_to_all | solution.py:215
  20.6 3.1 %collective-permute-start = (s32[4]{0:T(128)S(1)}, s32[4]{0:T(128)S(1)}, u32[]{:S(2)}, u32[]{:S(2)}) collective-permute-start(s32[4]{0:T(128)S(1)} %copy-done.8), channel_id=1, source_target_pairs={{0,16},{16,32},{32,48},{48,0},{1,17},{17,33},{33,49},{49,1},{2,18}... | collective-permute-start | bytes 56 | tf_op jit(solution)/shard_map/ppermute | solution.py:204
  23.7 4.4 %collective-permute-start.1 = (s32[4]{0:T(128)S(1)}, s32[4]{0:T(128)S(1)}, u32[]{:S(2)}, u32[]{:S(2)}) collective-permute-start(s32[4]{0:T(128)S(1)} %copy-done.8), channel_id=1, source_target_pairs={{0,32},{16,48},{32,0},{48,16},{1,33},{17,49},{33,1},{49,17},{2,34}... | collective-permute-start | bytes 56 | tf_op jit(solution)/shard_map/ppermute | solution.py:204
  28.1 3.1 %collective-permute-start.2 = (s32[4]{0:T(128)S(1)}, s32[4]{0:T(128)S(1)}, u32[]{:S(2)}, u32[]{:S(2)}) collective-permute-start(s32[4]{0:T(128)S(1)} %copy-done.8), channel_id=1, source_target_pairs={{0,48},{16,0},{32,16},{48,32},{1,49},{17,1},{33,17},{49,33},{2,50}... | collective-permute-start | bytes 56 | tf_op jit(solution)/shard_map/ppermute | solution.py:204
  31.2 1.6 %collective-permute-done.2.refs_3_ = s32[4]{0:T(128)S(1)} collective-permute-done((s32[4]{0:T(128)S(1)}, s32[4]{0:T(128)S(1)}, u32[]{:S(2)}, u32[]{:S(2)}) %collective-permute-start.2) | collective-permute-done | bytes 48 | tf_op jit(solution)/shard_map/ppermute | solution.py:204
  32.8 7.2 %all-to-all-done.panel_ref = bf16[8,72,512]{2,1,0:T(8,128)(2,1)S(1)} async-done(((bf16[8,72,512]{2,1,0:T(8,128)(2,1)}), bf16[8,72,512]{2,1,0:T(8,128)(2,1)S(1)}, u32[]{:S(2)}, u32[]{:S(2)}) %all-to-all-start) | async-done | bytes 589856 | tf_op jit(solution)/shard_map/all_to_all | solution.py:215
  40.0 1.3 select.1
  41.8 19.4 %all_to_all.25.panel0_ref.panel1_ref.panel_ref = bf16[4,4,72,512]{3,2,1,0:T(8,128)(2,1)} all-to-all(bf16[4,4,72,512]{3,2,1,0:T(8,128)(2,1)S(1)} %get-tuple-element.13), channel_id=1, replica_groups=mesh['z'=8,'x'=4,'y'=8,'c'=2] {'x'}, dimensions={0} | all-to-all | bytes 2359296 | tf_op jit(solution)/shard_map/all_to_all | solution.py:229
  61.3 3.6 %low.1 = (bf16[2,384,128]{2,1,0:T(8,128)(2,1)}, bf16[2,64,128]{2,1,0:T(8,128)(2,1)}) custom-call(s32[5]{0:T(128)} %copy-done.5, bf16[4,4,72,512]{3,2,1,0:T(8,128)(2,1)} %all_to_all.25.panel0_ref.panel1_ref.panel_ref, bf16[4,4,72,512]{3,2,1,0:T(8,128)(2,1)} %all_to_all.25.panel0_ref.panel1_ref.panel_ref, bf16[1536,512]{1,0:T(8,128)(2,1)} %x_ref.3, ...), custom_call_target="tpu_custom_call" | custom-call | tf_op jit(solution)/shard_map/low/pallas_call | solution.py:232
  64.8 3.8 %collective-permute-start.3 = (bf16[2,384,128]{2,1,0:T(8,128)(2,1)}, bf16[2,384,128]{2,1,0:T(8,128)(2,1)S(1)}, u32[]{:S(2)}, u32[]{:S(2)}) collective-permute-start(bf16[2,384,128]{2,1,0:T(8,128)(2,1)} %get-tuple-element.14.low_ref), channel_id=1, source_target_pairs={{0,1},{1,0},{2,3},{3,2},{4,5},{5,4},{6,7},{7,6},{8,9},{9,8},{10,11... | collective-permute-start | bytes 589832 | tf_op jit(solution)/shard_map/ppermute | solution.py:261
  68.6 1.3 collective-permute-done.3.other_ref
  69.9 0.9 copy-done.3
  71.6 1.5 project.1
  73.1 23.4 %all_to_all.26.got_ref = bf16[8,2,128,128]{3,2,1,0:T(8,128)(2,1)S(1)} all-to-all(bf16[8,2,128,128]{3,2,1,0:T(8,128)(2,1)S(1)} %project.1), channel_id=1, replica_groups=mesh['z'=8,'x'=4,'y'=8,'c'=2] {'y'}, dimensions={0} | all-to-all | bytes 1048576 | tf_op jit(solution)/shard_map/all_to_all | solution.py:283
  96.5 1.4 lower.1.low_ref
  97.9 3.6 %collective-permute-start.4 = (bf16[4,64,384]{2,1,0:T(8,128)(2,1)S(1)}, bf16[4,64,384]{2,1,0:T(8,128)(2,1)S(1)}, u32[]{:S(2)}, u32[]{:S(2)}) collective-permute-start(bf16[4,64,384]{2,1,0:T(8,128)(2,1)S(1)} %lower.1.low_ref), channel_id=1, source_target_pairs={{0,1},{1,0},{2,3},{3,2},{4,5},{5,4},{6,7},{7,6},{8,9},{9,8},{10,11... | collective-permute-start | bytes 589832 | tf_op jit(solution)/shard_map/ppermute | solution.py:297
  101.7 0.9 collective-permute-done.4.other_ref
  102.6 0.9 combine.1
  103.5 18.7 %all_to_all.27.got_ref = bf16[4,4,72,512]{3,2,1,0:T(8,128)(2,1)S(1)} all-to-all(bf16[4,4,72,512]{3,2,1,0:T(8,128)(2,1)S(1)} %get-tuple-element.18), channel_id=1, replica_groups=mesh['z'=8,'x'=4,'y'=8,'c'=2] {'x'}, dimensions={0} | all-to-all | bytes 2359296 | tf_op jit(solution)/shard_map/all_to_all | solution.py:346
  122.2 1.6 %sort.1 = bf16[8,72,512]{2,1,0:T(8,128)(2,1)} custom-call(s32[16]{0:T(128)S(1)} %get-tuple-element.17.place_ref, bf16[4,4,72,512]{3,2,1,0:T(8,128)(2,1)S(1)} %all_to_all.27.got_ref), custom_call_target="tpu_custom_call" | custom-call | tf_op jit(solution)/shard_map/sort/pallas_call | solution.py:348
  123.8 3.5 %all-to-all-start.4 = ((bf16[8,72,512]{2,1,0:T(8,128)(2,1)}), bf16[8,72,512]{2,1,0:T(8,128)(2,1)S(1)}, u32[]{:S(2)}, u32[]{:S(2)}) async-start(bf16[8,72,512]{2,1,0:T(8,128)(2,1)} %sort.1), calls=%async_computation.4 | async-start | bytes 1179648 | tf_op jit(solution)/shard_map/all_to_all | solution.py:357
  127.4 6.7 %backward.1 = bf16[1536,512]{1,0:T(8,128)(2,1)} custom-call(s32[5]{0:T(128)} %copy-done.5, bf16[4,64,384]{2,1,0:T(8,128)(2,1)} %copy-done.2, bf16[1024,1536]{1,0:T(8,128)(2,1)} %all-gather.2.cloned.1.call-done._.dy_ref, bf16[512,1024]{1,0:T(8,128)(2,1)} %weight_ref.1, bf16[4,4,72,512]{3,2,1,0:T(8,128)(2,1)} %all_to_all.25.panel0_ref.panel1_ref.panel_ref), custom_call_target="tpu_custom_call" | custom-call | flops 1711276032 | bytes 6291456 | tf_op jit(solution)/shard_map/backward/pallas_call | solution.py:324
  134.1 12.6 %all-to-all-done.4.got_ref = bf16[8,72,512]{2,1,0:T(8,128)(2,1)S(1)} async-done(((bf16[8,72,512]{2,1,0:T(8,128)(2,1)}), bf16[8,72,512]{2,1,0:T(8,128)(2,1)S(1)}, u32[]{:S(2)}, u32[]{:S(2)}) %all-to-all-start.4) | async-done | bytes 589856 | tf_op jit(solution)/shard_map/all_to_all | solution.py:357
  (24 shorter events, 3.0 us)
Async XLA Ops:
  7.2 13.4 %copy-start.8 = (s32[4]{0:T(128)S(1)}, s32[4]{0:T(128)}, u32[]{:S(2)}) copy-start(s32[4]{0:T(128)} %refs_0_.1) | copy-start | bytes 52
  7.2 32.8 %copy-start.7 = (s32[32]{0:T(128)S(1)}, s32[32]{0:T(128)}, u32[]{:S(2)}) copy-start(s32[32]{0:T(128)} %holder_ref.1) | copy-start | bytes 388
  7.2 54.1 %all-gather.2.cloned.1.call-start = ((), (), s32[]{:S(2)}) async-start(), calls=%async_computation.5 | async-start | bytes 3342336 | tf_op jit(solution)/shard_map/all_gather | solution.py:200
  9.7 30.2 %all-to-all-start = ((bf16[8,72,512]{2,1,0:T(8,128)(2,1)}), bf16[8,72,512]{2,1,0:T(8,128)(2,1)S(1)}, u32[]{:S(2)}, u32[]{:S(2)}) async-start(bf16[8,72,512]{2,1,0:T(8,128)(2,1)} %prepare.1), calls=%async_computation | async-start | bytes 1179648 | tf_op jit(solution)/shard_map/all_to_all | solution.py:215
  20.6 10.6 %collective-permute-start = (s32[4]{0:T(128)S(1)}, s32[4]{0:T(128)S(1)}, u32[]{:S(2)}, u32[]{:S(2)}) collective-permute-start(s32[4]{0:T(128)S(1)} %copy-done.8), channel_id=1, source_target_pairs={{0,16},{16,32},{32,48},{48,0},{1,17},{17,33},{33,49},{49,1},{2,18}... | collective-permute-start | bytes 56 | tf_op jit(solution)/shard_map/ppermute | solution.py:204
  23.7 7.4 %collective-permute-start.1 = (s32[4]{0:T(128)S(1)}, s32[4]{0:T(128)S(1)}, u32[]{:S(2)}, u32[]{:S(2)}) collective-permute-start(s32[4]{0:T(128)S(1)} %copy-done.8), channel_id=1, source_target_pairs={{0,32},{16,48},{32,0},{48,16},{1,33},{17,49},{33,1},{49,17},{2,34}... | collective-permute-start | bytes 56 | tf_op jit(solution)/shard_map/ppermute | solution.py:204
  28.1 4.7 %collective-permute-start.2 = (s32[4]{0:T(128)S(1)}, s32[4]{0:T(128)S(1)}, u32[]{:S(2)}, u32[]{:S(2)}) collective-permute-start(s32[4]{0:T(128)S(1)} %copy-done.8), channel_id=1, source_target_pairs={{0,48},{16,0},{32,16},{48,32},{1,49},{17,1},{33,17},{49,33},{2,50}... | collective-permute-start | bytes 56 | tf_op jit(solution)/shard_map/ppermute | solution.py:204
  41.3 0.5 copy-start.5
  61.2 8.7 %copy-start = (bf16[1024,1536]{1,0:T(8,128)(2,1)S(1)}, bf16[1024,1536]{1,0:T(8,128)(2,1)}, u32[]{:S(2)}) copy-start(bf16[1024,1536]{1,0:T(8,128)(2,1)} %all-gather.2.cloned.1.call-done._.dy_ref) | copy-start | bytes 9437188
  61.3 8.7 %copy-start.6 = (s32[5]{0:T(128)S(1)}, s32[5]{0:T(128)}, u32[]{:S(2)}) copy-start(s32[5]{0:T(128)} %copy-done.5) | copy-start | bytes 64
  64.8 5.1 %collective-permute-start.3 = (bf16[2,384,128]{2,1,0:T(8,128)(2,1)}, bf16[2,384,128]{2,1,0:T(8,128)(2,1)S(1)}, u32[]{:S(2)}, u32[]{:S(2)}) collective-permute-start(bf16[2,384,128]{2,1,0:T(8,128)(2,1)} %get-tuple-element.14.low_ref), channel_id=1, source_target_pairs={{0,1},{1,0},{2,3},{3,2},{4,5},{5,4},{6,7},{7,6},{8,9},{9,8},{10,11... | collective-permute-start | bytes 589832 | tf_op jit(solution)/shard_map/ppermute | solution.py:261
  69.9 0.9 copy-start.3
  70.8 0.8 copy-start.4
  96.5 6.1 %copy-start.1 = (bf16[1536,512]{1,0:T(8,128)(2,1)S(1)}, bf16[1536,512]{1,0:T(8,128)(2,1)}, u32[]{:S(2)}) copy-start(bf16[1536,512]{1,0:T(8,128)(2,1)} %x_ref.3) | copy-start | bytes 4718596
  97.9 4.7 %collective-permute-start.4 = (bf16[4,64,384]{2,1,0:T(8,128)(2,1)S(1)}, bf16[4,64,384]{2,1,0:T(8,128)(2,1)S(1)}, u32[]{:S(2)}, u32[]{:S(2)}) collective-permute-start(bf16[4,64,384]{2,1,0:T(8,128)(2,1)S(1)} %lower.1.low_ref), channel_id=1, source_target_pairs={{0,1},{1,0},{2,3},{3,2},{4,5},{5,4},{6,7},{7,6},{8,9},{9,8},{10,11... | collective-permute-start | bytes 589832 | tf_op jit(solution)/shard_map/ppermute | solution.py:297
  103.5 18.7 %copy-start.2 = (bf16[4,64,384]{2,1,0:T(8,128)(2,1)}, bf16[4,64,384]{2,1,0:T(8,128)(2,1)S(1)}, u32[]{:S(2)}) copy-start(bf16[4,64,384]{2,1,0:T(8,128)(2,1)S(1)} %get-tuple-element.16.low_ref) | copy-start | bytes 589828
  123.8 22.8 %all-to-all-start.4 = ((bf16[8,72,512]{2,1,0:T(8,128)(2,1)}), bf16[8,72,512]{2,1,0:T(8,128)(2,1)S(1)}, u32[]{:S(2)}, u32[]{:S(2)}) async-start(bf16[8,72,512]{2,1,0:T(8,128)(2,1)} %sort.1), calls=%async_computation.4 | async-start | bytes 1179648 | tf_op jit(solution)/shard_map/all_to_all | solution.py:357
Sparse Core Ops, SparseCore 0:
  10.1 49.3 all-gather.1

commit v7 on v6

--- a/solution.py
+++ b/solution.py
@@ -54,12 +54,11 @@
 
 
 def select(columns, panel_ref, holder_ref, *refs):
-    tenant_refs, (sent_ref, slot_ref, place_ref, table) = refs[:columns], refs[columns:]
+    tenant_refs, (sent_ref, slot_ref, place_ref, table) = refs[:columns], refs[-4:]
     seqs = sent_ref.shape[1]
     for t in range(holder_ref.shape[0]):
         table[holder_ref[t]] = jnp.int32(t)
     here = lax.axis_index("x")
-    slot_ref[seqs] = lax.axis_index("c")
     for back, tenant_ref in enumerate(tenant_refs):
         there = lax.rem(here + columns - back, columns)
         for s in range(seqs):
@@ -71,7 +70,19 @@
             sent_ref[there, s] = panel_ref[row]
 
 
-def low(slot_ref, panel0_ref, panel1_ref, x_ref, _, low_ref, ups_ref):
+def stack(chips, *refs):
+    slices, (out_ref, sem) = refs[:chips], refs[chips:]
+    here = lax.axis_index("y")
+    copies = []
+    for back, ref in enumerate(slices):
+        there = lax.rem(here + chips - back, chips)
+        copies.append(pltpu.make_async_copy(ref, out_ref.at[there], sem.at[back]))
+        copies[-1].start()
+    for copy in copies:
+        copy.wait()
+
+
+def low(slot_ref, panel0_ref, panel1_ref, x_ref, low_ref, ups_ref):
     rows, rank = low_ref.shape[1], low_ref.shape[2] // 2
     total = ups = 0.0
     for side, panel_ref in enumerate((panel0_ref, panel1_ref)):
@@ -90,9 +101,9 @@
     ups_ref[0] = ups.astype(BF16)
 
 
-def project(slot_ref, low_ref, other_ref, ups_ref, dy_ref, sent_ref):
+def project(low_ref, other_ref, ups_ref, dy_ref, sent_ref):
     rows = low_ref.shape[1]
-    chips, _, keys, _ = dy_ref.shape
+    chips, keys, _ = dy_ref.shape
     low_u = (low_ref[0].astype(F32) + other_ref[0].astype(F32)).astype(BF16)
     dy = dy_ref[...].reshape(chips * keys, 2 * rows)
     parts = [
@@ -105,9 +116,9 @@
         sent_ref[y, 0, keys:] = ups_ref[0]
 
 
-def lower(slot_ref, got_ref, dy_ref, low_ref):
+def lower(got_ref, dy_ref, low_ref):
     _, rank, rows = low_ref.shape
-    chips, _, keys, _ = dy_ref.shape
+    chips, keys, _ = dy_ref.shape
     ups = got_ref[:, 0, keys:].reshape(chips * keys, LANES)
     dy = dy_ref[...].reshape(chips * keys, 2 * rows)
     for side in range(2):
@@ -140,9 +151,17 @@
         sent_ref[x, 0] = panel
 
 
-def backward(slot_ref, low_ref, dy_ref, weight_ref, panel_ref, input_ref):
+def backward(slot_ref, low_ref, dy_ref, other_ref, weight_ref, panel_ref, input_ref):
+    first = lax.axis_index("c") == 0
+    dy, other = dy_ref[...], other_ref[...]
+    both = jnp.concatenate(
+        [jnp.where(first, dy, other), jnp.where(first, other, dy)], axis=1
+    )
     frozen = lax.dot_general(
-        dy_ref[...], weight_ref[...], (((0,), (1,)), ((), ())), preferred_element_type=F32
+        both.reshape(-1, dy.shape[2]),
+        weight_ref[...],
+        (((0,), (1,)), ((), ())),
+        preferred_element_type=F32,
     )
     update = lax.dot_general(
         low_ref[0],
@@ -197,8 +216,23 @@
     scale = ADAPTER_SCALE / math.sqrt(seqs * rows)
     struct = jax.ShapeDtypeStruct
 
-    dy = lax.all_gather(cotangent.T, ("y", "c"), axis=0, tiled=True)
-    dy_halves = dy.reshape(chips, 2, keys, dy.shape[1])
+    own = cotangent.T
+    slices = [own] + [
+        lax.ppermute(own, "y", [(y, (y + d) % chips) for y in range(chips)])
+        for d in range(1, chips)
+    ]
+    near = [slices[d] for d in sorted({1, chips - 1})]
+    anywhere = pl.BlockSpec(memory_space=pl.ANY)
+    dy = pl.pallas_call(
+        functools.partial(stack, chips),
+        out_shape=struct((chips,) + own.shape, BF16),
+        in_specs=[anywhere] * chips,
+        out_specs=anywhere,
+        scratch_shapes=[pltpu.SemaphoreType.DMA((chips,))],
+        compiler_params=PART,
+        name="stack",
+    )(*slices)
+    other_dy = lax.ppermute(dy, "c", SWAP)
 
     tenants = [sequence_tenant] + [
         lax.ppermute(sequence_tenant, "x", [(x, (x + d) % columns) for x in range(columns)])
@@ -217,15 +251,15 @@
         functools.partial(select, columns),
         out_shape=(
             struct((columns, seqs, tall, width), BF16),
-            struct((seqs + 1,), jnp.int32),
+            struct((seqs,), jnp.int32),
             struct((columns * seqs,), jnp.int32),
         ),
-        in_specs=[VMEM] + [SMEM] * (1 + columns),
+        in_specs=[VMEM] + [SMEM] * (1 + columns) + [anywhere] * len(near),
         out_specs=(VMEM, SMEM, SMEM),
         scratch_shapes=[pltpu.SMEM((slots,), jnp.int32)],
         compiler_params=PART,
         name="select",
-    )(panels, slot_holder_tenant, *tenants)
+    )(panels, slot_holder_tenant, *tenants, *near)
     panels = lax.all_to_all(sent, "x", 0, 0, tiled=True)
 
     pairs = seqs // 2
@@ -244,7 +278,6 @@
                     lambda p, slot: (slot[2 * p + 1] % columns, 2 * p + 1, 0, 0),
                 ),
                 pl.BlockSpec((2 * rows, width), lambda p, slot: (p, 0)),
-                pl.BlockSpec(memory_space=pl.ANY),
             ],
             out_specs=(
                 pl.BlockSpec((1, rows, 2 * rank), lambda p, slot: (p, 0, 0)),
@@ -257,43 +290,35 @@
         ),
         compiler_params=ALL,
         name="low",
-    )(slot_of, panels, panels, activations, dy)
+    )(slot_of, panels, panels, activations)
     other_low = lax.ppermute(low_u, "c", SWAP)
-    dy_pair = pl.BlockSpec(
-        (chips, 1, keys, 2 * rows), lambda p, slot: (0, slot[seqs], 0, p)
-    )
-    mixed = pl.BlockSpec((chips, 1, 2 * keys, 2 * rank), lambda p, slot: (0, p, 0, 0))
+    dy_pair = pl.BlockSpec((chips, keys, 2 * rows), lambda p: (0, 0, p))
+    mixed = pl.BlockSpec((chips, 1, 2 * keys, 2 * rank), lambda p: (0, p, 0, 0))
     sent = pl.pallas_call(
         project,
-        grid_spec=pltpu.PrefetchScalarGridSpec(
-            num_scalar_prefetch=1,
-            grid=(pairs,),
-            in_specs=[
-                pl.BlockSpec((1, rows, 2 * rank), lambda p, slot: (p, 0, 0)),
-                pl.BlockSpec((1, rows, 2 * rank), lambda p, slot: (p, 0, 0)),
-                pl.BlockSpec((1, keys, 2 * rank), lambda p, slot: (p, 0, 0)),
-                dy_pair,
-            ],
-            out_specs=mixed,
-        ),
+        grid=(pairs,),
+        in_specs=[
+            pl.BlockSpec((1, rows, 2 * rank), lambda p: (p, 0, 0)),
+            pl.BlockSpec((1, rows, 2 * rank), lambda p: (p, 0, 0)),
+            pl.BlockSpec((1, keys, 2 * rank), lambda p: (p, 0, 0)),
+            dy_pair,
+        ],
+        out_specs=mixed,
         out_shape=struct((chips, pairs, 2 * keys, 2 * rank), BF16),
         compiler_params=STEPS,
         name="project",
-    )(slot_of, low_u, other_low, ups, dy_halves)
+    )(low_u, other_low, ups, dy)
     got = lax.all_to_all(sent, "y", 0, 0, tiled=True)
 
     low_g = pl.pallas_call(
         lower,
-        grid_spec=pltpu.PrefetchScalarGridSpec(
-            num_scalar_prefetch=1,
-            grid=(pairs,),
-            in_specs=[mixed, dy_pair],
-            out_specs=pl.BlockSpec((2, rank, rows), lambda p, slot: (p, 0, 0)),
-        ),
+        grid=(pairs,),
+        in_specs=[mixed, dy_pair],
+        out_specs=pl.BlockSpec((2, rank, rows), lambda p: (p, 0, 0)),
         out_shape=struct((seqs, rank, rows), BF16),
         compiler_params=STEPS,
         name="lower",
-    )(slot_of, got, dy_halves)
+    )(got, dy)
     other_low = lax.ppermute(low_g, "c", SWAP)
     part_b = pl.pallas_call(
         functools.partial(tally, scale),
@@ -328,7 +353,8 @@
             grid=(seqs,),
             in_specs=[
                 pl.BlockSpec((1, rank, rows), lambda s, slot: (s, 0, 0)),
-                pl.BlockSpec((dy.shape[0], rows), lambda s, slot: (0, s)),
+                pl.BlockSpec((chips, keys, rows), lambda s, slot: (0, 0, s)),
+                pl.BlockSpec((chips, keys, rows), lambda s, slot: (0, 0, s)),
                 pl.BlockSpec(key_weight.shape, lambda s, slot: (0, 0)),
                 pl.BlockSpec((1, 1, tall, width), lambda s, slot: (slot[s] % columns, s, 0, 0)),
             ],
@@ -342,7 +368,7 @@
             transcendentals=0,
         ),
         name="backward",
-    )(slot_of, low_g, dy, key_weight, panels)
+    )(slot_of, low_g, dy, other_dy, key_weight, panels)
     got = lax.all_to_all(sent, "x", 0, 0, tiled=True)
 
     sent = pl.pallas_call(

time: 155 us -> 164 us (1.058)
  starting transfers between devices: 32.4 us -> 77.2 us
  blocking collectives: 61.5 us -> 25.5 us
  between operations: 14.2 us -> 0.94 us
  waiting for transfers between devices: 24.2 us -> 34.7 us
    all_to_all x2 -> x0, blocking collectives: 38.1 us -> none  [the longest x1 19.4 us: local(): panels = lax.all_to_all(sent, 'x', 0, 0, tiled=True)]
    ppermute x0 -> x8, starting transfers between devices: none -> 31.5 us  [the longest x7 28.9 us: local(): lax.ppermute(own, 'y', [(y, (y + d) % chips) for y in range(chips)])]
    all_to_all x0 -> x2, waiting for transfers between devices: none -> 13.4 us  [the longest x1 13.4 us: local(): got = lax.all_to_all(sent, 'x', 0, 0, tiled=True)]
    ppermute x0 -> x8, waiting for transfers between devices: none -> 8.56 us  [the longest x7 8.56 us: local(): lax.ppermute(own, 'y', [(y, (y + d) % chips) for y in range(chips)])]
    all_to_all x0 -> x2, starting transfers between devices: none -> 8.13 us  [the longest x1 4.11 us: local(): got = lax.all_to_all(sent, 'x', 0, 0, tiled=True)]
    all_to_all x1, waiting for transfers between devices: 7.18 us -> 0.44 us  [local(): panels = lax.all_to_all(sent, 'z', 0, 0, tiled=True)]
    all_to_all x1, starting transfers between devices: 3.54 us -> 6.44 us  [local(): got = lax.all_to_all(sent, 'z', 0, 0, tiled=True)]
    all_to_all x1, blocking collectives: 23.4 us -> 25.5 us  [local(): got = lax.all_to_all(sent, 'y', 0, 0, tiled=True)]
  transfers between devices with their start and end apart: 8 -> 17, of which waited for: 5 -> 7; matrix products, arithmetic and copies ran while one was open for 0% -> 0% of each run, Pallas kernels for 6% -> 8%
where the time goes in v7:
time: 164 us; the launch traced here: 163 us
  starting transfers between devices  77.2 us (47%)
  waiting for transfers between devices  34.7 us (21%)
  blocking collectives  25.5 us (16%)
  Pallas kernels  21 us (13%)
  local copies, waits for them, and re-layouts  3.26 us (2%)
    ppermute x7, starting transfers between devices, local(): lax.ppermute(own, 'y', [(y, (y + d) % chips) for y in range(chips)])  28.9 us
    all_to_all x1, blocking collectives, local(): got = lax.all_to_all(sent, 'y', 0, 0, tiled=True)  25.5 us
    all_to_all x1, waiting for transfers between devices, local(): got = lax.all_to_all(sent, 'x', 0, 0, tiled=True)  13.4 us
    ppermute x3, starting transfers between devices, local(): lax.ppermute(sequence_tenant, 'x', [(x, (x + d) % columns) for x in range...  11.1 us
    all_to_all x1, starting transfers between devices, local(): panels = lax.all_to_all(sent, 'z', 0, 0, tiled=True)  10.9 us
    all_to_all x1, waiting for transfers between devices, local(): got = lax.all_to_all(sent, 'z', 0, 0, tiled=True)  10.7 us
    ppermute x7, waiting for transfers between devices, local(): lax.ppermute(own, 'y', [(y, (y + d) % chips) for y in range(chips)])  8.56 us
    pallas_call x1, Pallas kernels, local(): pl.pallas_call(backward, grid_spec=pltpu.PrefetchScalarGridSpec(num_scala...  6.62 us
  transfers between devices with their start and end apart: 17, of which 7 were waited for; matrix products, arithmetic and copies ran while one was open for 0% of the time, Pallas kernels for 8%

profile of v7, /device:TPU:1, one launch (start us, length us, event | category | flops | bytes accessed | tf_op | source)
XLA Modules:
  0.0 162.5 jit_solution(3111296341455426556)
XLA Ops:
  2.5 10.9 %all-to-all-start = ((bf16[8,72,512]{2,1,0:T(8,128)(2,1)}), bf16[8,72,512]{2,1,0:T(8,128)(2,1)S(1)}, u32[]{:S(2)}, u32[]{:S(2)}) async-start(bf16[8,72,512]{2,1,0:T(8,128)(2,1)} %prepare.1), calls=%async_computation | async-start | bytes 1179648 | tf_op jit(solution)/shard_map/all_to_all | solution.py:249
  13.4 5.1 %collective-permute-start.4 = (bf16[64,1536]{1,0:T(8,128)(2,1)S(1)}, bf16[64,1536]{1,0:T(8,128)(2,1)S(1)}, u32[]{:S(2)}, u32[]{:S(2)}) collective-permute-start(bf16[64,1536]{1,0:T(8,128)(2,1)S(1)} %bitcast.1), channel_id=1, source_target_pairs={{0,14},{2,0},{4,2},{6,4},{8,6},{10,8},{12,10},{14,12},{1,15},{3,1}... | collective-permute-start | bytes 589832 | tf_op jit(solution)/shard_map/ppermute | solution.py:221
  20.4 4.7 %collective-permute-start.1 = (s32[4]{0:T(128)S(1)}, s32[4]{0:T(128)S(1)}, u32[]{:S(2)}, u32[]{:S(2)}) collective-permute-start(s32[4]{0:T(128)S(1)} %copy-done.9), channel_id=1, source_target_pairs={{0,32},{16,48},{32,0},{48,16},{1,33},{17,49},{33,1},{49,17},{2,34}... | collective-permute-start | bytes 56 | tf_op jit(solution)/shard_map/ppermute | solution.py:238
  25.1 2.2 %collective-permute-start = (s32[4]{0:T(128)S(1)}, s32[4]{0:T(128)S(1)}, u32[]{:S(2)}, u32[]{:S(2)}) collective-permute-start(s32[4]{0:T(128)S(1)} %copy-done.9), channel_id=1, source_target_pairs={{0,16},{16,32},{32,48},{48,0},{1,17},{17,33},{33,49},{49,1},{2,18}... | collective-permute-start | bytes 56 | tf_op jit(solution)/shard_map/ppermute | solution.py:238
  27.3 4.3 %collective-permute-start.2 = (s32[4]{0:T(128)S(1)}, s32[4]{0:T(128)S(1)}, u32[]{:S(2)}, u32[]{:S(2)}) collective-permute-start(s32[4]{0:T(128)S(1)} %copy-done.9), channel_id=1, source_target_pairs={{0,48},{16,0},{32,16},{48,32},{1,49},{17,1},{33,17},{49,33},{2,50}... | collective-permute-start | bytes 56 | tf_op jit(solution)/shard_map/ppermute | solution.py:238
  35.0 4.0 %all-to-all-start.1 = ((bf16[4,4,72,512]{3,2,1,0:T(8,128)(2,1)}), bf16[4,4,72,512]{3,2,1,0:T(8,128)(2,1)S(1)}, u32[]{:S(2)}, u32[]{:S(2)}) async-start(bf16[4,4,72,512]{3,2,1,0:T(8,128)(2,1)} %get-tuple-element.13), calls=%async_computation.1 | async-start | bytes 2359296 | tf_op jit(solution)/shard_map/all_to_all | solution.py:263
  39.0 5.9 %collective-permute-start.10 = (bf16[64,1536]{1,0:T(8,128)(2,1)S(1)}, bf16[64,1536]{1,0:T(8,128)(2,1)S(1)}, u32[]{:S(2)}, u32[]{:S(2)}) collective-permute-start(bf16[64,1536]{1,0:T(8,128)(2,1)S(1)} %bitcast.3), channel_id=1, source_target_pairs={{0,12},{2,14},{4,0},{6,2},{8,4},{10,6},{12,8},{14,10},{1,13},{3,15... | collective-permute-start | bytes 589832 | tf_op jit(solution)/shard_map/ppermute | solution.py:221
  44.9 3.6 %collective-permute-start.9 = (bf16[64,1536]{1,0:T(8,128)(2,1)S(1)}, bf16[64,1536]{1,0:T(8,128)(2,1)S(1)}, u32[]{:S(2)}, u32[]{:S(2)}) collective-permute-start(bf16[64,1536]{1,0:T(8,128)(2,1)S(1)} %bitcast.4), channel_id=1, source_target_pairs={{0,10},{2,12},{4,14},{6,0},{8,2},{10,4},{12,6},{14,8},{1,11},{3,13... | collective-permute-start | bytes 589832 | tf_op jit(solution)/shard_map/ppermute | solution.py:221
  48.6 4.8 %collective-permute-start.8 = (bf16[64,1536]{1,0:T(8,128)(2,1)S(1)}, bf16[64,1536]{1,0:T(8,128)(2,1)S(1)}, u32[]{:S(2)}, u32[]{:S(2)}) collective-permute-start(bf16[64,1536]{1,0:T(8,128)(2,1)S(1)} %bitcast.5), channel_id=1, source_target_pairs={{0,8},{2,10},{4,12},{6,14},{8,0},{10,2},{12,4},{14,6},{1,9},{3,11}... | collective-permute-start | bytes 589832 | tf_op jit(solution)/shard_map/ppermute | solution.py:221
  53.3 2.2 %collective-permute-start.7 = (bf16[64,1536]{1,0:T(8,128)(2,1)S(1)}, bf16[64,1536]{1,0:T(8,128)(2,1)S(1)}, u32[]{:S(2)}, u32[]{:S(2)}) collective-permute-start(bf16[64,1536]{1,0:T(8,128)(2,1)S(1)} %bitcast.6), channel_id=1, source_target_pairs={{0,6},{2,8},{4,10},{6,12},{8,14},{10,0},{12,2},{14,4},{1,7},{3,9},... | collective-permute-start | bytes 589832 | tf_op jit(solution)/shard_map/ppermute | solution.py:221
  55.5 5.4 %collective-permute-start.6 = (bf16[64,1536]{1,0:T(8,128)(2,1)S(1)}, bf16[64,1536]{1,0:T(8,128)(2,1)S(1)}, u32[]{:S(2)}, u32[]{:S(2)}) collective-permute-start(bf16[64,1536]{1,0:T(8,128)(2,1)S(1)} %bitcast.7), channel_id=1, source_target_pairs={{0,4},{2,6},{4,8},{6,10},{8,12},{10,14},{12,0},{14,2},{1,5},{3,7},... | collective-permute-start | bytes 589832 | tf_op jit(solution)/shard_map/ppermute | solution.py:221
  62.0 3.3 %low.1 = (bf16[2,384,128]{2,1,0:T(8,128)(2,1)}, bf16[2,64,128]{2,1,0:T(8,128)(2,1)}) custom-call(s32[4]{0:T(128)} %copy-done.7, bf16[4,4,72,512]{3,2,1,0:T(8,128)(2,1)} %copy-done.10, bf16[4,4,72,512]{3,2,1,0:T(8,128)(2,1)} %copy-done.10, bf16[1536,512]{1,0:T(8,128)(2,1)} %x_ref.3), custom_call_target="tpu_custom_call" | custom-call | tf_op jit(solution)/shard_map/low/pallas_call | solution.py:266
  65.3 4.9 %collective-permute-start.5 = (bf16[2,384,128]{2,1,0:T(8,128)(2,1)}, bf16[2,384,128]{2,1,0:T(8,128)(2,1)S(1)}, u32[]{:S(2)}, u32[]{:S(2)}) collective-permute-start(bf16[2,384,128]{2,1,0:T(8,128)(2,1)} %get-tuple-element.14.low_ref), channel_id=1, source_target_pairs={{0,1},{1,0},{2,3},{3,2},{4,5},{5,4},{6,7},{7,6},{8,9},{9,8},{10,11... | collective-permute-start | bytes 589832 | tf_op jit(solution)/shard_map/ppermute | solution.py:294
  70.3 5.1 %collective-permute-done.7.refs_3_ = bf16[64,1536]{1,0:T(8,128)(2,1)S(1)} collective-permute-done((bf16[64,1536]{1,0:T(8,128)(2,1)S(1)}, bf16[64,1536]{1,0:T(8,128)(2,1)S(1)}, u32[]{:S(2)}, u32[]{:S(2)}) %collective-permute-start.7) | collective-permute-done | bytes 196640 | tf_op jit(solution)/shard_map/ppermute | solution.py:221
  75.4 3.5 %collective-permute-done.6.refs_2_ = bf16[64,1536]{1,0:T(8,128)(2,1)S(1)} collective-permute-done((bf16[64,1536]{1,0:T(8,128)(2,1)S(1)}, bf16[64,1536]{1,0:T(8,128)(2,1)S(1)}, u32[]{:S(2)}, u32[]{:S(2)}) %collective-permute-start.6) | collective-permute-done | bytes 196640 | tf_op jit(solution)/shard_map/ppermute | solution.py:221
  78.8 2.1 %stack.1.dy_ref = bf16[8,64,1536]{2,1,0:T(8,128)(2,1)S(1)} custom-call(bf16[64,1536]{1,0:T(8,128)(2,1)S(1)} %bitcast.8, bf16[64,1536]{1,0:T(8,128)(2,1)S(1)} %collective-permute-done.3.refs_4_.refs_1_, bf16[64,1536]{1,0:T(8,128)(2,1)S(1)} %collective-permute-done.6.refs_2_, bf16[64,1536]{1,0:T(8,128)(2,1)S(1)} %collective-permute-done.7.refs_3_, ...), custom_call_target="tpu_custom_call" | custom-call | tf_op jit(solution)/shard_map/stack/pallas_call | solution.py:226
  81.9 25.5 %all_to_all.25.got_ref = bf16[8,2,128,128]{3,2,1,0:T(8,128)(2,1)S(1)} all-to-all(bf16[8,2,128,128]{3,2,1,0:T(8,128)(2,1)S(1)} %project.1), channel_id=1, replica_groups=mesh['z'=8,'x'=4,'y'=8,'c'=2] {'y'}, dimensions={0} | all-to-all | bytes 1048576 | tf_op jit(solution)/shard_map/all_to_all | solution.py:311
  108.3 4.2 %collective-permute-start.11 = (bf16[4,64,384]{2,1,0:T(8,128)(2,1)S(1)}, bf16[4,64,384]{2,1,0:T(8,128)(2,1)S(1)}, u32[]{:S(2)}, u32[]{:S(2)}) collective-permute-start(bf16[4,64,384]{2,1,0:T(8,128)(2,1)S(1)} %lower.1.low_ref), channel_id=1, source_target_pairs={{0,1},{1,0},{2,3},{3,2},{4,5},{5,4},{6,7},{7,6},{8,9},{9,8},{10,11... | collective-permute-start | bytes 589832 | tf_op jit(solution)/shard_map/ppermute | solution.py:322
  116.2 4.1 %all-to-all-start.3 = ((bf16[4,4,72,512]{3,2,1,0:T(8,128)(2,1)}), bf16[4,4,72,512]{3,2,1,0:T(8,128)(2,1)S(1)}, u32[]{:S(2)}, u32[]{:S(2)}) async-start(bf16[4,4,72,512]{3,2,1,0:T(8,128)(2,1)} %copy-done.2), calls=%async_computation.3 | async-start | bytes 2359296 | tf_op jit(solution)/shard_map/all_to_all | solution.py:372
  120.3 2.5 %collective-permute-start.12 = (bf16[8,64,1536]{2,1,0:T(8,128)(2,1)S(1)}, bf16[8,64,1536]{2,1,0:T(8,128)(2,1)}, u32[]{:S(2)}, u32[]{:S(2)}) collective-permute-start(bf16[8,64,1536]{2,1,0:T(8,128)(2,1)S(1)} %stack.1.dy_ref), channel_id=1, source_target_pairs={{0,1},{1,0},{2,3},{3,2},{4,5},{5,4},{6,7},{7,6},{8,9},{9,8},{10,11... | collective-permute-start | bytes 4718600 | tf_op jit(solution)/shard_map/ppermute | solution.py:235
  122.9 13.4 %all-to-all-done.3.got_ref = bf16[4,4,72,512]{3,2,1,0:T(8,128)(2,1)S(1)} async-done(((bf16[4,4,72,512]{3,2,1,0:T(8,128)(2,1)}), bf16[4,4,72,512]{3,2,1,0:T(8,128)(2,1)S(1)}, u32[]{:S(2)}, u32[]{:S(2)}) %all-to-all-start.3) | async-done | bytes 1179680 | tf_op jit(solution)/shard_map/all_to_all | solution.py:372
  137.9 6.4 %all-to-all-start.4 = ((bf16[8,72,512]{2,1,0:T(8,128)(2,1)}), bf16[8,72,512]{2,1,0:T(8,128)(2,1)S(1)}, u32[]{:S(2)}, u32[]{:S(2)}) async-start(bf16[8,72,512]{2,1,0:T(8,128)(2,1)} %sort.1), calls=%async_computation.4 | async-start | bytes 1179648 | tf_op jit(solution)/shard_map/all_to_all | solution.py:383
  144.3 6.6 %backward.1 = bf16[1536,512]{1,0:T(8,128)(2,1)} custom-call(s32[4]{0:T(128)} %copy-done.7, bf16[4,64,384]{2,1,0:T(8,128)(2,1)} %copy-done.3, bf16[8,64,1536]{2,1,0:T(8,128)(2,1)} %copy-done, bf16[8,64,1536]{2,1,0:T(8,128)(2,1)} %collective-permute-done.12.other_ref, bf16[512,1024]{1,0:T(8,128)(2,1)} %weight_ref.1, bf16[4,4,72,512]{3,2,1,0:T(8,128)(2,1)} %copy-done.10), custom_call_target="tpu_custom_call" | custom-call | flops 1711276032 | bytes 6291456 | tf_op jit(solution)/shard_map/backward/pallas_call | solution.py:349
  150.9 10.7 %all-to-all-done.4.got_ref = bf16[8,72,512]{2,1,0:T(8,128)(2,1)S(1)} async-done(((bf16[8,72,512]{2,1,0:T(8,128)(2,1)}), bf16[8,72,512]{2,1,0:T(8,128)(2,1)S(1)}, u32[]{:S(2)}, u32[]{:S(2)}) %all-to-all-start.4) | async-done | bytes 589856 | tf_op jit(solution)/shard_map/all_to_all | solution.py:383
  (44 shorter events, 16.1 us)
Async XLA Ops:
  0.6 12.8 %copy-start.4 = (bf16[1536,64]{0,1:T(8,128)(2,1)S(1)}, bf16[1536,64]{0,1:T(8,128)(2,1)}, u32[]{:S(2)}) copy-start(bf16[1536,64]{0,1:T(8,128)(2,1)} %param.8) | copy-start | bytes 589828
  0.6 19.8 %copy-start.9 = (s32[4]{0:T(128)S(1)}, s32[4]{0:T(128)}, u32[]{:S(2)}) copy-start(s32[4]{0:T(128)} %refs_0_.1) | copy-start | bytes 52
  0.7 32.1 %copy-start.8 = (s32[32]{0:T(128)S(1)}, s32[32]{0:T(128)}, u32[]{:S(2)}) copy-start(s32[32]{0:T(128)} %holder_ref.1) | copy-start | bytes 388
  2.5 30.2 %all-to-all-start = ((bf16[8,72,512]{2,1,0:T(8,128)(2,1)}), bf16[8,72,512]{2,1,0:T(8,128)(2,1)S(1)}, u32[]{:S(2)}, u32[]{:S(2)}) async-start(bf16[8,72,512]{2,1,0:T(8,128)(2,1)} %prepare.1), calls=%async_computation | async-start | bytes 1179648 | tf_op jit(solution)/shard_map/all_to_all | solution.py:249
  13.4 18.9 %collective-permute-start.4 = (bf16[64,1536]{1,0:T(8,128)(2,1)S(1)}, bf16[64,1536]{1,0:T(8,128)(2,1)S(1)}, u32[]{:S(2)}, u32[]{:S(2)}) collective-permute-start(bf16[64,1536]{1,0:T(8,128)(2,1)S(1)} %bitcast.1), channel_id=1, source_target_pairs={{0,14},{2,0},{4,2},{6,4},{8,6},{10,8},{12,10},{14,12},{1,15},{3,1}... | collective-permute-start | bytes 589832 | tf_op jit(solution)/shard_map/ppermute | solution.py:221
  18.5 13.8 %collective-permute-start.3 = (bf16[64,1536]{1,0:T(8,128)(2,1)S(1)}, bf16[64,1536]{1,0:T(8,128)(2,1)S(1)}, u32[]{:S(2)}, u32[]{:S(2)}) collective-permute-start(bf16[64,1536]{1,0:T(8,128)(2,1)S(1)} %bitcast.2), channel_id=1, source_target_pairs={{0,2},{2,4},{4,6},{6,8},{8,10},{10,12},{12,14},{14,0},{1,3},{3,5},... | collective-permute-start | bytes 589832 | tf_op jit(solution)/shard_map/ppermute | solution.py:221
  20.4 11.2 %collective-permute-start.1 = (s32[4]{0:T(128)S(1)}, s32[4]{0:T(128)S(1)}, u32[]{:S(2)}, u32[]{:S(2)}) collective-permute-start(s32[4]{0:T(128)S(1)} %copy-done.9), channel_id=1, source_target_pairs={{0,32},{16,48},{32,0},{48,16},{1,33},{17,49},{33,1},{49,17},{2,34}... | collective-permute-start | bytes 56 | tf_op jit(solution)/shard_map/ppermute | solution.py:238
  25.1 6.5 %collective-permute-start = (s32[4]{0:T(128)S(1)}, s32[4]{0:T(128)S(1)}, u32[]{:S(2)}, u32[]{:S(2)}) collective-permute-start(s32[4]{0:T(128)S(1)} %copy-done.9), channel_id=1, source_target_pairs={{0,16},{16,32},{32,48},{48,0},{1,17},{17,33},{33,49},{49,1},{2,18}... | collective-permute-start | bytes 56 | tf_op jit(solution)/shard_map/ppermute | solution.py:238
  27.3 5.0 %collective-permute-start.2 = (s32[4]{0:T(128)S(1)}, s32[4]{0:T(128)S(1)}, u32[]{:S(2)}, u32[]{:S(2)}) collective-permute-start(s32[4]{0:T(128)S(1)} %copy-done.9), channel_id=1, source_target_pairs={{0,48},{16,0},{32,16},{48,32},{1,49},{17,1},{33,17},{49,33},{2,50}... | collective-permute-start | bytes 56 | tf_op jit(solution)/shard_map/ppermute | solution.py:238
  35.0 26.0 %all-to-all-start.1 = ((bf16[4,4,72,512]{3,2,1,0:T(8,128)(2,1)}), bf16[4,4,72,512]{3,2,1,0:T(8,128)(2,1)S(1)}, u32[]{:S(2)}, u32[]{:S(2)}) async-start(bf16[4,4,72,512]{3,2,1,0:T(8,128)(2,1)} %get-tuple-element.13), calls=%async_computation.1 | async-start | bytes 2359296 | tf_op jit(solution)/shard_map/all_to_all | solution.py:263
  39.0 26.3 %collective-permute-start.10 = (bf16[64,1536]{1,0:T(8,128)(2,1)S(1)}, bf16[64,1536]{1,0:T(8,128)(2,1)S(1)}, u32[]{:S(2)}, u32[]{:S(2)}) collective-permute-start(bf16[64,1536]{1,0:T(8,128)(2,1)S(1)} %bitcast.3), channel_id=1, source_target_pairs={{0,12},{2,14},{4,0},{6,2},{8,4},{10,6},{12,8},{14,10},{1,13},{3,15... | collective-permute-start | bytes 589832 | tf_op jit(solution)/shard_map/ppermute | solution.py:221
  44.9 25.4 %collective-permute-start.9 = (bf16[64,1536]{1,0:T(8,128)(2,1)S(1)}, bf16[64,1536]{1,0:T(8,128)(2,1)S(1)}, u32[]{:S(2)}, u32[]{:S(2)}) collective-permute-start(bf16[64,1536]{1,0:T(8,128)(2,1)S(1)} %bitcast.4), channel_id=1, source_target_pairs={{0,10},{2,12},{4,14},{6,0},{8,2},{10,4},{12,6},{14,8},{1,11},{3,13... | collective-permute-start | bytes 589832 | tf_op jit(solution)/shard_map/ppermute | solution.py:221
  48.6 21.7 %collective-permute-start.8 = (bf16[64,1536]{1,0:T(8,128)(2,1)S(1)}, bf16[64,1536]{1,0:T(8,128)(2,1)S(1)}, u32[]{:S(2)}, u32[]{:S(2)}) collective-permute-start(bf16[64,1536]{1,0:T(8,128)(2,1)S(1)} %bitcast.5), channel_id=1, source_target_pairs={{0,8},{2,10},{4,12},{6,14},{8,0},{10,2},{12,4},{14,6},{1,9},{3,11}... | collective-permute-start | bytes 589832 | tf_op jit(solution)/shard_map/ppermute | solution.py:221
  53.3 22.0 %collective-permute-start.7 = (bf16[64,1536]{1,0:T(8,128)(2,1)S(1)}, bf16[64,1536]{1,0:T(8,128)(2,1)S(1)}, u32[]{:S(2)}, u32[]{:S(2)}) collective-permute-start(bf16[64,1536]{1,0:T(8,128)(2,1)S(1)} %bitcast.6), channel_id=1, source_target_pairs={{0,6},{2,8},{4,10},{6,12},{8,14},{10,0},{12,2},{14,4},{1,7},{3,9},... | collective-permute-start | bytes 589832 | tf_op jit(solution)/shard_map/ppermute | solution.py:221
  55.5 23.3 %collective-permute-start.6 = (bf16[64,1536]{1,0:T(8,128)(2,1)S(1)}, bf16[64,1536]{1,0:T(8,128)(2,1)S(1)}, u32[]{:S(2)}, u32[]{:S(2)}) collective-permute-start(bf16[64,1536]{1,0:T(8,128)(2,1)S(1)} %bitcast.7), channel_id=1, source_target_pairs={{0,4},{2,6},{4,8},{6,10},{8,12},{10,14},{12,0},{14,2},{1,5},{3,7},... | collective-permute-start | bytes 589832 | tf_op jit(solution)/shard_map/ppermute | solution.py:221
  65.3 15.6 %copy-start.5 = (bf16[2,384,128]{2,1,0:T(8,128)(2,1)S(1)}, bf16[2,384,128]{2,1,0:T(8,128)(2,1)}, u32[]{:S(2)}) copy-start(bf16[2,384,128]{2,1,0:T(8,128)(2,1)} %get-tuple-element.14.low_ref) | copy-start | bytes 589828
  65.3 15.6 %copy-start.6 = (bf16[2,64,128]{2,1,0:T(8,128)(2,1)S(1)}, bf16[2,64,128]{2,1,0:T(8,128)(2,1)}, u32[]{:S(2)}) copy-start(bf16[2,64,128]{2,1,0:T(8,128)(2,1)} %get-tuple-element.15.ups_ref) | copy-start | bytes 98308
  65.3 15.6 %collective-permute-start.5 = (bf16[2,384,128]{2,1,0:T(8,128)(2,1)}, bf16[2,384,128]{2,1,0:T(8,128)(2,1)S(1)}, u32[]{:S(2)}, u32[]{:S(2)}) collective-permute-start(bf16[2,384,128]{2,1,0:T(8,128)(2,1)} %get-tuple-element.14.low_ref), channel_id=1, source_target_pairs={{0,1},{1,0},{2,3},{3,2},{4,5},{5,4},{6,7},{7,6},{8,9},{9,8},{10,11... | collective-permute-start | bytes 589832 | tf_op jit(solution)/shard_map/ppermute | solution.py:294
  80.9 39.4 %copy-start = (bf16[8,64,1536]{2,1,0:T(8,128)(2,1)}, bf16[8,64,1536]{2,1,0:T(8,128)(2,1)S(1)}, u32[]{:S(2)}) copy-start(bf16[8,64,1536]{2,1,0:T(8,128)(2,1)S(1)} %stack.1.dy_ref) | copy-start | bytes 4718596
  107.4 6.2 %copy-start.1 = (bf16[1536,512]{1,0:T(8,128)(2,1)S(1)}, bf16[1536,512]{1,0:T(8,128)(2,1)}, u32[]{:S(2)}) copy-start(bf16[1536,512]{1,0:T(8,128)(2,1)} %x_ref.3) | copy-start | bytes 4718596
  108.3 5.3 %collective-permute-start.11 = (bf16[4,64,384]{2,1,0:T(8,128)(2,1)S(1)}, bf16[4,64,384]{2,1,0:T(8,128)(2,1)S(1)}, u32[]{:S(2)}, u32[]{:S(2)}) collective-permute-start(bf16[4,64,384]{2,1,0:T(8,128)(2,1)S(1)} %lower.1.low_ref), channel_id=1, source_target_pairs={{0,1},{1,0},{2,3},{3,2},{4,5},{5,4},{6,7},{7,6},{8,9},{9,8},{10,11... | collective-permute-start | bytes 589832 | tf_op jit(solution)/shard_map/ppermute | solution.py:322
  116.2 20.0 %all-to-all-start.3 = ((bf16[4,4,72,512]{3,2,1,0:T(8,128)(2,1)}), bf16[4,4,72,512]{3,2,1,0:T(8,128)(2,1)S(1)}, u32[]{:S(2)}, u32[]{:S(2)}) async-start(bf16[4,4,72,512]{3,2,1,0:T(8,128)(2,1)} %copy-done.2), calls=%async_computation.3 | async-start | bytes 2359296 | tf_op jit(solution)/shard_map/all_to_all | solution.py:372
  120.3 24.0 %collective-permute-start.12 = (bf16[8,64,1536]{2,1,0:T(8,128)(2,1)S(1)}, bf16[8,64,1536]{2,1,0:T(8,128)(2,1)}, u32[]{:S(2)}, u32[]{:S(2)}) collective-permute-start(bf16[8,64,1536]{2,1,0:T(8,128)(2,1)S(1)} %stack.1.dy_ref), channel_id=1, source_target_pairs={{0,1},{1,0},{2,3},{3,2},{4,5},{5,4},{6,7},{7,6},{8,9},{9,8},{10,11... | collective-permute-start | bytes 4718600 | tf_op jit(solution)/shard_map/ppermute | solution.py:235
  137.9 23.8 %all-to-all-start.4 = ((bf16[8,72,512]{2,1,0:T(8,128)(2,1)}), bf16[8,72,512]{2,1,0:T(8,128)(2,1)S(1)}, u32[]{:S(2)}, u32[]{:S(2)}) async-start(bf16[8,72,512]{2,1,0:T(8,128)(2,1)} %sort.1), calls=%async_computation.4 | async-start | bytes 1179648 | tf_op jit(solution)/shard_map/all_to_all | solution.py:383
  (4 other events, 3.2 us)

commit v8 on v5

--- a/solution.py
+++ b/solution.py
@@ -54,12 +54,11 @@
 
 
 def select(columns, panel_ref, holder_ref, *refs):
-    tenant_refs, (sent_ref, slot_ref, place_ref, table) = refs[:columns], refs[columns:]
+    tenant_refs, (sent_ref, slot_ref, place_ref, table) = refs[:columns], refs[-4:]
     seqs = sent_ref.shape[1]
     for t in range(holder_ref.shape[0]):
         table[holder_ref[t]] = jnp.int32(t)
     here = lax.axis_index("x")
-    slot_ref[seqs] = lax.axis_index("c")
     for back, tenant_ref in enumerate(tenant_refs):
         there = lax.rem(here + columns - back, columns)
         for s in range(seqs):
@@ -71,9 +70,28 @@
             sent_ref[there, s] = panel_ref[row]
 
 
+def bring(x_ref, *refs):
+    out_ref, sem = refs[-2:]
+    copy = pltpu.make_async_copy(x_ref, out_ref, sem)
+    copy.start()
+    copy.wait()
+
+
+def bring_half(dy_ref, *refs):
+    out_ref, sem = refs[-2:]
+    core = lax.axis_index("c")
+    copies = [
+        pltpu.make_async_copy(dy_ref.at[y, core], out_ref.at[y], sem.at[y])
+        for y in range(out_ref.shape[0])
+    ]
+    for copy in copies:
+        copy.start()
+    for copy in copies:
+        copy.wait()
+
+
 def low(slot_ref, panel0_ref, panel1_ref, x_ref, low_ref, down_ref, ups_ref):
-    rank = down_ref.shape[1]
-    rows = low_ref.shape[1]
+    rows, rank = low_ref.shape[1], low_ref.shape[2] // 2
     total = ups = 0.0
     for side, panel_ref in enumerate((panel0_ref, panel1_ref)):
         panel = panel_ref[0, 0]
@@ -92,9 +110,9 @@
     ups_ref[0] = ups.astype(BF16)
 
 
-def project(slot_ref, low_ref, other_ref, ups_ref, dy_ref, sent_ref):
+def project(low_ref, other_ref, ups_ref, dy_ref, sent_ref):
     rows = low_ref.shape[1]
-    chips, _, keys, _ = dy_ref.shape
+    chips, keys, _ = dy_ref.shape
     low_u = (low_ref[0].astype(F32) + other_ref[0].astype(F32)).astype(BF16)
     dy = dy_ref[...].reshape(chips * keys, 2 * rows)
     parts = [
@@ -107,9 +125,9 @@
         sent_ref[y, 0, keys:] = ups_ref[0]
 
 
-def lower(slot_ref, got_ref, dy_ref, low_ref):
+def lower(got_ref, dy_ref, low_ref):
     _, rank, rows = low_ref.shape
-    chips, _, keys, _ = dy_ref.shape
+    chips, keys, _ = dy_ref.shape
     ups = got_ref[:, 0, keys:].reshape(chips * keys, LANES)
     dy = dy_ref[...].reshape(chips * keys, 2 * rows)
     for side in range(2):
@@ -199,6 +217,17 @@
     dy = lax.all_gather(cotangent.T, ("y", "c"), axis=0, tiled=True)
     dy_halves = dy.reshape(chips, 2, keys, dy.shape[1])
 
+    anywhere = pl.BlockSpec(memory_space=pl.ANY)
+    near_x = pl.pallas_call(
+        bring,
+        out_shape=struct(activations.shape, BF16),
+        in_specs=[anywhere],
+        out_specs=anywhere,
+        scratch_shapes=[pltpu.SemaphoreType.DMA],
+        compiler_params=PART,
+        name="bring_x",
+    )(activations)
+
     tenants = [sequence_tenant] + [
         lax.ppermute(sequence_tenant, "x", [(x, (x + d) % columns) for x in range(columns)])
         for d in range(1, columns)
@@ -216,15 +245,15 @@
         functools.partial(select, columns),
         out_shape=(
             struct((columns, seqs, tall, width), BF16),
-            struct((seqs + 1,), jnp.int32),
+            struct((seqs,), jnp.int32),
             struct((columns * seqs,), jnp.int32),
         ),
-        in_specs=[VMEM] + [SMEM] * (1 + columns),
+        in_specs=[VMEM] + [SMEM] * (1 + columns) + [anywhere],
         out_specs=(VMEM, SMEM, SMEM),
         scratch_shapes=[pltpu.SMEM((slots,), jnp.int32)],
         compiler_params=PART,
         name="select",
-    )(panels, slot_holder_tenant, *tenants)
+    )(panels, slot_holder_tenant, *tenants, near_x)
     panels = lax.all_to_all(sent, "x", 0, 0, tiled=True)
 
     pairs = seqs // 2
@@ -255,45 +284,46 @@
             struct((seqs, rank, width), BF16),
             struct((pairs, keys, 2 * rank), BF16),
         ),
-        compiler_params=ALL,
+        compiler_params=STEPS,
         name="low",
-    )(slot_of, panels, panels, activations)
+    )(slot_of, panels, panels, near_x)
     other_low = lax.ppermute(low_u, "c", SWAP)
-    dy_pair = pl.BlockSpec(
-        (chips, 1, keys, 2 * rows), lambda p, slot: (0, slot[seqs], 0, p)
-    )
-    mixed = pl.BlockSpec((chips, 1, 2 * keys, 2 * rank), lambda p, slot: (0, p, 0, 0))
+    half_dy = pl.pallas_call(
+        bring_half,
+        out_shape=struct((chips, keys, dy.shape[1]), BF16),
+        in_specs=[anywhere, anywhere],
+        out_specs=anywhere,
+        scratch_shapes=[pltpu.SemaphoreType.DMA((chips,))],
+        compiler_params=PART,
+        name="bring_dy",
+    )(dy_halves, low_u)
+    dy_pair = pl.BlockSpec((chips, keys, 2 * rows), lambda p: (0, 0, p))
+    mixed = pl.BlockSpec((chips, 1, 2 * keys, 2 * rank), lambda p: (0, p, 0, 0))
     sent = pl.pallas_call(
         project,
-        grid_spec=pltpu.PrefetchScalarGridSpec(
-            num_scalar_prefetch=1,
-            grid=(pairs,),
-            in_specs=[
-                pl.BlockSpec((1, rows, 2 * rank), lambda p, slot: (p, 0, 0)),
-                pl.BlockSpec((1, rows, 2 * rank), lambda p, slot: (p, 0, 0)),
-                pl.BlockSpec((1, keys, 2 * rank), lambda p, slot: (p, 0, 0)),
-                dy_pair,
-            ],
-            out_specs=mixed,
-        ),
+        grid=(pairs,),
+        in_specs=[
+            pl.BlockSpec((1, rows, 2 * rank), lambda p: (p, 0, 0)),
+            pl.BlockSpec((1, rows, 2 * rank), lambda p: (p, 0, 0)),
+            pl.BlockSpec((1, keys, 2 * rank), lambda p: (p, 0, 0)),
+            dy_pair,
+        ],
+        out_specs=mixed,
         out_shape=struct((chips, pairs, 2 * keys, 2 * rank), BF16),
-        compiler_params=ALL,
+        compiler_params=STEPS,
         name="project",
-    )(slot_of, low_u, other_low, ups, dy_halves)
+    )(low_u, other_low, ups, half_dy)
     got = lax.all_to_all(sent, "y", 0, 0, tiled=True)
 
     low_g = pl.pallas_call(
         lower,
-        grid_spec=pltpu.PrefetchScalarGridSpec(
-            num_scalar_prefetch=1,
-            grid=(pairs,),
-            in_specs=[mixed, dy_pair],
-            out_specs=pl.BlockSpec((2, rank, rows), lambda p, slot: (p, 0, 0)),
-        ),
+        grid=(pairs,),
+        in_specs=[mixed, dy_pair],
+        out_specs=pl.BlockSpec((2, rank, rows), lambda p: (p, 0, 0)),
         out_shape=struct((seqs, rank, rows), BF16),
         compiler_params=STEPS,
         name="lower",
-    )(slot_of, got, dy_halves)
+    )(got, half_dy)
     other_low = lax.ppermute(low_g, "c", SWAP)
     part_b = pl.pallas_call(
         functools.partial(tally, scale),
@@ -320,7 +350,7 @@
         ),
         compiler_params=STEPS,
         name="combine",
-    )(low_g, other_low, part_b, activations)
+    )(low_g, other_low, part_b, near_x)
     input_gradient = pl.pallas_call(
         backward,
         grid=(seqs,),

time: 156 us -> 153 us (0.981)
  waiting for transfers between devices: 24.9 us -> 21.5 us
  local copies, waits for them, and re-layouts: 0.69 us -> 3.98 us
  Pallas kernels: 21.1 us -> 18 us
    unnamed x16 -> x12, local copies, waits for them, and re-layouts: 0.69 us -> 3.98 us
    pallas_call x1, Pallas kernels: 3.29 us -> 1.3 us  [local(): pl.pallas_call(low, grid_spec=pltpu.PrefetchScalarGridSpec(num_scalar_pre...]
    ppermute x3, waiting for transfers between devices: 1.6 us -> 0.01 us  [local(): lax.ppermute(sequence_tenant, 'x', [(x, (x + d) % columns) for x in range...]
    pallas_call x2 -> x4, Pallas kernels: 5.13 us -> 3.97 us  [the longest x1 2.07 us: local(): pl.pallas_call(bring_half, out_shape=struct((chips, keys, dy.shape[1]), B...]
  transfers between devices with their start and end apart: 8 -> 8, of which waited for: 5 -> 3; matrix products, arithmetic and copies ran while one was open for 0% -> 0% of each run, Pallas kernels for 8% -> 8%
where the time goes in v8:
time: 153 us; the launch traced here: 152 us
  blocking collectives  62.6 us (41%)
  starting transfers between devices  31.9 us (21%)
  waiting for transfers between devices  21.5 us (14%)
  Pallas kernels  18 us (12%)
  between operations  14.2 us (9%)
  local copies, waits for them, and re-layouts  3.98 us (3%)
    all_to_all x1, blocking collectives, local(): got = lax.all_to_all(sent, 'y', 0, 0, tiled=True)  24.6 us
    all_to_all x1, blocking collectives, local(): panels = lax.all_to_all(sent, 'x', 0, 0, tiled=True)  19.3 us
    all_to_all x1, blocking collectives, local(): got = lax.all_to_all(sent, 'x', 0, 0, tiled=True)  18.7 us
    all_to_all x1, waiting for transfers between devices, local(): got = lax.all_to_all(sent, 'z', 0, 0, tiled=True)  13.2 us
    ppermute x3, starting transfers between devices, local(): lax.ppermute(sequence_tenant, 'x', [(x, (x + d) % columns) for x in range...  11.1 us
    all_to_all x1, starting transfers between devices, local(): panels = lax.all_to_all(sent, 'z', 0, 0, tiled=True)  11 us
    all_to_all x1, waiting for transfers between devices, local(): panels = lax.all_to_all(sent, 'z', 0, 0, tiled=True)  6.62 us
    pallas_call x1, Pallas kernels, local(): pl.pallas_call(backward, grid=(seqs,), in_specs=[one, pl.BlockSpec((dy.sh...  6.02 us
  transfers between devices with their start and end apart: 8, of which 3 were waited for; matrix products, arithmetic and copies ran while one was open for 0% of the time, Pallas kernels for 8%

profile of v8, /device:TPU:1, one launch (start us, length us, event | category | flops | bytes accessed | tf_op | source)
XLA Modules:
  0.0 152.2 jit_solution(3739093236122527113)
XLA Ops:
  7.9 1.8 %prepare.1 = bf16[8,72,512]{2,1,0:T(8,128)(2,1)} custom-call(bf16[1,64,512]{2,1,0:T(8,128)(2,1)} %down_ref.1, bf16[1,64,64]{2,1,0:T(8,128)(2,1)} %up_ref.1), custom_call_target="tpu_custom_call" | custom-call | tf_op jit(solution)/shard_map/prepare/pallas_call | solution.py:235
  9.7 11.0 %all-to-all-start = ((bf16[8,72,512]{2,1,0:T(8,128)(2,1)}), bf16[8,72,512]{2,1,0:T(8,128)(2,1)S(1)}, u32[]{:S(2)}, u32[]{:S(2)}) async-start(bf16[8,72,512]{2,1,0:T(8,128)(2,1)} %prepare.1), calls=%async_computation | async-start | bytes 1179648 | tf_op jit(solution)/shard_map/all_to_all | solution.py:243
  20.7 4.7 %collective-permute-start.1 = (s32[4]{0:T(128)S(1)}, s32[4]{0:T(128)S(1)}, u32[]{:S(2)}, u32[]{:S(2)}) collective-permute-start(s32[4]{0:T(128)S(1)} %copy-done.3), channel_id=1, source_target_pairs={{0,32},{16,48},{32,0},{48,16},{1,33},{17,49},{33,1},{49,17},{2,34}... | collective-permute-start | bytes 56 | tf_op jit(solution)/shard_map/ppermute | solution.py:232
  25.4 2.2 %collective-permute-start = (s32[4]{0:T(128)S(1)}, s32[4]{0:T(128)S(1)}, u32[]{:S(2)}, u32[]{:S(2)}) collective-permute-start(s32[4]{0:T(128)S(1)} %copy-done.3), channel_id=1, source_target_pairs={{0,16},{16,32},{32,48},{48,0},{1,17},{17,33},{33,49},{49,1},{2,18}... | collective-permute-start | bytes 56 | tf_op jit(solution)/shard_map/ppermute | solution.py:232
  27.6 4.3 %collective-permute-start.2 = (s32[4]{0:T(128)S(1)}, s32[4]{0:T(128)S(1)}, u32[]{:S(2)}, u32[]{:S(2)}) collective-permute-start(s32[4]{0:T(128)S(1)} %copy-done.3), channel_id=1, source_target_pairs={{0,48},{16,0},{32,16},{48,32},{1,49},{17,1},{33,17},{49,33},{2,50}... | collective-permute-start | bytes 56 | tf_op jit(solution)/shard_map/ppermute | solution.py:232
  31.9 1.4 copy-done.1
  33.5 6.6 %all-to-all-done.panel_ref = bf16[8,72,512]{2,1,0:T(8,128)(2,1)S(1)} async-done(((bf16[8,72,512]{2,1,0:T(8,128)(2,1)}), bf16[8,72,512]{2,1,0:T(8,128)(2,1)S(1)}, u32[]{:S(2)}, u32[]{:S(2)}) %all-to-all-start) | async-done | bytes 589856 | tf_op jit(solution)/shard_map/all_to_all | solution.py:243
  40.1 1.3 select.1
  41.4 19.3 %all_to_all.25.panel0_ref.panel1_ref = bf16[4,4,72,512]{3,2,1,0:T(8,128)(2,1)S(1)} all-to-all(bf16[4,4,72,512]{3,2,1,0:T(8,128)(2,1)S(1)} %get-tuple-element.14), channel_id=1, replica_groups=mesh['z'=8,'x'=4,'y'=8,'c'=2] {'x'}, dimensions={0} | all-to-all | bytes 2359296 | tf_op jit(solution)/shard_map/all_to_all | solution.py:257
  60.8 1.3 low.1
  62.8 3.8 %collective-permute-start.3 = (bf16[2,384,128]{2,1,0:T(8,128)(2,1)S(1)}, bf16[2,384,128]{2,1,0:T(8,128)(2,1)S(1)}, u32[]{:S(2)}, u32[]{:S(2)}) collective-permute-start(bf16[2,384,128]{2,1,0:T(8,128)(2,1)S(1)} %get-tuple-element.15.refs_0_.low_ref), channel_id=1, source_target_pairs={{0,1},{1,0},{2,3},{3,2},{4,5},{5,4},{6,7},{7,6},{8,9},{9,8},{10,11... | collective-permute-start | bytes 589832 | tf_op jit(solution)/shard_map/ppermute | solution.py:290
  66.6 1.9 %copy-done = bf16[1024,1536]{1,0:T(8,128)(2,1)S(1)} copy-done((bf16[1024,1536]{1,0:T(8,128)(2,1)S(1)}, bf16[1024,1536]{1,0:T(8,128)(2,1)}, u32[]{:S(2)}) %copy-start) | copy-done | bytes 3145752
  68.5 2.1 %bring_dy.1.dy_ref = bf16[8,64,1536]{2,1,0:T(8,128)(2,1)S(1)} custom-call(bf16[8,2,64,1536]{3,2,1,0:T(8,128)(2,1)S(1)} %bitcast.2, bf16[2,384,128]{2,1,0:T(8,128)(2,1)S(1)} %get-tuple-element.15.refs_0_.low_ref), custom_call_target="tpu_custom_call" | custom-call | tf_op jit(solution)/shard_map/bring_dy/pallas_call | solution.py:291
  70.6 0.9 project.1
  71.5 24.6 %all_to_all.26.got_ref = bf16[8,2,128,128]{3,2,1,0:T(8,128)(2,1)S(1)} all-to-all(bf16[8,2,128,128]{3,2,1,0:T(8,128)(2,1)S(1)} %project.1), channel_id=1, replica_groups=mesh['z'=8,'x'=4,'y'=8,'c'=2] {'y'}, dimensions={0} | all-to-all | bytes 1048576 | tf_op jit(solution)/shard_map/all_to_all | solution.py:316
  96.2 0.9 lower.1.low_ref
  97.0 2.4 %collective-permute-start.4 = (bf16[4,64,384]{2,1,0:T(8,128)(2,1)S(1)}, bf16[4,64,384]{2,1,0:T(8,128)(2,1)S(1)}, u32[]{:S(2)}, u32[]{:S(2)}) collective-permute-start(bf16[4,64,384]{2,1,0:T(8,128)(2,1)S(1)} %lower.1.low_ref), channel_id=1, source_target_pairs={{0,1},{1,0},{2,3},{3,2},{4,5},{5,4},{6,7},{7,6},{8,9},{9,8},{10,11... | collective-permute-start | bytes 589832 | tf_op jit(solution)/shard_map/ppermute | solution.py:327
  99.6 0.9 collective-permute-done.4.other_ref
  100.4 0.9 combine.1
  101.4 18.7 %all_to_all.27.got_ref = bf16[4,4,72,512]{3,2,1,0:T(8,128)(2,1)S(1)} all-to-all(bf16[4,4,72,512]{3,2,1,0:T(8,128)(2,1)S(1)} %get-tuple-element.20), channel_id=1, replica_groups=mesh['z'=8,'x'=4,'y'=8,'c'=2] {'x'}, dimensions={0} | all-to-all | bytes 2359296 | tf_op jit(solution)/shard_map/all_to_all | solution.py:373
  120.1 1.6 %sort.1 = bf16[8,72,512]{2,1,0:T(8,128)(2,1)} custom-call(s32[16]{0:T(128)S(1)} %get-tuple-element.19.place_ref, bf16[4,4,72,512]{3,2,1,0:T(8,128)(2,1)S(1)} %all_to_all.27.got_ref), custom_call_target="tpu_custom_call" | custom-call | tf_op jit(solution)/shard_map/sort/pallas_call | solution.py:375
  121.7 3.5 %all-to-all-start.4 = ((bf16[8,72,512]{2,1,0:T(8,128)(2,1)}), bf16[8,72,512]{2,1,0:T(8,128)(2,1)S(1)}, u32[]{:S(2)}, u32[]{:S(2)}) async-start(bf16[8,72,512]{2,1,0:T(8,128)(2,1)} %sort.1), calls=%async_computation.4 | async-start | bytes 1179648 | tf_op jit(solution)/shard_map/all_to_all | solution.py:384
  125.2 6.0 %backward.1 = bf16[1536,512]{1,0:T(8,128)(2,1)} custom-call(bf16[4,64,384]{2,1,0:T(8,128)(2,1)} %copy-done.5, bf16[1024,1536]{1,0:T(8,128)(2,1)} %all-gather.2.cloned.1.call-done.dy_ref, bf16[512,1024]{1,0:T(8,128)(2,1)} %weight_ref.1, bf16[4,64,512]{2,1,0:T(8,128)(2,1)} %copy-done.4), custom_call_target="tpu_custom_call" | custom-call | flops 1711276032 | bytes 6291456 | tf_op jit(solution)/shard_map/backward/pallas_call | solution.py:354
  131.3 13.2 %all-to-all-done.4.got_ref = bf16[8,72,512]{2,1,0:T(8,128)(2,1)S(1)} async-done(((bf16[8,72,512]{2,1,0:T(8,128)(2,1)}), bf16[8,72,512]{2,1,0:T(8,128)(2,1)S(1)}, u32[]{:S(2)}, u32[]{:S(2)}) %all-to-all-start.4) | async-done | bytes 589856 | tf_op jit(solution)/shard_map/all_to_all | solution.py:384
  (20 shorter events, 2.5 us)
Async XLA Ops:
  7.2 13.6 %copy-start.3 = (s32[4]{0:T(128)S(1)}, s32[4]{0:T(128)}, u32[]{:S(2)}) copy-start(s32[4]{0:T(128)} %refs_0_.1) | copy-start | bytes 52
  7.2 59.4 %all-gather.2.cloned.1.call-start = ((), (), s32[]{:S(2)}) async-start(), calls=%async_computation.5 | async-start | bytes 3342336 | tf_op jit(solution)/shard_map/all_gather | solution.py:217
  9.7 30.4 %copy-start.2 = (s32[32]{0:T(128)S(1)}, s32[32]{0:T(128)}, u32[]{:S(2)}) copy-start(s32[32]{0:T(128)} %holder_ref.1) | copy-start | bytes 388
  9.7 30.4 %all-to-all-start = ((bf16[8,72,512]{2,1,0:T(8,128)(2,1)}), bf16[8,72,512]{2,1,0:T(8,128)(2,1)S(1)}, u32[]{:S(2)}, u32[]{:S(2)}) async-start(bf16[8,72,512]{2,1,0:T(8,128)(2,1)} %prepare.1), calls=%async_computation | async-start | bytes 1179648 | tf_op jit(solution)/shard_map/all_to_all | solution.py:243
  20.7 12.7 %collective-permute-start.1 = (s32[4]{0:T(128)S(1)}, s32[4]{0:T(128)S(1)}, u32[]{:S(2)}, u32[]{:S(2)}) collective-permute-start(s32[4]{0:T(128)S(1)} %copy-done.3), channel_id=1, source_target_pairs={{0,32},{16,48},{32,0},{48,16},{1,33},{17,49},{33,1},{49,17},{2,34}... | collective-permute-start | bytes 56 | tf_op jit(solution)/shard_map/ppermute | solution.py:232
  25.4 8.1 %collective-permute-start = (s32[4]{0:T(128)S(1)}, s32[4]{0:T(128)S(1)}, u32[]{:S(2)}, u32[]{:S(2)}) collective-permute-start(s32[4]{0:T(128)S(1)} %copy-done.3), channel_id=1, source_target_pairs={{0,16},{16,32},{32,48},{48,0},{1,17},{17,33},{33,49},{49,1},{2,18}... | collective-permute-start | bytes 56 | tf_op jit(solution)/shard_map/ppermute | solution.py:232
  27.6 5.8 %collective-permute-start.2 = (s32[4]{0:T(128)S(1)}, s32[4]{0:T(128)S(1)}, u32[]{:S(2)}, u32[]{:S(2)}) collective-permute-start(s32[4]{0:T(128)S(1)} %copy-done.3), channel_id=1, source_target_pairs={{0,48},{16,0},{32,16},{48,32},{1,49},{17,1},{33,17},{49,33},{2,50}... | collective-permute-start | bytes 56 | tf_op jit(solution)/shard_map/ppermute | solution.py:232
  31.9 1.4 copy-start.1
  62.1 0.7 copy-start.4
  62.8 7.8 %collective-permute-start.3 = (bf16[2,384,128]{2,1,0:T(8,128)(2,1)S(1)}, bf16[2,384,128]{2,1,0:T(8,128)(2,1)S(1)}, u32[]{:S(2)}, u32[]{:S(2)}) collective-permute-start(bf16[2,384,128]{2,1,0:T(8,128)(2,1)S(1)} %get-tuple-element.15.refs_0_.low_ref), channel_id=1, source_target_pairs={{0,1},{1,0},{2,3},{3,2},{4,5},{5,4},{6,7},{7,6},{8,9},{9,8},{10,11... | collective-permute-start | bytes 589832 | tf_op jit(solution)/shard_map/ppermute | solution.py:290
  66.6 1.9 %copy-start = (bf16[1024,1536]{1,0:T(8,128)(2,1)S(1)}, bf16[1024,1536]{1,0:T(8,128)(2,1)}, u32[]{:S(2)}) copy-start(bf16[1024,1536]{1,0:T(8,128)(2,1)} %all-gather.2.cloned.1.call-done.dy_ref) | copy-start | bytes 9437188
  97.0 3.4 %collective-permute-start.4 = (bf16[4,64,384]{2,1,0:T(8,128)(2,1)S(1)}, bf16[4,64,384]{2,1,0:T(8,128)(2,1)S(1)}, u32[]{:S(2)}, u32[]{:S(2)}) collective-permute-start(bf16[4,64,384]{2,1,0:T(8,128)(2,1)S(1)} %lower.1.low_ref), channel_id=1, source_target_pairs={{0,1},{1,0},{2,3},{3,2},{4,5},{5,4},{6,7},{7,6},{8,9},{9,8},{10,11... | collective-permute-start | bytes 589832 | tf_op jit(solution)/shard_map/ppermute | solution.py:327
  101.4 20.3 %copy-start.5 = (bf16[4,64,384]{2,1,0:T(8,128)(2,1)}, bf16[4,64,384]{2,1,0:T(8,128)(2,1)S(1)}, u32[]{:S(2)}) copy-start(bf16[4,64,384]{2,1,0:T(8,128)(2,1)S(1)} %get-tuple-element.17.low_ref) | copy-start | bytes 589828
  121.7 22.8 %all-to-all-start.4 = ((bf16[8,72,512]{2,1,0:T(8,128)(2,1)}), bf16[8,72,512]{2,1,0:T(8,128)(2,1)S(1)}, u32[]{:S(2)}, u32[]{:S(2)}) async-start(bf16[8,72,512]{2,1,0:T(8,128)(2,1)} %sort.1), calls=%async_computation.4 | async-start | bytes 1179648 | tf_op jit(solution)/shard_map/all_to_all | solution.py:384
Sparse Core Ops, SparseCore 0:
  10.1 49.4 all-gather.1

commit v9 on v5

--- a/solution.py
+++ b/solution.py
@@ -54,7 +54,7 @@
 
 
 def select(columns, panel_ref, holder_ref, *refs):
-    tenant_refs, (sent_ref, slot_ref, place_ref, table) = refs[:columns], refs[columns:]
+    tenant_refs, (sent_ref, slot_ref, place_ref, table) = refs[:columns], refs[-4:]
     seqs = sent_ref.shape[1]
     for t in range(holder_ref.shape[0]):
         table[holder_ref[t]] = jnp.int32(t)
@@ -71,9 +71,15 @@
             sent_ref[there, s] = panel_ref[row]
 
 
+def bring(x_ref, *refs):
+    out_ref, sem = refs[-2:]
+    copy = pltpu.make_async_copy(x_ref, out_ref, sem)
+    copy.start()
+    copy.wait()
+
+
 def low(slot_ref, panel0_ref, panel1_ref, x_ref, low_ref, down_ref, ups_ref):
-    rank = down_ref.shape[1]
-    rows = low_ref.shape[1]
+    rows, rank = low_ref.shape[1], low_ref.shape[2] // 2
     total = ups = 0.0
     for side, panel_ref in enumerate((panel0_ref, panel1_ref)):
         panel = panel_ref[0, 0]
@@ -197,7 +203,17 @@
     struct = jax.ShapeDtypeStruct
 
     dy = lax.all_gather(cotangent.T, ("y", "c"), axis=0, tiled=True)
-    dy_halves = dy.reshape(chips, 2, keys, dy.shape[1])
+
+    anywhere = pl.BlockSpec(memory_space=pl.ANY)
+    near_x = pl.pallas_call(
+        bring,
+        out_shape=struct(activations.shape, BF16),
+        in_specs=[anywhere],
+        out_specs=anywhere,
+        scratch_shapes=[pltpu.SemaphoreType.DMA],
+        compiler_params=PART,
+        name="bring_x",
+    )(activations)
 
     tenants = [sequence_tenant] + [
         lax.ppermute(sequence_tenant, "x", [(x, (x + d) % columns) for x in range(columns)])
@@ -219,13 +235,15 @@
             struct((seqs + 1,), jnp.int32),
             struct((columns * seqs,), jnp.int32),
         ),
-        in_specs=[VMEM] + [SMEM] * (1 + columns),
+        in_specs=[VMEM] + [SMEM] * (1 + columns) + [anywhere],
         out_specs=(VMEM, SMEM, SMEM),
         scratch_shapes=[pltpu.SMEM((slots,), jnp.int32)],
         compiler_params=PART,
         name="select",
-    )(panels, slot_holder_tenant, *tenants)
+    )(panels, slot_holder_tenant, *tenants, near_x)
     panels = lax.all_to_all(sent, "x", 0, 0, tiled=True)
+    panels, dy = lax.optimization_barrier((panels, dy))
+    dy_halves = dy.reshape(chips, 2, keys, dy.shape[1])
 
     pairs = seqs // 2
     low_u, down, ups = pl.pallas_call(
@@ -255,9 +273,9 @@
             struct((seqs, rank, width), BF16),
             struct((pairs, keys, 2 * rank), BF16),
         ),
-        compiler_params=ALL,
+        compiler_params=STEPS,
         name="low",
-    )(slot_of, panels, panels, activations)
+    )(slot_of, panels, panels, near_x)
     other_low = lax.ppermute(low_u, "c", SWAP)
     dy_pair = pl.BlockSpec(
         (chips, 1, keys, 2 * rows), lambda p, slot: (0, slot[seqs], 0, p)
@@ -277,7 +295,7 @@
             out_specs=mixed,
         ),
         out_shape=struct((chips, pairs, 2 * keys, 2 * rank), BF16),
-        compiler_params=ALL,
+        compiler_params=STEPS,
         name="project",
     )(slot_of, low_u, other_low, ups, dy_halves)
     got = lax.all_to_all(sent, "y", 0, 0, tiled=True)
@@ -320,7 +338,7 @@
         ),
         compiler_params=STEPS,
         name="combine",
-    )(low_g, other_low, part_b, activations)
+    )(low_g, other_low, part_b, near_x)
     input_gradient = pl.pallas_call(
         backward,
         grid=(seqs,),

time: 156 us -> 151 us (0.968)
  Pallas kernels: 21.1 us -> 17.1 us
  waiting for transfers between devices: 24.9 us -> 23.1 us
    pallas_call x1, Pallas kernels: 3.7 us -> 1.48 us  [local(): pl.pallas_call(project, grid_spec=pltpu.PrefetchScalarGridSpec(num_scalar...]
    pallas_call x1, Pallas kernels: 3.29 us -> 1.29 us  [local(): pl.pallas_call(low, grid_spec=pltpu.PrefetchScalarGridSpec(num_scalar_pre...]
  transfers between devices with their start and end apart: 8 -> 8, of which waited for: 5 -> 5; matrix products, arithmetic and copies ran while one was open for 0% -> 0% of each run, Pallas kernels for 8% -> 6%
where the time goes in v9:
time: 151 us; the launch traced here: 150 us
  blocking collectives  61.3 us (41%)
  starting transfers between devices  32.6 us (22%)
  waiting for transfers between devices  23.1 us (15%)
  Pallas kernels  17.1 us (11%)
  between operations  14.2 us (9%)
  local copies, waits for them, and re-layouts  2.1 us (1%)
    all_to_all x1, blocking collectives, local(): got = lax.all_to_all(sent, 'y', 0, 0, tiled=True)  23.3 us
    all_to_all x1, blocking collectives, local(): panels = lax.all_to_all(sent, 'x', 0, 0, tiled=True)  19.3 us
    all_to_all x1, blocking collectives, local(): got = lax.all_to_all(sent, 'x', 0, 0, tiled=True)  18.7 us
    all_to_all x1, waiting for transfers between devices, local(): got = lax.all_to_all(sent, 'z', 0, 0, tiled=True)  13.3 us
    all_to_all x1, starting transfers between devices, local(): panels = lax.all_to_all(sent, 'z', 0, 0, tiled=True)  11 us
    ppermute x3, starting transfers between devices, local(): lax.ppermute(sequence_tenant, 'x', [(x, (x + d) % columns) for x in range...  10.5 us
    all_to_all x1, waiting for transfers between devices, local(): panels = lax.all_to_all(sent, 'z', 0, 0, tiled=True)  7.18 us
    pallas_call x1, Pallas kernels, local(): pl.pallas_call(backward, grid=(seqs,), in_specs=[one, pl.BlockSpec((dy.sh...  6.02 us
  transfers between devices with their start and end apart: 8, of which 5 were waited for; matrix products, arithmetic and copies ran while one was open for 0% of the time, Pallas kernels for 6%

profile of v9, /device:TPU:1, one launch (start us, length us, event | category | flops | bytes accessed | tf_op | source)
XLA Modules:
  0.0 150.4 jit_solution(15462451791793045588)
XLA Ops:
  7.9 1.8 %prepare.1 = bf16[8,72,512]{2,1,0:T(8,128)(2,1)} custom-call(bf16[1,64,512]{2,1,0:T(8,128)(2,1)} %down_ref.1, bf16[1,64,64]{2,1,0:T(8,128)(2,1)} %up_ref.1), custom_call_target="tpu_custom_call" | custom-call | tf_op jit(solution)/shard_map/prepare/pallas_call | solution.py:222
  9.7 11.0 %all-to-all-start = ((bf16[8,72,512]{2,1,0:T(8,128)(2,1)}), bf16[8,72,512]{2,1,0:T(8,128)(2,1)S(1)}, u32[]{:S(2)}, u32[]{:S(2)}) async-start(bf16[8,72,512]{2,1,0:T(8,128)(2,1)} %prepare.1), calls=%async_computation | async-start | bytes 1179648 | tf_op jit(solution)/shard_map/all_to_all | solution.py:230
  20.7 3.1 %collective-permute-start = (s32[4]{0:T(128)S(1)}, s32[4]{0:T(128)S(1)}, u32[]{:S(2)}, u32[]{:S(2)}) collective-permute-start(s32[4]{0:T(128)S(1)} %copy-done.3), channel_id=1, source_target_pairs={{0,16},{16,32},{32,48},{48,0},{1,17},{17,33},{33,49},{49,1},{2,18}... | collective-permute-start | bytes 56 | tf_op jit(solution)/shard_map/ppermute | solution.py:219
  23.9 4.4 %collective-permute-start.1 = (s32[4]{0:T(128)S(1)}, s32[4]{0:T(128)S(1)}, u32[]{:S(2)}, u32[]{:S(2)}) collective-permute-start(s32[4]{0:T(128)S(1)} %copy-done.3), channel_id=1, source_target_pairs={{0,32},{16,48},{32,0},{48,16},{1,33},{17,49},{33,1},{49,17},{2,34}... | collective-permute-start | bytes 56 | tf_op jit(solution)/shard_map/ppermute | solution.py:219
  28.2 3.1 %collective-permute-start.2 = (s32[4]{0:T(128)S(1)}, s32[4]{0:T(128)S(1)}, u32[]{:S(2)}, u32[]{:S(2)}) collective-permute-start(s32[4]{0:T(128)S(1)} %copy-done.3), channel_id=1, source_target_pairs={{0,48},{16,0},{32,16},{48,32},{1,49},{17,1},{33,17},{49,33},{2,50}... | collective-permute-start | bytes 56 | tf_op jit(solution)/shard_map/ppermute | solution.py:219
  31.3 1.4 copy-done.1
  32.9 7.2 %all-to-all-done.panel_ref = bf16[8,72,512]{2,1,0:T(8,128)(2,1)S(1)} async-done(((bf16[8,72,512]{2,1,0:T(8,128)(2,1)}), bf16[8,72,512]{2,1,0:T(8,128)(2,1)S(1)}, u32[]{:S(2)}, u32[]{:S(2)}) %all-to-all-start) | async-done | bytes 589856 | tf_op jit(solution)/shard_map/all_to_all | solution.py:230
  40.1 1.3 select.1
  41.4 19.3 %all_to_all.25.panel0_ref.panel1_ref = bf16[4,4,72,512]{3,2,1,0:T(8,128)(2,1)S(1)} all-to-all(bf16[4,4,72,512]{3,2,1,0:T(8,128)(2,1)S(1)} %get-tuple-element.16), channel_id=1, replica_groups=mesh['z'=8,'x'=4,'y'=8,'c'=2] {'x'}, dimensions={0} | all-to-all | bytes 2359296 | tf_op jit(solution)/shard_map/all_to_all | solution.py:244
  60.8 1.3 low.1
  62.8 3.8 %collective-permute-start.3 = (bf16[2,384,128]{2,1,0:T(8,128)(2,1)S(1)}, bf16[2,384,128]{2,1,0:T(8,128)(2,1)S(1)}, u32[]{:S(2)}, u32[]{:S(2)}) collective-permute-start(bf16[2,384,128]{2,1,0:T(8,128)(2,1)S(1)} %get-tuple-element.18.low_ref), channel_id=1, source_target_pairs={{0,1},{1,0},{2,3},{3,2},{4,5},{5,4},{6,7},{7,6},{8,9},{9,8},{10,11... | collective-permute-start | bytes 589832 | tf_op jit(solution)/shard_map/ppermute | solution.py:279
  66.6 1.0 collective-permute-done.3.other_ref
  67.7 1.5 project.1
  69.1 23.3 %all_to_all.26.got_ref = bf16[8,2,128,128]{3,2,1,0:T(8,128)(2,1)S(1)} all-to-all(bf16[8,2,128,128]{3,2,1,0:T(8,128)(2,1)S(1)} %project.1), channel_id=1, replica_groups=mesh['z'=8,'x'=4,'y'=8,'c'=2] {'y'}, dimensions={0} | all-to-all | bytes 1048576 | tf_op jit(solution)/shard_map/all_to_all | solution.py:301
  92.5 1.4 lower.1.low_ref
  93.9 3.6 %collective-permute-start.4 = (bf16[4,64,384]{2,1,0:T(8,128)(2,1)S(1)}, bf16[4,64,384]{2,1,0:T(8,128)(2,1)S(1)}, u32[]{:S(2)}, u32[]{:S(2)}) collective-permute-start(bf16[4,64,384]{2,1,0:T(8,128)(2,1)S(1)} %lower.1.low_ref), channel_id=1, source_target_pairs={{0,1},{1,0},{2,3},{3,2},{4,5},{5,4},{6,7},{7,6},{8,9},{9,8},{10,11... | collective-permute-start | bytes 589832 | tf_op jit(solution)/shard_map/ppermute | solution.py:315
  97.7 0.9 collective-permute-done.4.other_ref
  98.6 0.9 combine.1
  99.6 18.7 %all_to_all.27.got_ref = bf16[4,4,72,512]{3,2,1,0:T(8,128)(2,1)S(1)} all-to-all(bf16[4,4,72,512]{3,2,1,0:T(8,128)(2,1)S(1)} %get-tuple-element.24), channel_id=1, replica_groups=mesh['z'=8,'x'=4,'y'=8,'c'=2] {'x'}, dimensions={0} | all-to-all | bytes 2359296 | tf_op jit(solution)/shard_map/all_to_all | solution.py:361
  118.2 1.7 %sort.1 = bf16[8,72,512]{2,1,0:T(8,128)(2,1)} custom-call(s32[16]{0:T(128)S(1)} %get-tuple-element.23.place_ref, bf16[4,4,72,512]{3,2,1,0:T(8,128)(2,1)S(1)} %all_to_all.27.got_ref), custom_call_target="tpu_custom_call" | custom-call | tf_op jit(solution)/shard_map/sort/pallas_call | solution.py:363
  119.9 3.5 %all-to-all-start.4 = ((bf16[8,72,512]{2,1,0:T(8,128)(2,1)}), bf16[8,72,512]{2,1,0:T(8,128)(2,1)S(1)}, u32[]{:S(2)}, u32[]{:S(2)}) async-start(bf16[8,72,512]{2,1,0:T(8,128)(2,1)} %sort.1), calls=%async_computation.4 | async-start | bytes 1179648 | tf_op jit(solution)/shard_map/all_to_all | solution.py:372
  123.5 6.0 %backward.1 = bf16[1536,512]{1,0:T(8,128)(2,1)} custom-call(bf16[4,64,384]{2,1,0:T(8,128)(2,1)} %copy-done.5, bf16[1024,1536]{1,0:T(8,128)(2,1)} %all-gather.2.cloned.1.call-done.dy_ref, bf16[512,1024]{1,0:T(8,128)(2,1)} %weight_ref.1, bf16[4,64,512]{2,1,0:T(8,128)(2,1)} %copy-done.4), custom_call_target="tpu_custom_call" | custom-call | flops 1711276032 | bytes 6291456 | tf_op jit(solution)/shard_map/backward/pallas_call | solution.py:342
  129.5 13.3 %all-to-all-done.4.got_ref = bf16[8,72,512]{2,1,0:T(8,128)(2,1)S(1)} async-done(((bf16[8,72,512]{2,1,0:T(8,128)(2,1)}), bf16[8,72,512]{2,1,0:T(8,128)(2,1)S(1)}, u32[]{:S(2)}, u32[]{:S(2)}) %all-to-all-start.4) | async-done | bytes 589856 | tf_op jit(solution)/shard_map/all_to_all | solution.py:372
  142.7 0.8 finish.1
  (19 shorter events, 1.8 us)
Async XLA Ops:
  7.2 13.6 %copy-start.3 = (s32[4]{0:T(128)S(1)}, s32[4]{0:T(128)}, u32[]{:S(2)}) copy-start(s32[4]{0:T(128)} %refs_0_.1) | copy-start | bytes 52
  7.2 53.6 %all-gather.2.cloned.1.call-start = ((), (), s32[]{:S(2)}) async-start(), calls=%async_computation.5 | async-start | bytes 3342336 | tf_op jit(solution)/shard_map/all_gather | solution.py:205
  9.7 30.4 %copy-start.2 = (s32[32]{0:T(128)S(1)}, s32[32]{0:T(128)}, u32[]{:S(2)}) copy-start(s32[32]{0:T(128)} %holder_ref.1) | copy-start | bytes 388
  9.7 30.4 %all-to-all-start = ((bf16[8,72,512]{2,1,0:T(8,128)(2,1)}), bf16[8,72,512]{2,1,0:T(8,128)(2,1)S(1)}, u32[]{:S(2)}, u32[]{:S(2)}) async-start(bf16[8,72,512]{2,1,0:T(8,128)(2,1)} %prepare.1), calls=%async_computation | async-start | bytes 1179648 | tf_op jit(solution)/shard_map/all_to_all | solution.py:230
  20.7 12.1 %collective-permute-start = (s32[4]{0:T(128)S(1)}, s32[4]{0:T(128)S(1)}, u32[]{:S(2)}, u32[]{:S(2)}) collective-permute-start(s32[4]{0:T(128)S(1)} %copy-done.3), channel_id=1, source_target_pairs={{0,16},{16,32},{32,48},{48,0},{1,17},{17,33},{33,49},{49,1},{2,18}... | collective-permute-start | bytes 56 | tf_op jit(solution)/shard_map/ppermute | solution.py:219
  23.9 9.0 %collective-permute-start.1 = (s32[4]{0:T(128)S(1)}, s32[4]{0:T(128)S(1)}, u32[]{:S(2)}, u32[]{:S(2)}) collective-permute-start(s32[4]{0:T(128)S(1)} %copy-done.3), channel_id=1, source_target_pairs={{0,32},{16,48},{32,0},{48,16},{1,33},{17,49},{33,1},{49,17},{2,34}... | collective-permute-start | bytes 56 | tf_op jit(solution)/shard_map/ppermute | solution.py:219
  28.2 4.7 %collective-permute-start.2 = (s32[4]{0:T(128)S(1)}, s32[4]{0:T(128)S(1)}, u32[]{:S(2)}, u32[]{:S(2)}) collective-permute-start(s32[4]{0:T(128)S(1)} %copy-done.3), channel_id=1, source_target_pairs={{0,48},{16,0},{32,16},{48,32},{1,49},{17,1},{33,17},{49,33},{2,50}... | collective-permute-start | bytes 56 | tf_op jit(solution)/shard_map/ppermute | solution.py:219
  31.3 1.4 copy-start.1
  60.8 6.9 %copy-start = (bf16[1024,1536]{1,0:T(8,128)(2,1)S(1)}, bf16[1024,1536]{1,0:T(8,128)(2,1)}, u32[]{:S(2)}) copy-start(bf16[1024,1536]{1,0:T(8,128)(2,1)} %all-gather.2.cloned.1.call-done.dy_ref) | copy-start | bytes 9437188
  62.1 0.7 copy-start.4
  62.8 4.9 %collective-permute-start.3 = (bf16[2,384,128]{2,1,0:T(8,128)(2,1)S(1)}, bf16[2,384,128]{2,1,0:T(8,128)(2,1)S(1)}, u32[]{:S(2)}, u32[]{:S(2)}) collective-permute-start(bf16[2,384,128]{2,1,0:T(8,128)(2,1)S(1)} %get-tuple-element.18.low_ref), channel_id=1, source_target_pairs={{0,1},{1,0},{2,3},{3,2},{4,5},{5,4},{6,7},{7,6},{8,9},{9,8},{10,11... | collective-permute-start | bytes 589832 | tf_op jit(solution)/shard_map/ppermute | solution.py:279
  93.9 4.7 %collective-permute-start.4 = (bf16[4,64,384]{2,1,0:T(8,128)(2,1)S(1)}, bf16[4,64,384]{2,1,0:T(8,128)(2,1)S(1)}, u32[]{:S(2)}, u32[]{:S(2)}) collective-permute-start(bf16[4,64,384]{2,1,0:T(8,128)(2,1)S(1)} %lower.1.low_ref), channel_id=1, source_target_pairs={{0,1},{1,0},{2,3},{3,2},{4,5},{5,4},{6,7},{7,6},{8,9},{9,8},{10,11... | collective-permute-start | bytes 589832 | tf_op jit(solution)/shard_map/ppermute | solution.py:315
  99.5 18.7 %copy-start.5 = (bf16[4,64,384]{2,1,0:T(8,128)(2,1)}, bf16[4,64,384]{2,1,0:T(8,128)(2,1)S(1)}, u32[]{:S(2)}) copy-start(bf16[4,64,384]{2,1,0:T(8,128)(2,1)S(1)} %get-tuple-element.21.low_ref) | copy-start | bytes 589828
  119.9 22.8 %all-to-all-start.4 = ((bf16[8,72,512]{2,1,0:T(8,128)(2,1)}), bf16[8,72,512]{2,1,0:T(8,128)(2,1)S(1)}, u32[]{:S(2)}, u32[]{:S(2)}) async-start(bf16[8,72,512]{2,1,0:T(8,128)(2,1)} %sort.1), calls=%async_computation.4 | async-start | bytes 1179648 | tf_op jit(solution)/shard_map/all_to_all | solution.py:372
Sparse Core Ops, SparseCore 0:
  10.1 49.4 all-gather.1

commit v10 on v9

--- a/solution.py
+++ b/solution.py
@@ -78,13 +78,12 @@
     copy.wait()
 
 
-def low(slot_ref, panel0_ref, panel1_ref, x_ref, low_ref, down_ref, ups_ref):
+def low(slot_ref, panel0_ref, panel1_ref, x_ref, low_ref, ups_ref):
     rows, rank = low_ref.shape[1], low_ref.shape[2] // 2
     total = ups = 0.0
     for side, panel_ref in enumerate((panel0_ref, panel1_ref)):
         panel = panel_ref[0, 0]
         down = panel[:rank]
-        down_ref[side] = down
         blank = jnp.zeros_like(down)
         wide = jnp.concatenate([blank, down] if side else [down, blank], axis=0)
         total = total + lax.dot_general(
@@ -96,6 +95,12 @@
         ups = ups + unpack(panel.astype(F32)[rank:], side == 1)
     low_ref[0] = total.astype(BF16)
     ups_ref[0] = ups.astype(BF16)
+
+
+def keep(slot_ref, panel_ref, _, down_ref):
+    seqs, rank, _ = down_ref.shape
+    for s in range(seqs):
+        down_ref[s] = panel_ref[lax.rem(slot_ref[s], panel_ref.shape[0]), s][:rank]
 
 
 def project(slot_ref, low_ref, other_ref, ups_ref, dy_ref, sent_ref):
@@ -246,7 +251,7 @@
     dy_halves = dy.reshape(chips, 2, keys, dy.shape[1])
 
     pairs = seqs // 2
-    low_u, down, ups = pl.pallas_call(
+    low_u, ups = pl.pallas_call(
         low,
         grid_spec=pltpu.PrefetchScalarGridSpec(
             num_scalar_prefetch=1,
@@ -264,19 +269,25 @@
             ],
             out_specs=(
                 pl.BlockSpec((1, rows, 2 * rank), lambda p, slot: (p, 0, 0)),
-                pl.BlockSpec((2, rank, width), lambda p, slot: (p, 0, 0)),
                 pl.BlockSpec((1, keys, 2 * rank), lambda p, slot: (p, 0, 0)),
             ),
         ),
         out_shape=(
             struct((pairs, rows, 2 * rank), BF16),
-            struct((seqs, rank, width), BF16),
             struct((pairs, keys, 2 * rank), BF16),
         ),
         compiler_params=STEPS,
         name="low",
     )(slot_of, panels, panels, near_x)
     other_low = lax.ppermute(low_u, "c", SWAP)
+    down = pl.pallas_call(
+        keep,
+        out_shape=struct((seqs, rank, width), BF16),
+        in_specs=[SMEM, VMEM, anywhere],
+        out_specs=VMEM,
+        compiler_params=PART,
+        name="keep",
+    )(slot_of, panels, low_u)
     dy_pair = pl.BlockSpec(
         (chips, 1, keys, 2 * rows), lambda p, slot: (0, slot[seqs], 0, p)
     )

time: 151 us -> 150 us (level)
  waiting for transfers between devices: 23.1 us -> 21.3 us
  transfers between devices with their start and end apart: 8 -> 8, of which waited for: 5 -> 4; matrix products, arithmetic and copies ran while one was open for 0% -> 0% of each run, Pallas kernels for 6% -> 7%
where the time goes in v10:
time: 150 us
  blocking collectives  61.3 us (41%)
  starting transfers between devices  33.2 us (22%)
  waiting for transfers between devices  21.3 us (14%)
  Pallas kernels  17.6 us (12%)
  between operations  14.2 us (9%)
  local copies, waits for them, and re-layouts  2.1 us (1%)
    all_to_all x1, blocking collectives, local(): got = lax.all_to_all(sent, 'y', 0, 0, tiled=True)  23.3 us
    all_to_all x1, blocking collectives, local(): panels = lax.all_to_all(sent, 'x', 0, 0, tiled=True)  19.3 us
    all_to_all x1, blocking collectives, local(): got = lax.all_to_all(sent, 'x', 0, 0, tiled=True)  18.7 us
    all_to_all x1, waiting for transfers between devices, local(): got = lax.all_to_all(sent, 'z', 0, 0, tiled=True)  12 us
    ppermute x3, starting transfers between devices, local(): lax.ppermute(sequence_tenant, 'x', [(x, (x + d) % columns) for x in range...  11.1 us
    all_to_all x1, starting transfers between devices, local(): panels = lax.all_to_all(sent, 'z', 0, 0, tiled=True)  11 us
    all_to_all x1, waiting for transfers between devices, local(): panels = lax.all_to_all(sent, 'z', 0, 0, tiled=True)  6.62 us
    pallas_call x1, Pallas kernels, local(): pl.pallas_call(backward, grid=(seqs,), in_specs=[one, pl.BlockSpec((dy.sh...  5.99 us
  transfers between devices with their start and end apart: 8, of which 4 were waited for; matrix products, arithmetic and copies ran while one was open for 0% of the time, Pallas kernels for 7%

profile of v10, /device:TPU:1, one launch (start us, length us, event | category | flops | bytes accessed | tf_op | source)
XLA Modules:
  0.0 149.7 jit_solution(2446021114972079230)
XLA Ops:
  7.9 1.8 %prepare.1 = bf16[8,72,512]{2,1,0:T(8,128)(2,1)} custom-call(bf16[1,64,512]{2,1,0:T(8,128)(2,1)} %down_ref.1, bf16[1,64,64]{2,1,0:T(8,128)(2,1)} %up_ref.1), custom_call_target="tpu_custom_call" | custom-call | tf_op jit(solution)/shard_map/prepare/pallas_call | solution.py:227
  9.7 11.0 %all-to-all-start = ((bf16[8,72,512]{2,1,0:T(8,128)(2,1)}), bf16[8,72,512]{2,1,0:T(8,128)(2,1)S(1)}, u32[]{:S(2)}, u32[]{:S(2)}) async-start(bf16[8,72,512]{2,1,0:T(8,128)(2,1)} %prepare.1), calls=%async_computation | async-start | bytes 1179648 | tf_op jit(solution)/shard_map/all_to_all | solution.py:235
  20.7 4.7 %collective-permute-start.1 = (s32[4]{0:T(128)S(1)}, s32[4]{0:T(128)S(1)}, u32[]{:S(2)}, u32[]{:S(2)}) collective-permute-start(s32[4]{0:T(128)S(1)} %copy-done.4), channel_id=1, source_target_pairs={{0,32},{16,48},{32,0},{48,16},{1,33},{17,49},{33,1},{49,17},{2,34}... | collective-permute-start | bytes 56 | tf_op jit(solution)/shard_map/ppermute | solution.py:224
  25.4 2.2 %collective-permute-start = (s32[4]{0:T(128)S(1)}, s32[4]{0:T(128)S(1)}, u32[]{:S(2)}, u32[]{:S(2)}) collective-permute-start(s32[4]{0:T(128)S(1)} %copy-done.4), channel_id=1, source_target_pairs={{0,16},{16,32},{32,48},{48,0},{1,17},{17,33},{33,49},{49,1},{2,18}... | collective-permute-start | bytes 56 | tf_op jit(solution)/shard_map/ppermute | solution.py:224
  27.6 4.3 %collective-permute-start.2 = (s32[4]{0:T(128)S(1)}, s32[4]{0:T(128)S(1)}, u32[]{:S(2)}, u32[]{:S(2)}) collective-permute-start(s32[4]{0:T(128)S(1)} %copy-done.4), channel_id=1, source_target_pairs={{0,48},{16,0},{32,16},{48,32},{1,49},{17,1},{33,17},{49,33},{2,50}... | collective-permute-start | bytes 56 | tf_op jit(solution)/shard_map/ppermute | solution.py:224
  31.9 1.4 copy-done.1
  33.5 6.6 %all-to-all-done.panel_ref = bf16[8,72,512]{2,1,0:T(8,128)(2,1)S(1)} async-done(((bf16[8,72,512]{2,1,0:T(8,128)(2,1)}), bf16[8,72,512]{2,1,0:T(8,128)(2,1)S(1)}, u32[]{:S(2)}, u32[]{:S(2)}) %all-to-all-start) | async-done | bytes 589856 | tf_op jit(solution)/shard_map/all_to_all | solution.py:235
  40.1 1.3 select.1
  41.4 19.3 %all_to_all.25.panel0_ref.panel1_ref.panel_ref = bf16[4,4,72,512]{3,2,1,0:T(8,128)(2,1)S(1)} all-to-all(bf16[4,4,72,512]{3,2,1,0:T(8,128)(2,1)S(1)} %get-tuple-element.15), channel_id=1, replica_groups=mesh['z'=8,'x'=4,'y'=8,'c'=2] {'x'}, dimensions={0} | all-to-all | bytes 2359296 | tf_op jit(solution)/shard_map/all_to_all | solution.py:249
  60.8 1.3 low.1
  62.1 3.9 %collective-permute-start.3 = (bf16[2,384,128]{2,1,0:T(8,128)(2,1)S(1)}, bf16[2,384,128]{2,1,0:T(8,128)(2,1)S(1)}, u32[]{:S(2)}, u32[]{:S(2)}) collective-permute-start(bf16[2,384,128]{2,1,0:T(8,128)(2,1)S(1)} %get-tuple-element.17.low_ref._), channel_id=1, source_target_pairs={{0,1},{1,0},{2,3},{3,2},{4,5},{5,4},{6,7},{7,6},{8,9},{9,8},{10,11... | collective-permute-start | bytes 589832 | tf_op jit(solution)/shard_map/ppermute | solution.py:282
  65.9 1.0 collective-permute-done.3.other_ref
  67.0 1.5 project.1
  68.5 23.3 %all_to_all.26.got_ref = bf16[8,2,128,128]{3,2,1,0:T(8,128)(2,1)S(1)} all-to-all(bf16[8,2,128,128]{3,2,1,0:T(8,128)(2,1)S(1)} %project.1), channel_id=1, replica_groups=mesh['z'=8,'x'=4,'y'=8,'c'=2] {'y'}, dimensions={0} | all-to-all | bytes 1048576 | tf_op jit(solution)/shard_map/all_to_all | solution.py:312
  91.8 1.4 lower.1.low_ref
  93.2 3.6 %collective-permute-start.4 = (bf16[4,64,384]{2,1,0:T(8,128)(2,1)S(1)}, bf16[4,64,384]{2,1,0:T(8,128)(2,1)S(1)}, u32[]{:S(2)}, u32[]{:S(2)}) collective-permute-start(bf16[4,64,384]{2,1,0:T(8,128)(2,1)S(1)} %lower.1.low_ref), channel_id=1, source_target_pairs={{0,1},{1,0},{2,3},{3,2},{4,5},{5,4},{6,7},{7,6},{8,9},{9,8},{10,11... | collective-permute-start | bytes 589832 | tf_op jit(solution)/shard_map/ppermute | solution.py:326
  97.0 0.9 collective-permute-done.4.other_ref
  97.9 0.9 combine.1
  98.9 18.7 %all_to_all.27.got_ref = bf16[4,4,72,512]{3,2,1,0:T(8,128)(2,1)S(1)} all-to-all(bf16[4,4,72,512]{3,2,1,0:T(8,128)(2,1)S(1)} %get-tuple-element.22), channel_id=1, replica_groups=mesh['z'=8,'x'=4,'y'=8,'c'=2] {'x'}, dimensions={0} | all-to-all | bytes 2359296 | tf_op jit(solution)/shard_map/all_to_all | solution.py:372
  117.6 1.7 %sort.1 = bf16[8,72,512]{2,1,0:T(8,128)(2,1)} custom-call(s32[16]{0:T(128)S(1)} %get-tuple-element.21.place_ref, bf16[4,4,72,512]{3,2,1,0:T(8,128)(2,1)S(1)} %all_to_all.27.got_ref), custom_call_target="tpu_custom_call" | custom-call | tf_op jit(solution)/shard_map/sort/pallas_call | solution.py:374
  119.2 3.5 %all-to-all-start.4 = ((bf16[8,72,512]{2,1,0:T(8,128)(2,1)}), bf16[8,72,512]{2,1,0:T(8,128)(2,1)S(1)}, u32[]{:S(2)}, u32[]{:S(2)}) async-start(bf16[8,72,512]{2,1,0:T(8,128)(2,1)} %sort.1), calls=%async_computation.4 | async-start | bytes 1179648 | tf_op jit(solution)/shard_map/all_to_all | solution.py:383
  124.0 6.0 %backward.1 = bf16[1536,512]{1,0:T(8,128)(2,1)} custom-call(bf16[4,64,384]{2,1,0:T(8,128)(2,1)} %copy-done.5, bf16[1024,1536]{1,0:T(8,128)(2,1)} %all-gather.2.cloned.1.call-done.dy_ref, bf16[512,1024]{1,0:T(8,128)(2,1)} %weight_ref.1, bf16[4,64,512]{2,1,0:T(8,128)(2,1)} %copy-done.2), custom_call_target="tpu_custom_call" | custom-call | flops 1711276032 | bytes 6291456 | tf_op jit(solution)/shard_map/backward/pallas_call | solution.py:353
  130.0 12.0 %all-to-all-done.4.got_ref = bf16[8,72,512]{2,1,0:T(8,128)(2,1)S(1)} async-done(((bf16[8,72,512]{2,1,0:T(8,128)(2,1)}), bf16[8,72,512]{2,1,0:T(8,128)(2,1)S(1)}, u32[]{:S(2)}, u32[]{:S(2)}) %all-to-all-start.4) | async-done | bytes 589856 | tf_op jit(solution)/shard_map/all_to_all | solution.py:383
  142.1 0.8 finish.1
  (20 shorter events, 2.3 us)
Async XLA Ops:
  7.2 13.6 %copy-start.4 = (s32[4]{0:T(128)S(1)}, s32[4]{0:T(128)}, u32[]{:S(2)}) copy-start(s32[4]{0:T(128)} %refs_0_.1) | copy-start | bytes 52
  7.2 53.6 %all-gather.2.cloned.1.call-start = ((), (), s32[]{:S(2)}) async-start(), calls=%async_computation.5 | async-start | bytes 3342336 | tf_op jit(solution)/shard_map/all_gather | solution.py:210
  9.7 30.4 %copy-start.3 = (s32[32]{0:T(128)S(1)}, s32[32]{0:T(128)}, u32[]{:S(2)}) copy-start(s32[32]{0:T(128)} %holder_ref.1) | copy-start | bytes 388
  9.7 30.4 %all-to-all-start = ((bf16[8,72,512]{2,1,0:T(8,128)(2,1)}), bf16[8,72,512]{2,1,0:T(8,128)(2,1)S(1)}, u32[]{:S(2)}, u32[]{:S(2)}) async-start(bf16[8,72,512]{2,1,0:T(8,128)(2,1)} %prepare.1), calls=%async_computation | async-start | bytes 1179648 | tf_op jit(solution)/shard_map/all_to_all | solution.py:235
  20.7 12.7 %collective-permute-start.1 = (s32[4]{0:T(128)S(1)}, s32[4]{0:T(128)S(1)}, u32[]{:S(2)}, u32[]{:S(2)}) collective-permute-start(s32[4]{0:T(128)S(1)} %copy-done.4), channel_id=1, source_target_pairs={{0,32},{16,48},{32,0},{48,16},{1,33},{17,49},{33,1},{49,17},{2,34}... | collective-permute-start | bytes 56 | tf_op jit(solution)/shard_map/ppermute | solution.py:224
  25.4 8.1 %collective-permute-start = (s32[4]{0:T(128)S(1)}, s32[4]{0:T(128)S(1)}, u32[]{:S(2)}, u32[]{:S(2)}) collective-permute-start(s32[4]{0:T(128)S(1)} %copy-done.4), channel_id=1, source_target_pairs={{0,16},{16,32},{32,48},{48,0},{1,17},{17,33},{33,49},{49,1},{2,18}... | collective-permute-start | bytes 56 | tf_op jit(solution)/shard_map/ppermute | solution.py:224
  27.6 5.8 %collective-permute-start.2 = (s32[4]{0:T(128)S(1)}, s32[4]{0:T(128)S(1)}, u32[]{:S(2)}, u32[]{:S(2)}) collective-permute-start(s32[4]{0:T(128)S(1)} %copy-done.4), channel_id=1, source_target_pairs={{0,48},{16,0},{32,16},{48,32},{1,49},{17,1},{33,17},{49,33},{2,50}... | collective-permute-start | bytes 56 | tf_op jit(solution)/shard_map/ppermute | solution.py:224
  31.9 1.4 copy-start.1
  60.8 6.2 %copy-start = (bf16[1024,1536]{1,0:T(8,128)(2,1)S(1)}, bf16[1024,1536]{1,0:T(8,128)(2,1)}, u32[]{:S(2)}) copy-start(bf16[1024,1536]{1,0:T(8,128)(2,1)} %all-gather.2.cloned.1.call-done.dy_ref) | copy-start | bytes 9437188
  62.1 4.9 %collective-permute-start.3 = (bf16[2,384,128]{2,1,0:T(8,128)(2,1)S(1)}, bf16[2,384,128]{2,1,0:T(8,128)(2,1)S(1)}, u32[]{:S(2)}, u32[]{:S(2)}) collective-permute-start(bf16[2,384,128]{2,1,0:T(8,128)(2,1)S(1)} %get-tuple-element.17.low_ref._), channel_id=1, source_target_pairs={{0,1},{1,0},{2,3},{3,2},{4,5},{5,4},{6,7},{7,6},{8,9},{9,8},{10,11... | collective-permute-start | bytes 589832 | tf_op jit(solution)/shard_map/ppermute | solution.py:282
  93.2 4.7 %collective-permute-start.4 = (bf16[4,64,384]{2,1,0:T(8,128)(2,1)S(1)}, bf16[4,64,384]{2,1,0:T(8,128)(2,1)S(1)}, u32[]{:S(2)}, u32[]{:S(2)}) collective-permute-start(bf16[4,64,384]{2,1,0:T(8,128)(2,1)S(1)} %lower.1.low_ref), channel_id=1, source_target_pairs={{0,1},{1,0},{2,3},{3,2},{4,5},{5,4},{6,7},{7,6},{8,9},{9,8},{10,11... | collective-permute-start | bytes 589832 | tf_op jit(solution)/shard_map/ppermute | solution.py:326
  98.9 18.7 %copy-start.5 = (bf16[4,64,384]{2,1,0:T(8,128)(2,1)}, bf16[4,64,384]{2,1,0:T(8,128)(2,1)S(1)}, u32[]{:S(2)}) copy-start(bf16[4,64,384]{2,1,0:T(8,128)(2,1)S(1)} %get-tuple-element.20.low_ref) | copy-start | bytes 589828
  119.2 22.8 %all-to-all-start.4 = ((bf16[8,72,512]{2,1,0:T(8,128)(2,1)}), bf16[8,72,512]{2,1,0:T(8,128)(2,1)S(1)}, u32[]{:S(2)}, u32[]{:S(2)}) async-start(bf16[8,72,512]{2,1,0:T(8,128)(2,1)} %sort.1), calls=%async_computation.4 | async-start | bytes 1179648 | tf_op jit(solution)/shard_map/all_to_all | solution.py:383
  123.4 0.7 copy-start.2
Sparse Core Ops, SparseCore 0:
  10.1 49.4 all-gather.1
